TPU v7x, 32 devices: a whole 2x2x4 slice. The times are simulated.
32 devices in a mesh: dp: 8 (over z, core), row: 2 (over x), col: 2 (over y).
Axes of the slice: x: 2, y: 2, z: 4, core: 2. Of those that a mesh axis runs over, the one named last changes fastest.
Arguments:
- inputs: bfloat16 [8192, 1280], P(('dp', 'row'), 'col'), may hold values from -6 to 6
- gain_attn: float32 [1280], P('col'), may hold values from 0.1 to 1.9
- w_qkv: bfloat16 [1280, 3, 1280], P('col', None, 'row'), may hold values from -0.25 to 0.25
- query_scale: float32 [80], replicated, may hold values from -1 to 1
- w_out: bfloat16 [1280, 1280], P('row', 'col'), may hold values from -0.625 to 0.625
- gain_mlp: float32 [1280], P('col'), may hold values from 0.1 to 1.9
- w_up: bfloat16 [1280, 1280], P('col', 'row'), may hold values from -0.15625 to 0.15625
- b_up: bfloat16 [1280], P('row'), may hold values from -3 to 3
- w_down: bfloat16 [1280, 1280], P('row', 'col'), may hold values from -0.15625 to 0.15625
- b_down: bfloat16 [1280], P('col'), may hold values from -2 to 2
- series_ids: int32 [8192], P('dp'), may hold values from 0 to 15, never falling along the last dimension, each value on 1 to 1024 neighbouring positions
- pad_mask: int32 [8192], P('dp'), may hold values 0 or 1
- cotangent: bfloat16 [8192, 1280], P(('dp', 'row'), 'col'), may hold values from -6 to 6
Outputs:
- layer_out: bfloat16 [8192, 1280], P(('dp', 'row'), 'col')
- grad_inputs: float32 [8192, 1280], P(('dp', 'row'), 'col')
- grad_gain_attn: float32 [1280], P('col')
- grad_w_qkv: float32 [1280, 3, 1280], P('col', None, 'row')
- grad_query_scale: float32 [80], replicated
- grad_w_out: float32 [1280, 1280], P('row', 'col')
- grad_gain_mlp: float32 [1280], P('col')
- grad_w_up: float32 [1280, 1280], P('col', 'row')
- grad_b_up: float32 [1280], P('row')
- grad_w_down: float32 [1280, 1280], P('row', 'col')
- grad_b_down: float32 [1280], P('col')
Inputs may be any that keep to these rules, and one draw needn't show every extreme that they name: series_ids never falls along the tokens; a series has 1 to 1024 tokens.
All inputs are finite; a program needn't handle non-finite values. No bound on the sum of `pad_mask` on one device may be relied on, other than what follows from the above.
Results may differ from a plain program's by a relative error of at most 0.015.
The roundings to bfloat16 on the way count: a program that leaves them out, or rounds other values in their place, can miss the bound.
Values may be sent and summed in bfloat16 or wider, within the bound.
No kernel may reach another device: no remote copies, remote signals or barrier semaphores. Data moves between devices by JAX's collectives and lax.ppermute only.
A program may use at most 128 MiB of HBM per device.

v0:
```python
import functools
import math

import jax
import jax.numpy as jnp
from jax import lax
from jax.experimental import pallas as pl
from jax.experimental.pallas import tpu as pltpu
from jax.sharding import Mesh
from jax.sharding import PartitionSpec as P

D = 1280
HEAD_DIM = 80
EPS = 1e-06
QUERY_CONST = 1.442695041
MASKED = -1e30
BF = jnp.bfloat16
F32 = jnp.float32
VMEM_LIMIT = 60 * 1024 * 1024
CHUNK = 1024
VMEM_LARGE = 60 * 1024 * 1024
CHEAP = pl.CostEstimate(flops=1, bytes_accessed=1, transcendentals=0)


def size(axis):
    return lax.axis_size(axis)


def swap(x, axis):
    return lax.ppermute(x, axis, [(0, 1), (1, 0)])


def flip(blocks, axis):
    if size(axis) != 2:
        return list(blocks)
    first = lax.axis_index(axis) == 0
    a, b = blocks
    return [jnp.where(first, a, b), jnp.where(first, b, a)]


def flip_dim(x, axis, dim):
    if size(axis) != 2:
        return x
    return jnp.concatenate(flip(jnp.split(x, 2, axis=dim), axis), axis=dim)


def gather(x, axis):
    if size(axis) == 2:
        return [x, swap(x, axis)]
    whole = lax.all_gather(x, axis, axis=0, tiled=False)
    return [whole[i] for i in range(size(axis))]


def gather_grid(x):
    if size("row") != 2:
        return [gather(b, "col") for b in gather(x, "row")]
    along_row, along_col = swap(x, "row"), swap(x, "col")
    half = x.shape[0] // 2
    across = jnp.concatenate(
        [swap(along_row[:half], "col"), swap(along_col[half:], "row")], axis=0
    )
    return [[x, along_col], [along_row, across]]


def scatter_sum(x, axis, dim):
    if size(axis) != 2:
        return lax.psum_scatter(x, axis, scatter_dimension=dim, tiled=True)
    mine, theirs = jnp.split(x, 2, axis=dim)
    return (mine.astype(F32) + swap(theirs, axis).astype(F32)).astype(x.dtype)


def exchange(x, axis, split, join):
    if size(axis) != 2:
        return lax.all_to_all(x, axis, split, join, tiled=True)
    mine, theirs = jnp.split(x, 2, axis=split)
    return jnp.concatenate([mine, swap(theirs, axis)], axis=join)


def core_half(x, dim):
    return lax.dynamic_slice_in_dim(
        x, lax.axis_index("core") * (x.shape[dim] // 2), x.shape[dim] // 2, dim
    )


def weight_gather(w, row_dim):
    part = core_half(w, 0)
    blocks = gather_grid(part)
    if row_dim == 1:
        blocks = [list(b) for b in zip(*blocks)]
    mine = jnp.stack([jnp.concatenate(b, axis=1) for b in blocks])
    other = swap(mine, "core")
    first = lax.axis_index("core") == 0
    both = jnp.stack([jnp.where(first, mine, other), jnp.where(first, other, mine)], axis=1)
    return both.reshape(-1, both.shape[-1])


def weight_sum(g, row_dim):
    dim_axis = ("row", "col") if row_dim == 0 else ("col", "row")
    n0 = size(dim_axis[0])
    g = g.reshape(n0, 2, g.shape[0] // n0 // 2, g.shape[1])
    core = lax.axis_index("core")
    keep = lax.dynamic_index_in_dim(g, core, 1, keepdims=False)
    give = lax.dynamic_index_in_dim(g, 1 - core, 1, keepdims=False).astype(BF)
    part = (keep + swap(give, "core").astype(F32)).astype(BF)
    part = scatter_sum(part, dim_axis[0], 0)
    part = scatter_sum(part[0], dim_axis[1], 1)
    return z_sum(part)


def z_sum(part):
    total = lax.psum(part, "z")
    other = swap(total, "core")
    return flip_core(total, other)


def flip_core(total, other):
    first = lax.axis_index("core") == 0
    return jnp.concatenate(
        [jnp.where(first, total, other), jnp.where(first, other, total)], axis=-2
    ).astype(F32)


def dot(a, b, contract):
    return lax.dot_general(a, b, ((contract[0:1], contract[1:2]), ((), ())), preferred_element_type=F32)


def bias_block(series_row, series_col, key_pos, q0, k0, qb, kb, diagonal):
    q_pos = q0 + lax.broadcasted_iota(jnp.int32, (1, qb), 1)
    allowed = (series_col == series_row) & (key_pos <= q_pos)
    if diagonal:
        k_pos = k0 + lax.broadcasted_iota(jnp.int32, (kb, 1), 0)
        allowed = allowed | (k_pos == q_pos)
    return jnp.where(allowed, 0.0, MASKED)


def forward_kernel(block, at, qkv_ref, srow_ref, scol_ref, kpos_ref, out_ref, lse_ref, *rest):
    *pieces, bias_ref, krow_ref, s_ref = rest
    t = qkv_ref.shape[3]
    n = t // block
    krow_ref[...] = qkv_ref[1, 0].astype(F32).T.astype(BF)

    def bias_slot(j, i):
        return j * (j + 1) // 2 + i

    @pl.when(pl.program_id(0) == 0)
    def _():
        for j in range(n):
            for i in range(j + 1):
                keys = pl.ds(i * block, block)
                bias_ref[bias_slot(j, i)] = bias_block(
                    srow_ref[:, j * block : (j + 1) * block],
                    scol_ref[keys, :],
                    kpos_ref[keys, :],
                    j * block,
                    i * block,
                    block,
                    block,
                    i == j,
                )

    for j in range(n):
        cols = slice(j * block, (j + 1) * block)
        q = qkv_ref[0, 0, :, cols]
        top = None
        for i in range(j + 1):
            s = dot(krow_ref[i * block : (i + 1) * block, :], q, (1, 0)) + bias_ref[bias_slot(j, i)]
            s_ref[i * block : (i + 1) * block, :] = s
            here = jnp.max(s, axis=0, keepdims=True)
            top = here if top is None else jnp.maximum(top, here)
        total = jnp.zeros((1, block), F32)
        acc = jnp.zeros((HEAD_DIM, block), F32)
        for i in range(j + 1):
            p = jnp.exp(s_ref[i * block : (i + 1) * block, :] - top)
            total += jnp.sum(p, axis=0, keepdims=True)
            acc += dot(qkv_ref[2, 0, :, i * block : (i + 1) * block], p.astype(BF), (1, 0))
        found = (acc / total).astype(BF)
        out_ref[0, :, cols] = found
        if pieces:
            pieces[0][j, 0] = found
        lse_ref[0, :, cols] = top + jnp.log(total)


def backward_kernel(
    block, at, qkv_ref, raw_ref, factor_ref, out_ref, lse_ref, srow_ref, scol_ref, kpos_ref, *rest
):
    piece, grad_ref, gscale_ref, bias_ref, krow_ref, vrow_ref, gk_ref, gv_ref, gout_ref = rest
    wide = piece.shape[3]
    for j in range(piece.shape[0]):
        gout_ref[:, j * wide : (j + 1) * wide] = piece[j, 0]
    t = qkv_ref.shape[3]
    n = t // block
    krow_ref[...] = qkv_ref[1, 0].astype(F32).T.astype(BF)
    vrow_ref[...] = qkv_ref[2, 0].astype(F32).T.astype(BF)

    def bias_slot(j, i):
        return j * (j + 1) // 2 + i

    @pl.when(pl.program_id(0) == 0)
    def _():
        for j in range(n):
            for i in range(j + 1):
                keys = pl.ds(i * block, block)
                bias_ref[bias_slot(j, i)] = bias_block(
                    srow_ref[:, j * block : (j + 1) * block],
                    scol_ref[keys, :],
                    kpos_ref[keys, :],
                    j * block,
                    i * block,
                    block,
                    block,
                    i == j,
                )

    gscale = jnp.zeros((HEAD_DIM, 1), F32)
    for j in range(n):
        cols = slice(j * block, (j + 1) * block)
        q = qkv_ref[0, 0, :, cols]
        go = gout_ref[:, cols]
        lse = lse_ref[0, :, cols]
        delta = jnp.sum(go.astype(F32) * out_ref[0, :, cols].astype(F32), axis=0, keepdims=True)
        gq = jnp.zeros((HEAD_DIM, block), F32)
        step = max(1, CHUNK // block)
        for i in range(0, j + 1, step):
            many = min(step, j + 1 - i)
            keys = slice(i * block, (i + many) * block)
            slot = bias_slot(j, i)
            bias = bias_ref[slot : slot + many].reshape(many * block, block)
            p = jnp.exp(dot(krow_ref[keys, :], q, (1, 0)) + bias - lse)
            gp = dot(vrow_ref[keys, :], go, (1, 0))
            gs = (p * (gp - delta)).astype(BF)
            gq += dot(qkv_ref[1, 0, :, keys], gs, (1, 0))
            gk = dot(q, gs, (1, 1))
            gv = dot(go, p.astype(BF), (1, 1))
            before, last = slice(i * block, min(i + many, j) * block), slice(j * block, (j + 1) * block)
            old = (min(i + many, j) - i) * block
            if old:
                gk_ref[:, before] += gk[:, :old]
                gv_ref[:, before] += gv[:, :old]
            if i + many == j + 1:
                gk_ref[:, last] = gk[:, old:]
                gv_ref[:, last] = gv[:, old:]
        gscale += jnp.sum(gq * raw_ref[0, :, cols], axis=1, keepdims=True)
        grad_ref[0, 0, :, cols] = (gq * factor_ref[...]).astype(BF)
    grad_ref[1, 0] = gk_ref[...].astype(BF)
    grad_ref[2, 0] = gv_ref[...].astype(BF)
    gscale_ref[0] = gscale


def mask_args(series, padding):
    t = series.shape[0]
    pos = jnp.arange(t, dtype=jnp.int32)
    return series.reshape(1, t), series.reshape(t, 1), jnp.where(padding == 0, pos, t).reshape(t, 1)


def attention_forward(at, qkv, masks, pieces=0):
    _, heads, hd, t = qkv.shape
    block = min(256, t) if t <= 2048 else 512
    n = t // block
    whole = lambda shape: pl.BlockSpec(shape, lambda h: (0,) * len(shape))
    return pl.pallas_call(
        functools.partial(forward_kernel, block),
        grid=(heads,),
        in_specs=[
            pl.BlockSpec(memory_space=pltpu.SMEM),
            pl.BlockSpec((3, 1, hd, t), lambda h: (0, h, 0, 0)),
            whole((1, t)),
            whole((t, 1)),
            whole((t, 1)),
        ],
        out_specs=[
            pl.BlockSpec((1, hd, t), lambda h: (h, 0, 0)),
            pl.BlockSpec((1, 1, t), lambda h: (h, 0, 0)),
        ]
        + [pl.BlockSpec((n, 1, hd, block), lambda h: (0, h, 0, 0))] * pieces,
        out_shape=[
            jax.ShapeDtypeStruct((heads, hd, t), BF),
            jax.ShapeDtypeStruct((heads, 1, t), F32),
        ]
        + [jax.ShapeDtypeStruct((n, heads, hd, block), BF)] * pieces,
        scratch_shapes=[
            pltpu.VMEM((n * (n + 1) // 2, block, block), F32),
            pltpu.VMEM((t, hd), BF),
            pltpu.VMEM((t, block), F32),
        ],
        compiler_params=pltpu.CompilerParams(vmem_limit_bytes=VMEM_LARGE),
        cost_estimate=CHEAP,
        name="attention_forward",
    )(at, qkv, *masks)


def attention_backward(at, qkv, raw, factor, out, piece, lse, masks):
    _, heads, hd, t = qkv.shape
    block = min(256, t) if t <= 2048 else 512
    n = t // block
    whole = lambda shape: pl.BlockSpec(shape, lambda h: (0,) * len(shape))
    head = lambda wide=t: pl.BlockSpec((1, hd, wide), lambda h: (h, 0, 0))
    return pl.pallas_call(
        functools.partial(backward_kernel, block),
        grid=(heads,),
        in_specs=[
            pl.BlockSpec(memory_space=pltpu.SMEM),
            pl.BlockSpec((3, 1, hd, t), lambda h: (0, h, 0, 0)),
            head(),
            whole((hd, 1)),
            head(),
            pl.BlockSpec((1, 1, t), lambda h: (h, 0, 0)),
            whole((1, t)),
            whole((t, 1)),
            whole((t, 1)),
        ]
        + [pl.BlockSpec((piece.shape[0], 1, hd, piece.shape[3]), lambda h: (0, h, 0, 0))],
        out_specs=[
            pl.BlockSpec((3, 1, hd, t), lambda h: (0, h, 0, 0)),
            pl.BlockSpec((1, hd, 1), lambda h: (h, 0, 0)),
        ],
        out_shape=[
            jax.ShapeDtypeStruct((3, heads, hd, t), BF),
            jax.ShapeDtypeStruct((heads, hd, 1), F32),
        ],
        scratch_shapes=[
            pltpu.VMEM((n * (n + 1) // 2, block, block), F32),
            pltpu.VMEM((t, hd), BF),
            pltpu.VMEM((t, hd), BF),
            pltpu.VMEM((hd, t), F32),
            pltpu.VMEM((hd, t), F32),
            pltpu.VMEM((hd, t), BF),
        ],
        compiler_params=pltpu.CompilerParams(vmem_limit_bytes=VMEM_LARGE),
        cost_estimate=CHEAP,
        name="attention_backward",
    )(at, qkv, raw, factor, out, lse, *masks, piece)


def norm_scale(x):
    return lax.rsqrt(jnp.mean(x * x, axis=1, keepdims=True) + EPS)


def body_any(
    inputs, gain_attn, w_qkv, query_scale, w_out, gain_mlp, w_up, b_up, w_down, b_down, series_ids, pad_mask, cotangent
):
    rows, cols = size("row"), size("col")
    tok = inputs.shape[0]
    feat = inputs.shape[1]
    share = tok // cols
    t = series_ids.shape[0]
    head_rows = w_qkv.shape[2] // cols
    heads = head_rows // HEAD_DIM
    r, c = lax.axis_index("row"), lax.axis_index("col")

    blocks = gather_grid(inputs)
    strips = [jnp.concatenate(b, axis=1) for b in blocks]
    x_own = strips[0] if rows == 2 else lax.dynamic_index_in_dim(jnp.stack(strips), r, 0, keepdims=False)
    x_all = jnp.concatenate(flip(strips, "row"), axis=0)
    gain_one = jnp.concatenate(gather(gain_attn, "col"))
    gain_two = jnp.concatenate(gather(gain_mlp, "col"))
    bias_up = jnp.concatenate(gather(b_up, "row")).astype(F32)
    bias_down = jnp.concatenate(gather(b_down, "col")).astype(F32)

    w3 = jnp.transpose(w_qkv, (1, 0, 2)).reshape(3, feat, cols, head_rows)
    w_mine = lax.dynamic_index_in_dim(w3, c, 2, keepdims=False)
    w_give = lax.dynamic_index_in_dim(w3, 1 - c, 2, keepdims=False)
    w_half = swap(core_half(w_give, 1), "col")
    w_other = swap(w_half, "core")
    first = lax.axis_index("core") == 0
    w_full = jnp.concatenate(
        [w_mine, jnp.where(first, w_half, w_other), jnp.where(first, w_other, w_half)], axis=1
    )

    xf = x_all.astype(F32)
    scale_one = norm_scale(xf)
    normed_one = (xf * scale_one * gain_one).astype(BF)
    projected = jnp.einsum("td,sdh->sht", normed_one, w_full, preferred_element_type=F32)
    projected = projected.reshape(3, heads, HEAD_DIM, t)
    factor = QUERY_CONST / math.sqrt(HEAD_DIM) * jax.nn.softplus(query_scale)
    raw_q = projected[0]
    qkv = jnp.stack([raw_q * factor[None, :, None], projected[1], projected[2]]).astype(BF)
    masks = mask_args(series_ids, pad_mask)
    at = jnp.zeros((4,), jnp.int32)
    attended, lse = attention_forward(at, qkv, masks)

    def to_tokens(y):
        y = flip_dim(y.reshape(head_rows, rows, cols, share), "row", 1)
        y = flip_dim(y, "col", 2)
        y = exchange(y.reshape(1, head_rows, rows, cols, share), "row", 2, 0)
        y = exchange(y.reshape(rows, 1, head_rows, cols, share), "col", 3, 1)
        y = flip_dim(y.reshape(rows, cols, head_rows, share), "col", 1)
        return y.reshape(rows * cols * head_rows, share)

    def to_heads(y):
        y = flip_dim(y.reshape(rows, cols, head_rows, share), "col", 1)
        y = exchange(y.reshape(rows, cols, head_rows, 1, share), "col", 1, 3)
        y = exchange(y.reshape(rows, head_rows, 1, cols, share), "row", 0, 2)
        y = flip_dim(y.reshape(head_rows, rows, cols, share), "col", 2)
        return flip_dim(y, "row", 1).reshape(head_rows, t)

    w_out_all = weight_gather(w_out, 0)
    w_up_all = weight_gather(w_up, 1)
    w_down_all = weight_gather(w_down, 0)

    def my_share(y):
        return lax.dynamic_slice_in_dim(y, c * share, share, 0)

    att = to_tokens(attended.reshape(head_rows, t))
    x_mine = my_share(x_own).astype(F32)
    middle = x_mine + dot(att, w_out_all, (0, 0))
    scale_two = norm_scale(middle)
    normed_two = (middle * scale_two * gain_two).astype(BF)
    pre_act = dot(normed_two, w_up_all, (1, 0)) + bias_up
    sig = jax.nn.sigmoid(pre_act)
    hidden = (pre_act * sig).astype(BF)
    result = (middle + dot(hidden, w_down_all, (1, 0)) + bias_down).astype(BF)

    def to_block(y):
        mine, theirs = jnp.split(y, 2, axis=1)
        return jnp.concatenate(flip([mine, swap(theirs, "col")], "col"), axis=0)

    layer_out = to_block(result)

    g_give = lax.dynamic_slice_in_dim(cotangent, (1 - c) * share, share, 0)
    g = jnp.concatenate([my_share(cotangent), swap(g_give, "col")], axis=1)
    grad_w_down = dot(hidden, g, (0, 0))
    grad_hidden = dot(g, w_down_all, (1, 1))
    grad_pre_f = grad_hidden * sig * (1.0 + pre_act * (1.0 - sig))
    grad_pre = grad_pre_f.astype(BF)
    grad_b_up = jnp.sum(grad_pre.astype(F32), axis=0)
    grad_w_up = dot(normed_two, grad_pre, (0, 0))
    grad_normed_two = dot(grad_pre, w_up_all, (1, 1))
    weighted = grad_normed_two * gain_two
    inner = jnp.sum(weighted * middle, axis=1, keepdims=True)
    grad_middle = g.astype(F32) + scale_two * weighted - middle * (scale_two**3 * inner / D)
    grad_gain_mlp = jnp.sum(grad_normed_two * middle * scale_two, axis=0)
    grad_branch = grad_middle.astype(BF)
    grad_w_out = dot(att, grad_branch, (1, 0))
    grad_att = dot(w_out_all, grad_branch, (1, 1)).astype(BF)
    grad_attended = to_heads(grad_att).reshape(heads, HEAD_DIM, t)
    grad_middle_block = to_block(grad_middle)

    sum_down = weight_sum(grad_w_down, 0)
    sum_up = weight_sum(grad_w_up, 1)
    sum_out = weight_sum(grad_w_out, 0)

    grad_proj, gscale = attention_backward(
        at, qkv, raw_q, factor.reshape(HEAD_DIM, 1), attended, grad_attended[None], lse, masks
    )
    slope = QUERY_CONST / math.sqrt(HEAD_DIM) * jax.nn.sigmoid(query_scale)
    grad_query_scale = jnp.sum(gscale, axis=(0, 2)) * slope
    grad_proj = grad_proj.reshape(3, head_rows, t)
    grad_normed_one = jnp.einsum("sht,sdh->td", grad_proj, w_full, preferred_element_type=F32)
    weighted_one = grad_normed_one * gain_one
    inner_one = jnp.sum(weighted_one * xf, axis=1)
    grad_gain_attn = jnp.sum(grad_normed_one * xf * scale_one, axis=0)
    inner_one = lax.psum(inner_one, ("row", "col"))
    grad_w = jnp.einsum("td,sht->sdh", normed_one, grad_proj, preferred_element_type=F32)
    grad_w = grad_w.reshape(3, cols, 2, feat // 2, head_rows)
    core = lax.axis_index("core")
    keep = lax.dynamic_index_in_dim(grad_w, core, 2, keepdims=False)
    give = lax.dynamic_index_in_dim(grad_w, 1 - core, 2, keepdims=False).astype(BF)
    part = (keep + swap(give, "core").astype(F32)).astype(BF)
    part = jnp.concatenate(flip([part[:, 0], swap(part[:, 1], "col")], "col"), axis=2)
    sum_qkv = jnp.transpose(z_sum(part), (1, 0, 2))

    e = jnp.concatenate(flip(jnp.split(grad_normed_one.astype(BF), 2, axis=0), "row"), axis=0) if rows == 2 else (
        grad_normed_one.astype(BF)
    )
    e = scatter_sum(e, "row", 0)
    e = scatter_sum(e, "col", 1).astype(F32)
    my_rows = lambda y: lax.dynamic_slice_in_dim(y, r * tok, tok, 0)
    scale_mine = my_rows(scale_one)
    inner_mine = my_rows(inner_one.reshape(t, 1))
    grad_inputs = grad_middle_block + scale_mine * (e * gain_attn) - inputs.astype(F32) * (
        scale_mine**3 * inner_mine / D
    )

    grad_b_down = jnp.sum(g.astype(F32), axis=0)
    vectors = jnp.concatenate(
        [
            flip_dim(grad_gain_attn, "col", 0),
            flip_dim(grad_gain_mlp, "col", 0),
            flip_dim(grad_b_down, "col", 0),
            flip_dim(grad_b_up, "row", 0),
            grad_query_scale,
        ]
    )
    vectors = lax.psum(vectors, ("z", "core", "row", "col"))
    mine_col = lambda at: lax.dynamic_slice_in_dim(vectors, at * D + c * feat, feat, 0)
    units = b_up.shape[0]
    return (
        layer_out,
        grad_inputs,
        mine_col(0),
        sum_qkv,
        vectors[4 * D :],
        sum_out,
        mine_col(1),
        sum_up,
        lax.dynamic_slice_in_dim(vectors, 3 * D + r * units, units, 0),
        sum_down,
        mine_col(2),
    )


SMEM = pl.BlockSpec(memory_space=pltpu.SMEM)
ANY = pl.BlockSpec(memory_space=pl.ANY)


def call(kernel, name, args, specs, outs, scratch=(), limit=VMEM_LIMIT, out_specs=None):
    more = {} if out_specs is None else {"out_specs": out_specs}
    return pl.pallas_call(
        kernel,
        in_specs=specs,
        **more,
        out_shape=outs,
        scratch_shapes=list(scratch),
        compiler_params=pltpu.CompilerParams(vmem_limit_bytes=limit),
        cost_estimate=CHEAP,
        name=name,
    )(*args)


VM = pl.BlockSpec(memory_space=pltpu.VMEM)
HBM = pl.BlockSpec(memory_space=pltpu.HBM)


def shape(dims, kind):
    return jax.ShapeDtypeStruct(dims, kind)


def project_kernel(
    at, x00, x01, x10, x11, gain, factor, w_mine, w_a, w_b, qkv, raw, normed, scale_own, w_full
):
    r, k = at[0], at[2]
    tok, feat = x00.shape
    hr = w_mine.shape[1]
    half = hr // 2
    for s in range(3):
        w_full[pl.ds(s * hr, hr), 0:feat] = w_mine[s]
        w_full[pl.ds(pl.multiple_of(s * hr + k * half, 16), half), feat:] = w_a[s]
        w_full[pl.ds(pl.multiple_of(s * hr + (1 - k) * half, 16), half), feat:] = w_b[s]
    for i, (a_ref, b_ref) in enumerate(((x00, x01), (x10, x11))):
        a, b = a_ref[...].astype(F32), b_ref[...].astype(F32)
        total = jnp.sum(a * a, axis=1, keepdims=True) + jnp.sum(b * b, axis=1, keepdims=True)
        scale = lax.rsqrt(total / (2 * feat) + EPS)
        if i == 0:
            scale_own[...] = scale
        rows = pl.ds(pl.multiple_of((r ^ i) * tok, tok), tok)
        normed[rows, 0:feat] = (a * scale * gain[:, 0:feat]).astype(BF)
        normed[rows, feat:] = (b * scale * gain[:, feat:]).astype(BF)
        y = normed[rows, :]
        q = dot(w_full[0:hr, :], y, (1, 1))
        raw[:, rows] = q
        qkv[0, :, rows] = (q * factor[...]).astype(BF)
        qkv[1, :, rows] = dot(w_full[hr : 2 * hr, :], y, (1, 1)).astype(BF)
        qkv[2, :, rows] = dot(w_full[2 * hr : 3 * hr, :], y, (1, 1)).astype(BF)


def feed_kernel(
    at, gain, bias_up, bias_down, a, x_own, x_col, g_own, g_col,
    w_out, w_up, w_down, hx, hy, d0, d1, hx2, hy2, d02, d12,
    out_own, gm_own, post, ts, vectors, att, hidden_out, normed_out, g_out, pre_out, branch_out,
    w, x_ref, sems, more_sems,
):
    r, c, k = at[0], at[1], at[2]
    _, hr, share = a.shape
    feat = x_own.shape[1]
    half = feat // 2
    first = d0.shape[1]
    rows = pl.ds(pl.multiple_of(c * share, share), share)

    def start(pairs, sem):
        copies = [pltpu.make_async_copy(src, dst, sem.at[m]) for m, (src, dst) in enumerate(pairs)]
        for copy in copies:
            copy.start()
        return copies

    def place(s):
        return pl.ds(pl.multiple_of(((s // 2) ^ r) * 2 * hr + (s % 2) * hr, 16), hr)

    small = [(a.at[s], att.at[place(s), :]) for s in range(4)]
    small += [(x_own.at[rows, :], x_ref.at[:, 0:feat]), (x_col.at[rows, :], x_ref.at[:, feat:])]
    small += [(g_own.at[rows, :], g_out.at[:, 0:feat]), (g_col, g_out.at[:, feat:])]
    small = start(small, more_sems)
    copies = []
    for n, shard in enumerate((w_out, w_up, w_down)):
        rx, cx, ry, cy = (0, feat, feat, 0) if n == 1 else (feat, 0, 0, feat)
        mine = [(shard, w.at[n, 0:feat, 0:feat])]
        for core, (px, py, p0, p1) in ((k, (hx, hy, d0, d1)), (1 - k, (hx2, hy2, d02, d12))):
            down = core * half
            at_x = pl.ds(pl.multiple_of(rx + down, 16), half)
            at_y = pl.ds(pl.multiple_of(ry + down, 16), half)
            at_0 = pl.ds(pl.multiple_of(feat + down, 16), first)
            at_1 = pl.ds(pl.multiple_of(feat + down + first, 16), half - first)
            mine.append((px.at[n], w.at[n, at_x, cx : cx + feat]))
            mine.append((py.at[n], w.at[n, at_y, cy : cy + feat]))
            mine.append((p0.at[n], w.at[n, at_0, feat : 2 * feat]))
            mine.append((p1.at[n], w.at[n, at_1, feat : 2 * feat]))
        copies.append(start(mine, sems.at[n]))

    for copy in small + copies[0]:
        copy.wait()
    middle = x_ref[...].astype(F32) + dot(att[...], w[0], (0, 0))
    scale = lax.rsqrt(jnp.sum(middle * middle, axis=1, keepdims=True) / D + EPS)
    normed = (middle * scale * gain[...]).astype(BF)
    normed_out[...] = normed
    for copy in copies[1]:
        copy.wait()
    pre = dot(normed, w[1], (1, 0)) + bias_up[...]
    sig = jax.nn.sigmoid(pre)
    hidden = (pre * sig).astype(BF)
    hidden_out[...] = hidden
    for copy in copies[2]:
        copy.wait()
    result = (middle + dot(hidden, w[2], (1, 0)) + bias_down[...]).astype(BF)
    out_own[...] = result[:, :feat]
    post[0] = result[:, feat:]

    grad_pre_f = dot(g_out[...], w[2], (1, 1)) * sig * (1.0 + pre * (1.0 - sig))
    grad_pre = grad_pre_f.astype(BF)
    pre_out[...] = grad_pre
    grad_normed = dot(grad_pre, w[1], (1, 1))
    weighted = grad_normed * gain[...]
    inner = jnp.sum(weighted * middle, axis=1, keepdims=True)
    gf = g_out[...].astype(F32)
    grad_middle = gf + scale * weighted - middle * (scale * scale * scale * inner / D)
    gm_own[...] = grad_middle[:, :feat]
    post[1] = grad_middle[:, feat:].astype(BF)
    branch = grad_middle.astype(BF)
    branch_out[...] = branch
    for s in range(4):
        ts[s] = dot(w[0, place(s), :], branch, (1, 1)).astype(BF)
    vectors[...] = jnp.concatenate(
        [
            jnp.sum(grad_normed * (middle * scale), axis=0, keepdims=True),
            jnp.sum(gf, axis=0, keepdims=True),
            jnp.sum(grad_pre.astype(F32), axis=0, keepdims=True),
        ],
        axis=0,
    )


def feed_weights_kernel(at, att, hidden, normed, g, grad_pre, branch, *rest):
    *grads, stage, turned, sems = rest
    k = at[2]
    feat = g.shape[1] // 2
    half = feat // 2
    quarter = half // 2
    copies = []

    def weight_grad(n, left_ref, right):
        for core, begin in ((k, 0), (1 - k, 8)):
            up, low = (begin + 4, begin) if n == 1 else (begin, begin + 4)
            for b in range(2):
                part = pl.ds(pl.multiple_of(b * feat + core * half, 16), half)
                y = dot(left_ref[part, :], right, (1, 0)).astype(BF)
                for j in range(2):
                    cut = slice(j * feat, (j + 1) * feat)
                    for to, value in ((up + 2 * j + (1 - b), y[:quarter, cut]), (low + 2 * b + (1 - j), y[quarter:, cut])):
                        stage[to, n] = value
                        copy = pltpu.make_async_copy(stage.at[to, n], grads[to].at[n], sems.at[to, n])
                        copy.start()
                        copies.append(copy)

    turned[0] = hidden[...].astype(F32).T.astype(BF)
    weight_grad(2, turned.at[0], g[...])
    turned[1] = normed[...].astype(F32).T.astype(BF)
    weight_grad(1, turned.at[1], grad_pre[...])
    weight_grad(0, att, branch[...])
    for copy in copies:
        copy.wait()


def weight_back_kernel(at, grad, normed, keep, give):
    k = at[2]
    part = keep.shape[2]
    feat = keep.shape[3]
    for ref, core in ((give, 1 - k), (keep, k)):
        for s in range(3):
            rows = pl.ds(pl.multiple_of(core * part, 16), part)
            y = dot(grad[s, rows, :], normed[...], (1, 0)).astype(BF)
            ref[0, s] = y[:, :feat]
            ref[1, s] = y[:, feat:]


def project_back_kernel(
    at, grad, w_full, x00, x01, x10, x11, gain, vectors, scale_grad, es
):
    r, c = at[0], at[1]
    tok, feat = x00.shape
    sums = [jnp.zeros((1, feat), F32), jnp.zeros((1, feat), F32)]
    inners = []
    for i, xs in enumerate(((x00, x01), (x10, x11))):
        rows = pl.ds(pl.multiple_of((r ^ i) * tok, tok), tok)
        left = grad[:, rows]
        products, squares, inner = [], 0.0, 0.0
        for j in range(2):
            cut = slice(j * feat, (j + 1) * feat)
            e = dot(left, w_full[:, cut], (0, 0))
            x = xs[j][...].astype(F32)
            product = e * x
            inner = inner + jnp.sum(product * gain[:, cut], axis=1, keepdims=True)
            squares = squares + jnp.sum(x * x, axis=1, keepdims=True)
            es[2 * (r ^ i) + (c ^ j), 0:tok, :] = e.astype(BF)
            products.append(product)
        scale = lax.rsqrt(squares / (2 * feat) + EPS)
        for j in range(2):
            sums[j] += jnp.sum(products[j] * scale, axis=0, keepdims=True)
        line = jnp.broadcast_to(inner, (tok, 128)).T[0:1, :]
        high = line.astype(BF).astype(F32)
        inners.append(jnp.concatenate([high, line - high], axis=0))
    rows = []
    pairs = [(sums[0], sums[1], c)]
    pairs += [(vectors[n : n + 1, :feat], vectors[n : n + 1, feat:], (c, c, r)[n]) for n in range(3)]
    for own, other, place in pairs:
        rows += [jnp.where(place == 0, own, other), jnp.where(place == 0, other, own)]
    rows = jnp.concatenate(rows + [scale_grad[...], jnp.zeros((5, feat), F32)], axis=0)
    for i in range(2):
        inner = jnp.concatenate([inners[i], jnp.zeros((2, feat - tok), F32)], axis=1)
        extra = jnp.concatenate([inner, rows], axis=0).astype(BF)
        for j in range(2):
            es[2 * (r ^ i) + (c ^ j), tok:, :] = extra


def finish_qkv_kernel(at, mine, theirs, mine2, theirs2, out, rows):
    c, k = at[1], at[2]
    half = mine.shape[1]
    for s in range(3):
        for ref, col, core in ((mine, c, k), (theirs, 1 - c, k), (mine2, c, 1 - k), (theirs2, 1 - c, 1 - k)):
            rows[pl.ds(pl.multiple_of((2 * col + core) * half, 16), half), :] = ref[s].astype(F32)
        out[s] = rows[...].T


def finish_feed_kernel(at, a, b, a2, b2, *outs):
    k = at[2]
    quarter = a.shape[1]
    for n, out in enumerate(outs):
        upper, lower = ((b, b2), (a, a2)) if n == 1 else ((a, a2), (b, b2))
        for i, core in ((0, k), (1, 1 - k)):
            for j, refs in enumerate((upper, lower)):
                to = pl.multiple_of((2 * core + j) * quarter, 16)
                out[pl.ds(to, quarter), :] = refs[i][n].astype(F32)


together = lax.optimization_barrier


def after(x, *earlier):
    return lax.optimization_barrier((x, *earlier))[0]


def add(*parts):
    total = parts[0].astype(F32)
    for part in parts[1:]:
        total = total + part.astype(F32)
    return total.astype(BF)


def all_four(x):
    return lax.all_to_all(x, ("row", "col"), 0, 0, tiled=True)


def z_swap(x, step):
    n = size("z")
    return lax.ppermute(x, "z", [(i, i ^ step) for i in range(n)])


def z_first():
    z = lax.axis_index("z")
    return (z == 0) | (z == 3)


def body_four(
    inputs, gain_attn, w_qkv, query_scale, w_out, gain_mlp, w_up, b_up, w_down, b_down, series_ids, pad_mask, cotangent
):
    tok, feat = inputs.shape
    share = tok // 2
    t = series_ids.shape[0]
    hr = w_qkv.shape[2] // 2
    heads = hr // HEAD_DIM
    half = feat // 2
    r, c, k = lax.axis_index("row"), lax.axis_index("col"), lax.axis_index("core")
    at = jnp.stack([r, c, k, 2 * r + c]).astype(jnp.int32)
    mine_rows = lambda y, part: lax.dynamic_slice_in_dim(y, part * share, share, 0)

    few = heads // 2
    quarter = half // 2
    first_rows = (half * 7 // 20) // 16 * 16
    x01 = swap(inputs, "col")
    x10 = swap(inputs, "row")
    small = swap(jnp.concatenate([gain_attn, gain_mlp, b_down.astype(F32)]), "col")
    up_other = swap(b_up.astype(F32), "row")
    w_turned = jnp.transpose(w_qkv, (1, 2, 0)).reshape(3, 2, hr, feat)
    w_mine = lax.dynamic_index_in_dim(w_turned, c, 1, keepdims=False)
    w_give = lax.dynamic_index_in_dim(w_turned, 1 - c, 1, keepdims=False)
    w_half = core_half(w_give, 1)
    w_a = swap(w_half, "col")
    part = jnp.stack([core_half(w_out, 0), core_half(w_up, 0), core_half(w_down, 0)])
    g_give = mine_rows(cotangent, 1 - c)
    x01, x10, small, up_other, part, g_give, w_mine = lax.optimization_barrier(
        (x01, x10, small, up_other, part, g_give, w_mine)
    )
    x11 = swap(after(x01, w_half), "row")
    w_b = swap(w_a, "core")
    gain_one = jnp.concatenate([gain_attn, small[:feat]]).reshape(1, D)
    gain_two = jnp.concatenate([gain_mlp, small[feat : 2 * feat]]).reshape(1, D)
    bias_down = jnp.concatenate([b_down.astype(F32), small[2 * feat :]]).reshape(1, D)
    bias_up = jnp.concatenate([b_up.astype(F32), up_other]).reshape(1, D)
    factor = QUERY_CONST / math.sqrt(HEAD_DIM) * jax.nn.softplus(query_scale)
    factor_col = factor.reshape(HEAD_DIM, 1)

    part = after(part, x11, w_a)
    hx, hy = swap(part, "row"), swap(part, "col")
    hx2, hy2 = swap(hx, "core"), swap(hy, "core")
    qkv, raw, normed_one, scale_own, w_full = call(
        project_kernel,
        "project",
        (at, inputs, x01, x10, x11, gain_one, jnp.tile(factor_col, (heads, 1)), w_mine, w_a, w_b),
        [SMEM] + [VM] * 9,
        [
            shape((3, hr, t), BF),
            shape((hr, t), F32),
            shape((t, D), BF),
            shape((tok, 1), F32),
            shape((3 * hr, D), BF),
        ],
        limit=VMEM_LARGE,
    )
    qkv = qkv.reshape(3, heads, HEAD_DIM, t)
    masks = mask_args(series_ids, pad_mask)
    attended, lse, a = attention_forward(at, qkv, masks, pieces=1)
    a = all_four(a.reshape(4, hr, share))
    hx_on, hy_on, g_give = lax.optimization_barrier((hx, hy, g_give, lse))[:3]
    d0 = swap(hx_on[:, :first_rows], "col")
    d1 = swap(hy_on[:, first_rows:], "row")
    g_col = swap(g_give, "col")
    d0, d1, g_col, a = together((d0, d1, g_col, a))
    d02, d12 = swap(d0, "core"), swap(d1, "core")
    out_own, gm_own, post, ts, vectors, *factors = call(
        feed_kernel,
        "feed_forward",
        (at, gain_two, bias_up, bias_down, a, inputs, x01, cotangent, g_col)
        + (w_out, w_up, w_down, hx, hy, d0, d1, hx2, hy2, d02, d12),
        [SMEM] + [VM] * 3 + [HBM] * 16,
        [
            shape((share, feat), BF),
            shape((share, feat), F32),
            shape((2, share, feat), BF),
            shape((4, hr, share), BF),
            shape((3, D), F32),
            shape((D, share), BF),
        ]
        + [shape((share, D), BF)] * 5,
        scratch=[
            pltpu.VMEM((3, D, D), BF),
            pltpu.VMEM((share, D), BF),
            pltpu.SemaphoreType.DMA((3, 9)),
            pltpu.SemaphoreType.DMA((8,)),
        ],
        limit=VMEM_LARGE,
    )
    grads = call(
        feed_weights_kernel,
        "feed_weights",
        (at, *factors),
        [SMEM] + [VM] * 6,
        [shape((3, quarter, feat), BF)] * 16,
        scratch=[
            pltpu.VMEM((16, 3, quarter, feat), BF),
            pltpu.VMEM((2, D, share), BF),
            pltpu.SemaphoreType.DMA((16, 3)),
        ],
        out_specs=[HBM] * 16,
        limit=VMEM_LARGE,
    )
    ts = all_four(ts)
    others = grads[8:]
    over = lambda n: swap(others[n], "core")
    grads, osx0, osx1, osy0, osy1 = grads[:8], over(0), over(2), over(4), over(6)
    sx0, kx0, sx1, kx1, sy0, ky0, sy1, ky1 = grads
    sx1, sy1 = add(sx1, osx1), add(sy1, osy1)
    ox0, ox1, oy0, oy1 = over(1), over(3), over(5), over(7)
    sx0, sy0 = add(sx0, osx0), add(sy0, osy0)
    ts, sx1, sy1, sx0, sy0 = together((ts, sx1, sy1, sx0, sy0))
    rx1, ry1 = swap(sx1, "row"), swap(sy1, "col")
    rx0, ry0 = swap(sx0, "row"), swap(sy0, "col")
    ts = ts.reshape(4, heads, HEAD_DIM, share)
    raw = raw.reshape(heads, HEAD_DIM, t)

    grad_proj, gscale = attention_backward(at, qkv, raw, factor_col, attended, ts, lse, masks)
    grad_proj = grad_proj.reshape(3, hr, t)
    kept, sent = call(
        weight_back_kernel,
        "weight_back",
        (at, grad_proj, normed_one),
        [SMEM] + [VM] * 2,
        [shape((2, 3, hr // 2, feat), BF)] * 2,
    )
    sent, rx1, ry1, rx0, ry0, ox0, ox1, oy0, oy1 = together((sent, rx1, ry1, rx0, ry0, ox0, ox1, oy0, oy1))
    got = swap(sent, "core")
    px1, py1 = add(kx1, ox1, rx1), add(ky1, oy1, ry1)
    qx, qy = swap(px1, "col"), swap(py1, "row")
    w_pair = add(kept, got)
    first = z_first()
    got_w = z_swap(jnp.where(first, w_pair[1], w_pair[0]), 1)
    slope = QUERY_CONST / math.sqrt(HEAD_DIM) * jax.nn.sigmoid(query_scale)
    grad_query_scale = jnp.sum(gscale, axis=(0, 2)) * slope
    scale_grad = jnp.pad(grad_query_scale, (0, feat - HEAD_DIM)).reshape(1, feat)
    es = call(
        project_back_kernel,
        "project_back",
        (at, after(grad_proj, w_pair, px1, py1).reshape(3 * hr, t), w_full, inputs, x01, x10, x11, gain_one, vectors, scale_grad),
        [SMEM] + [VM] * 9,
        shape((4, tok + 16, feat), BF),
    )
    kx0, ky0 = together((kx0, ky0, es))[:2]
    fx0 = kx0.astype(F32) + ox0.astype(F32) + rx0.astype(F32)
    fy0 = ky0.astype(F32) + oy0.astype(F32) + ry0.astype(F32)
    qx, qy, got_w, w_pair, es, fx0, fy0 = together((qx, qy, got_w, w_pair, es, fx0, fy0))

    mine_w = add(jnp.where(first, w_pair[0], w_pair[1]), got_w)
    met_w = z_swap(mine_w, 3)
    fx, fy = add(fx0, qx), add(fy0, qy)
    got_c = z_swap(jnp.where(first, fy, fx), 1)
    es = all_four(after(es, fx, fy, mine_w))
    met_w, mine_w, got_c, fx, fy, post = together((met_w, mine_w, got_c, fx, fy, post))

    mine_w = add(mine_w, met_w)
    other_w = z_swap(mine_w, 1)
    w_own, w_theirs = jnp.where(first, mine_w, other_w), jnp.where(first, other_w, mine_w)
    mine_c = add(jnp.where(first, fx, fy), got_c)
    met_c = z_swap(mine_c, 3)
    post = swap(post, "col")
    w_theirs = swap(w_theirs, "col")
    total = jnp.sum(es[:, tok + 2 : tok + 11].astype(F32), axis=0)
    total = total + swap(total, "core")
    total = total + z_swap(total, 1)
    total = total + z_swap(total, 2)
    met_c, mine_c, w_own, w_theirs, post, total = together((met_c, mine_c, w_own, w_theirs, post, total))
    mine_c = add(mine_c, met_c)
    other_c = z_swap(mine_c, 1)
    w_args = (at, w_own, w_theirs, swap(w_own, "core"), swap(w_theirs, "core"))
    sum_qkv = call(
        finish_qkv_kernel,
        "finish_qkv",
        w_args,
        [SMEM] + [VM] * 4,
        shape((3, feat, 2 * hr), F32),
        scratch=[pltpu.VMEM((2 * hr, feat), F32)],
    )
    sum_qkv = jnp.transpose(sum_qkv, (1, 0, 2))

    e = jnp.sum(es[:, :tok].astype(F32), axis=0)
    inner = jnp.sum(es[:, tok : tok + 2, :tok].astype(F32), axis=(0, 1)).reshape(tok, 1)
    grad_middle = jnp.concatenate(flip([gm_own, post[1].astype(F32)], "col"), axis=0)
    grad_inputs = grad_middle + scale_own * (e * gain_attn) - inputs.astype(F32) * (scale_own**3 * inner / D)
    layer_out = jnp.concatenate(flip([out_own, post[0]], "col"), axis=0)

    pick = lambda n, place: lax.dynamic_index_in_dim(total, 2 * n + place, 0, keepdims=False)
    mine_c = after(mine_c, sum_qkv, grad_inputs, layer_out, total)
    fx, fy = jnp.where(first, mine_c, other_c), jnp.where(first, other_c, mine_c)
    sum_out, sum_up, sum_down = call(
        finish_feed_kernel,
        "finish_feed",
        (at, fx, fy, swap(fx, "core"), swap(fy, "core")),
        [SMEM] + [VM] * 4,
        [shape((feat, feat), F32)] * 3,
        limit=24 * 1024 * 1024,
    )

    return (
        layer_out,
        grad_inputs,
        pick(0, c),
        sum_qkv,
        total[8, :HEAD_DIM],
        sum_out,
        pick(1, c),
        sum_up,
        pick(3, r),
        sum_down,
        pick(2, c),
    )


def solution(mesh):
    dp, rows, cols = mesh.shape["dp"], mesh.shape["row"], mesh.shape["col"]
    split = Mesh(mesh.devices.reshape(dp // 2, 2, rows, cols), ("z", "core", "row", "col"))
    tokens = P(("z", "core", "row"), "col")
    in_specs = (
        tokens,
        P("col"),
        P("col", None, "row"),
        P(),
        P("row", "col"),
        P("col"),
        P("col", "row"),
        P("row"),
        P("row", "col"),
        P("col"),
        P(("z", "core")),
        P(("z", "core")),
        tokens,
    )
    out_specs = (
        tokens,
        tokens,
        P("col"),
        P("col", None, "row"),
        P(),
        P("row", "col"),
        P("col"),
        P("col", "row"),
        P("row"),
        P("row", "col"),
        P("col"),
    )
    body = body_four if (dp, rows, cols) == (8, 2, 2) else body_any
    return jax.shard_map(body, mesh=split, in_specs=in_specs, out_specs=out_specs, check_vma=False)
```

profile of v0, /device:TPU:0, one launch (start us, length us, event | category | flops | bytes accessed | tf_op | source)
XLA Modules:
  0.0 289.2 jit_solution(18017354632560926317)
XLA Ops:
  0.6 3.0 %collective-permute-start = (bf16[512,640]{1,0:T(8,128)(2,1)}, bf16[512,640]{1,0:T(8,128)(2,1)S(1)}, u32[]{:S(2)}, u32[]{:S(2)}) collective-permute-start(bf16[512,640]{1,0:T(8,128)(2,1)} %x00.3), channel_id=1, source_target_pairs={{0,1},{1,0},{2,3},{3,2},{4,5},{5,4},{6,7},{7,6},{8,9},{9,8},{10,11... | collective-permute-start | bytes 1966088 | tf_op jit(solution)/shard_map/ppermute | solution.py:30
  3.7 1.5 collective-permute-start.1
  7.9 3.9 %copy.27 = bf16[640,3,640]{0,2,1:T(8,128)(2,1)S(1)} copy(bf16[640,3,640]{2,0,1:T(8,128)(2,1)} %param.15) | data formatting | bytes 4915200 | tf_op args[2]
  11.9 1.1 dynamic-slice_bitcast_fusion.4
  13.3 1.1 dynamic-slice_bitcast_fusion.w_mine
  14.5 1.2 pad_maximum_fusion
  16.5 3.8 %collective-permute-done.3 = f32[640]{0:T(1024)S(1)} collective-permute-done((f32[640]{0:T(1024)S(1)}, f32[640]{0:T(1024)S(1)}, u32[]{:S(2)}, u32[]{:S(2)}) %collective-permute-start.3) | collective-permute-done | bytes 2592 | tf_op jit(solution)/shard_map/ppermute | solution.py:30
  20.3 1.6 collective-permute-start.4
  22.3 13.7 %collective-permute-done.5.w_a = bf16[3,160,640]{2,1,0:T(8,128)(2,1)S(1)} collective-permute-done((bf16[3,160,640]{2,1,0:T(8,128)(2,1)S(1)}, bf16[3,160,640]{2,1,0:T(8,128)(2,1)S(1)}, u32[]{:S(2)}, u32[]{:S(2)}) %collective-permute-start.5) | collective-permute-done | bytes 614432 | tf_op jit(solution)/shard_map/ppermute | solution.py:30
  38.9 1.0 copy.30.kpos_ref
  39.9 1.0 copy.29.scol_ref
  42.8 8.1 %project.1 = (bf16[3,320,1024]{2,1,0:T(8,128)(2,1)}, f32[320,1024]{1,0:T(8,128)}, bf16[1024,1280]{1,0:T(8,128)(2,1)}, f32[512,1]{1,0:T(8,128)}, bf16[960,1280]{1,0:T(8,128)(2,1)}) custom-call(s32[4]{0:T(128)} %pad_add_fusion.at, bf16[512,640]{1,0:T(8,128)(2,1)} %x00.3, bf16[512,640]{1,0:T(8,128)(2,1)} %copy-done.2, ...), custom_call_target="tpu_custom_call" | custom-call | flops 1 | bytes 1 | tf_op jit(solution)/shard_map/project/pallas_call | solution.py:508
  50.9 10.4 %attention_forward.1 = (bf16[4,80,1024]{2,1,0:T(8,128)(2,1)}, f32[4,1,1024]{2,1,0:T(1,128)}, bf16[4,4,80,256]{3,2,1,0:T(8,128)(2,1)}) custom-call(s32[4]{0:T(128)} %pad_add_fusion.at, bf16[3,4,80,1024]{3,2,1,0:T(8,128)(2,1)} %bitcast.46, s32[1,1024]{1,0:T(1,128)} %bitcast.53, s32[1024,1]{1,0:T(8,128)} %copy.29.scol_ref, s32[1024,1]{1,0:T(8,128)} %copy.30.kpos_ref), custom_call_target="tpu_custom_call" | custom-call | flops 1 | bytes 1 | tf_op jit(solution)/shard_map/attention_forward/pallas_call | solution.py:260
  61.3 2.3 collective-permute-done.6.hx
  63.8 1.0 slice.49
  64.8 1.4 collective-permute-start.10
  66.2 3.7 %all-to-all-start = ((bf16[4,320,256]{2,1,0:T(8,128)(2,1)}), bf16[4,320,256]{2,1,0:T(8,128)(2,1)S(1)}, u32[]{:S(2)}, u32[]{:S(2)}) async-start(bf16[4,320,256]{2,1,0:T(8,128)(2,1)} %bitcast.16), calls=%async_computation | async-start | bytes 1310720 | tf_op jit(solution)/shard_map/all_to_all | solution.py:757
  69.9 1.1 slice.48
  70.9 1.9 collective-permute-start.9
  73.5 16.3 %all-to-all-done.a = bf16[4,320,256]{2,1,0:T(8,128)(2,1)S(1)} async-done(((bf16[4,320,256]{2,1,0:T(8,128)(2,1)}), bf16[4,320,256]{2,1,0:T(8,128)(2,1)S(1)}, u32[]{:S(2)}, u32[]{:S(2)}) %all-to-all-start) | async-done | bytes 655392 | tf_op jit(solution)/shard_map/all_to_all | solution.py:757
  89.8 3.8 %collective-permute-done.11.g_col = bf16[256,640]{1,0:T(8,128)(2,1)} collective-permute-done((bf16[256,640]{1,0:T(8,128)(2,1)}, bf16[256,640]{1,0:T(8,128)(2,1)}, u32[]{:S(2)}, u32[]{:S(2)}) %collective-permute-start.11) | collective-permute-done | bytes 327712 | tf_op jit(solution)/shard_map/ppermute | solution.py:30
  99.2 13.4 %feed_forward.1 = (bf16[256,640]{1,0:T(8,128)(2,1)}, f32[256,640]{1,0:T(8,128)}, bf16[2,256,640]{2,1,0:T(8,128)(2,1)}, bf16[4,320,256]{2,1,0:T(8,128)(2,1)}, f32...) custom-call(s32[4]{0:T(128)} %pad_add_fusion.at, ...), custom_call_target="tpu_custom_call" | custom-call | flops 1 | bytes 1 | tf_op jit(solution)/shard_map/feed_forward/pallas_call | solution.py:508
  112.7 6.8 %feed_weights.1 = (bf16[3,160,640]{2,1,0:T(8,128)(2,1)}, bf16[3,160,640]{2,1,0:T(8,128)(2,1)}, bf16[3,160,640]{2,1,0:T(8,128)(2,1)}, bf16[3,160,640]{2,1,0:T(8,1...) custom-call(s32[4]{0:T(128)} %pad_add_fusion.at, ...), custom_call_target="tpu_custom_call" | custom-call | flops 1 | bytes 1 | tf_op jit(solution)/shard_map/feed_weights/pallas_call | solution.py:508
  120.6 3.7 %all-to-all-start.1 = ((bf16[4,320,256]{2,1,0:T(8,128)(2,1)}), bf16[4,320,256]{2,1,0:T(8,128)(2,1)S(1)}, u32[]{:S(2)}, u32[]{:S(2)}) async-start(bf16[4,320,256]{2,1,0:T(8,128)(2,1)} %get-tuple-element.136), calls=%async_computation.1 | async-start | bytes 1310720 | tf_op jit(solution)/shard_map/all_to_all | solution.py:757
  125.3 1.2 add_convert_fusion.8
  127.1 1.2 add_convert_fusion.9
  129.1 1.2 add_convert_fusion.10
  131.2 1.2 add_convert_fusion.11
  132.4 1.6 all-to-all-done.1
  134.0 1.4 collective-permute-start.20
  136.0 1.5 collective-permute-start.22
  138.8 12.5 %attention_backward.1 = (bf16[3,4,80,1024]{3,2,1,0:T(8,128)(2,1)}, f32[4,80,1]{2,1,0:T(8,128)}) custom-call(s32[4]{0:T(128)} %pad_add_fusion.at, bf16[3,4,80,1024]{3,2,1,0:T(8,128)(2,1)} %bitcast.47, f32[4,80,1024]{2,1,0:T(8,128)} %bitcast.52, f32[80,1]{1,0:T(8,128)} %copy.31.factor_ref, bf16[4,80,1024]{2,1,0:T(8,128)(2,1)} %get-tuple-element.135.out_ref, ...), custom_call_target="tpu_custom_call" | custom-call | flops 1 | bytes 1 | tf_op jit(solution)/shard_map/attention_backward/pallas_call | solution.py:297
  151.3 6.2 %weight_back.1 = (bf16[2,3,160,640]{3,2,1,0:T(8,128)(2,1)}, bf16[2,3,160,640]{3,2,1,0:T(8,128)(2,1)}) custom-call(s32[4]{0:T(128)} %pad_add_fusion.at, bf16[3,320,1024]{2,1,0:T(8,128)(2,1)} %bitcast.44, bf16[1024,1280]{1,0:T(8,128)(2,1)} %get-tuple-element.147.normed), custom_call_target="tpu_custom_call" | custom-call | flops 1 | bytes 1 | tf_op jit(solution)/shard_map/weight_back/pallas_call | solution.py:508
  157.5 5.2 %collective-permute-done.22 = bf16[3,160,640]{2,1,0:T(8,128)(2,1)} collective-permute-done((bf16[3,160,640]{2,1,0:T(8,128)(2,1)S(1)}, bf16[3,160,640]{2,1,0:T(8,128)(2,1)}, u32[]{:S(2)}, u32[]{:S(2)}) %collective-permute-start.22) | collective-permute-done | bytes 614432 | tf_op jit(solution)/shard_map/ppermute | solution.py:30
  162.7 1.5 collective-permute-done.23
  164.3 1.5 add_convert_fusion.6
  166.3 1.6 add_convert_fusion.7
  170.1 1.6 collective-permute-start.31
  172.3 8.6 %project_back.1 = bf16[4,528,640]{2,1,0:T(8,128)(2,1)} custom-call(s32[4]{0:T(128)} %pad_add_fusion.at, bf16[960,1024]{1,0:T(8,128)(2,1)} %bitcast.45, bf16[960,1280]{1,0:T(8,128)(2,1)} %get-tuple-element.165.w_full, bf16[512,640]{1,0:T(8,128)(2,1)} %x00.3, bf16[512,640]{1,0:T(8,128)(2,1)} %copy-done.2, bf16[512,640]{1,0:T(8,128)(2,1)} %collective-permute-done.1.x10, ...), custom_call_target="tpu_custom_call" | custom-call | flops 1 | bytes 1 | tf_op jit(solution)/shard_map/project_back/pallas_call | solution.py:508
  180.9 1.5 convert_add_fusion.1
  182.4 1.5 convert_add_fusion.2
  184.0 2.0 collective-permute-done.31
  186.2 2.7 broadcast_select_fusion.4
  188.9 3.9 %all-to-all-start.2 = ((bf16[4,528,640]{2,1,0:T(8,128)(2,1)}), bf16[4,528,640]{2,1,0:T(8,128)(2,1)S(1)}, u32[]{:S(2)}, u32[]{:S(2)}) async-start(bf16[4,528,640]{2,1,0:T(8,128)(2,1)} %project_back.1), calls=%async_computation.2 | async-start | bytes 5406720 | tf_op jit(solution)/shard_map/all_to_all | solution.py:757
  192.9 1.6 collective-permute-start.33
  194.5 2.5 collective-permute-start.32
  197.0 12.2 %collective-permute-done.33 = bf16[3,160,640]{2,1,0:T(8,128)(2,1)S(1)} collective-permute-done((bf16[3,160,640]{2,1,0:T(8,128)(2,1)}, bf16[3,160,640]{2,1,0:T(8,128)(2,1)S(1)}, u32[]{:S(2)}, u32[]{:S(2)}) %collective-permute-start.33) | collective-permute-done | bytes 614432 | tf_op jit(solution)/shard_map/ppermute | solution.py:762
  209.1 14.0 %collective-permute-done.32 = bf16[3,160,640]{2,1,0:T(8,128)(2,1)S(1)} collective-permute-done((bf16[3,160,640]{2,1,0:T(8,128)(2,1)S(1)}, bf16[3,160,640]{2,1,0:T(8,128)(2,1)S(1)}, u32[]{:S(2)}, u32[]{:S(2)}) %collective-permute-start.32) | collective-permute-done | bytes 614432 | tf_op jit(solution)/shard_map/ppermute | solution.py:762
  224.2 1.5 add_convert_fusion.3
  225.6 3.2 %collective-permute-start.34 = (bf16[3,160,640]{2,1,0:T(8,128)(2,1)S(1)}, bf16[3,160,640]{2,1,0:T(8,128)(2,1)}, u32[]{:S(2)}, u32[]{:S(2)}) collective-permute-start(bf16[3,160,640]{2,1,0:T(8,128)(2,1)S(1)} %add_convert_fusion.3), channel_id=1, source_target_pairs={{0,24},{8,16},{16,8},{24,0},{1,25},{9,17},{17,9},{25,1},{2,26},{10... | collective-permute-start | bytes 1843208 | tf_op jit(solution)/shard_map/ppermute | solution.py:762
  228.8 1.4 collective-permute-start.37
  230.2 21.4 %collective-permute-done.35 = bf16[3,160,640]{2,1,0:T(8,128)(2,1)} collective-permute-done((bf16[3,160,640]{2,1,0:T(8,128)(2,1)}, bf16[3,160,640]{2,1,0:T(8,128)(2,1)}, u32[]{:S(2)}, u32[]{:S(2)}) %collective-permute-start.35) | collective-permute-done | bytes 614432 | tf_op jit(solution)/shard_map/ppermute | solution.py:762
  251.6 2.4 broadcast_select_fusion.2
  254.8 1.4 convert_reduce_fusion
  256.5 3.8 %collective-permute-done.39 = f32[9,640]{1,0:T(8,128)S(1)} collective-permute-done((f32[9,640]{1,0:T(8,128)S(1)}, f32[9,640]{1,0:T(8,128)S(1)}, u32[]{:S(2)}, u32[]{:S(2)}) %collective-permute-start.39) | collective-permute-done | bytes 23072 | tf_op jit(solution)/shard_map/ppermute | solution.py:762
  260.3 1.2 fusion.7
  261.5 3.8 %collective-permute-done.40 = f32[9,640]{1,0:T(8,128)S(1)} collective-permute-done((f32[9,640]{1,0:T(8,128)S(1)}, f32[9,640]{1,0:T(8,128)S(1)}, u32[]{:S(2)}, u32[]{:S(2)}) %collective-permute-start.40) | collective-permute-done | bytes 23072 | tf_op jit(solution)/shard_map/ppermute | solution.py:762
  265.9 1.2 add_convert_fusion.1
  267.4 1.1 bitcast_select_fusion.1
  269.4 1.2 convert_select_fusion.1
  271.0 1.4 fusion
  274.0 5.5 %finish_qkv.1 = f32[3,640,640]{2,1,0:T(8,128)} custom-call(s32[4]{0:T(128)} %pad_add_fusion.at, bf16[3,160,640]{2,1,0:T(8,128)(2,1)} %get-tuple-element.195.mine, bf16[3,160,640]{2,1,0:T(8,128)(2,1)} %collective-permute-done.36.theirs, bf16[3,160,640]{2,1,0:T(8,128)(2,1)} %copy-done.27, bf16[3,160,640]{2,1,0:T(8,128)(2,1)} %copy-done.28), custom_call_target="tpu_custom_call" | custom-call | flops 1 | bytes 1 | tf_op jit(solution)/shard_map/finish_qkv/pallas_call | solution.py:508
  279.5 3.6 %collective-permute-done.43 = bf16[3,160,640]{2,1,0:T(8,128)(2,1)S(1)} collective-permute-done((bf16[3,160,640]{2,1,0:T(8,128)(2,1)S(1)}, bf16[3,160,640]{2,1,0:T(8,128)(2,1)S(1)}, u32[]{:S(2)}, u32[]{:S(2)}) %collective-permute-start.43) | collective-permute-done | bytes 614432 | tf_op jit(solution)/shard_map/ppermute | solution.py:762
  286.2 3.0 %finish_feed.1 = (f32[640,640]{1,0:T(8,128)}, f32[640,640]{1,0:T(8,128)}, f32[640,640]{1,0:T(8,128)}) custom-call(s32[4]{0:T(128)S(1)} %copy-done, bf16[3,160,640]{2,1,0:T(8,128)(2,1)S(1)} %get-tuple-element.215.a, bf16[3,160,640]{2,1,0:T(8,128)(2,1)S(1)} %get-tuple-element.214.b, bf16[3,160,640]{2,1,0:T(8,128)(2,1)S(1)} %collective-permute-done.44.a2, ...), custom_call_target="tpu_custom_call" | custom-call | flops 1 | bytes 1 | tf_op jit(solution)/shard_map/finish_feed/pallas_call | solution.py:508
  (188 shorter events, 34.5 us)
Async XLA Ops:
  0.6 19.6 %collective-permute-start = (bf16[512,640]{1,0:T(8,128)(2,1)}, bf16[512,640]{1,0:T(8,128)(2,1)S(1)}, u32[]{:S(2)}, u32[]{:S(2)}) collective-permute-start(bf16[512,640]{1,0:T(8,128)(2,1)} %x00.3), channel_id=1, source_target_pairs={{0,1},{1,0},{2,3},{3,2},{4,5},{5,4},{6,7},{7,6},{8,9},{9,8},{10,11... | collective-permute-start | bytes 1966088 | tf_op jit(solution)/shard_map/ppermute | solution.py:30
  3.7 16.6 %collective-permute-start.1 = (bf16[512,640]{1,0:T(8,128)(2,1)}, bf16[512,640]{1,0:T(8,128)(2,1)}, u32[]{:S(2)}, u32[]{:S(2)}) collective-permute-start(bf16[512,640]{1,0:T(8,128)(2,1)} %x00.3), channel_id=1, source_target_pairs={{0,2},{2,0},{1,3},{3,1},{4,6},{6,4},{5,7},{7,5},{8,10},{10,8},{9,1... | collective-permute-start | bytes 1966088 | tf_op jit(solution)/shard_map/ppermute | solution.py:30
  6.6 13.7 %collective-permute-start.2 = (f32[1920]{0:T(1024)S(1)}, f32[1920]{0:T(1024)S(1)}, u32[]{:S(2)}, u32[]{:S(2)}) collective-permute-start(f32[1920]{0:T(1024)S(1)} %pad_maximum_fusion.2), channel_id=1, source_target_pairs={{0,1},{1,0},{2,3},{3,2},{4,5},{5,4},{6,7},{7,6},{8,9},{9,8},{10,11... | collective-permute-start | bytes 23048 | tf_op jit(solution)/shard_map/ppermute | solution.py:30
  7.8 12.5 %collective-permute-start.3 = (f32[640]{0:T(1024)S(1)}, f32[640]{0:T(1024)S(1)}, u32[]{:S(2)}, u32[]{:S(2)}) collective-permute-start(f32[640]{0:T(1024)S(1)} %convert_element_type.167), channel_id=1, source_target_pairs={{0,2},{2,0},{1,3},{3,1},{4,6},{6,4},{5,7},{7,5},{8,10},{10,8},{9,1... | collective-permute-start | bytes 7688 | tf_op jit(solution)/shard_map/ppermute | solution.py:30
  14.5 23.5 %copy-start.38 = (f32[80]{0:T(128)S(1)}, f32[80]{0:T(128)}, u32[]{:S(2)}) copy-start(f32[80]{0:T(128)} %param.16) | copy-start | bytes 964
  14.5 24.4 %copy-start.36 = (s32[1024]{0:T(1024)S(1)}, s32[1024]{0:T(1024)}, u32[]{:S(2)}) copy-start(s32[1024]{0:T(1024)} %param.24) | copy-start | bytes 12292
  15.7 24.3 %copy-start.32 = (s32[1024]{0:T(1024)S(1)}, s32[1024]{0:T(1024)}, u32[]{:S(2)}) copy-start(s32[1024]{0:T(1024)} %param.23) | copy-start | bytes 12292
  15.7 26.5 %copy-start.33 = (f32[640]{0:T(1024)S(1)}, f32[640]{0:T(1024)}, u32[]{:S(2)}) copy-start(f32[640]{0:T(1024)} %param.14) | copy-start | bytes 7684
  20.2 41.1 %copy-start.37 = (f32[640]{0:T(1024)}, f32[640]{0:T(1024)S(1)}, u32[]{:S(2)}) copy-start(f32[640]{0:T(1024)S(1)} %collective-permute-done.3) | copy-start | bytes 7684
  20.2 22.6 %copy-start.2 = (bf16[512,640]{1,0:T(8,128)(2,1)}, bf16[512,640]{1,0:T(8,128)(2,1)S(1)}, u32[]{:S(2)}) copy-start(bf16[512,640]{1,0:T(8,128)(2,1)S(1)} %collective-permute-done.x01.x_col) | copy-start | bytes 1966084
  20.3 15.7 %collective-permute-start.4 = (bf16[512,640]{1,0:T(8,128)(2,1)S(1)}, bf16[512,640]{1,0:T(8,128)(2,1)S(1)}, u32[]{:S(2)}, u32[]{:S(2)}) collective-permute-start(bf16[512,640]{1,0:T(8,128)(2,1)S(1)} %collective-permute-done.x01.x_col), channel_id=1, source_target_pairs={{0,2},{2,0},{1,3},{3,1},{4,6},{6,4},{5,7},{7,5},{8,10},{10,8},{9,1... | collective-permute-start | bytes 1966088 | tf_op jit(solution)/shard_map/ppermute | solution.py:30
  21.8 14.2 %collective-permute-start.5 = (bf16[3,160,640]{2,1,0:T(8,128)(2,1)S(1)}, bf16[3,160,640]{2,1,0:T(8,128)(2,1)S(1)}, u32[]{:S(2)}, u32[]{:S(2)}) collective-permute-start(bf16[3,160,640]{2,1,0:T(8,128)(2,1)S(1)} %dynamic-slice_bitcast_fusion.1), channel_id=1, source_target_pairs={{0,1},{1,0},{2,3},{3,2},{4,5},{5,4},{6,7},{7,6},{8,9},{9,8},{10,11... | collective-permute-start | bytes 1843208 | tf_op jit(solution)/shard_map/ppermute | solution.py:30
  36.8 26.7 %collective-permute-start.6 = (bf16[3,320,640]{2,1,0:T(8,128)(2,1)}, bf16[3,320,640]{2,1,0:T(8,128)(2,1)}, u32[]{:S(2)}, u32[]{:S(2)}) collective-permute-start(bf16[3,320,640]{2,1,0:T(8,128)(2,1)} %pad_maximum_fusion), channel_id=1, source_target_pairs={{0,2},{2,0},{1,3},{3,1},{4,6},{6,4},{5,7},{7,5},{8,10},{10,8},{9,1... | collective-permute-start | bytes 3686408 | tf_op jit(solution)/shard_map/ppermute | solution.py:30
  37.4 26.4 %collective-permute-start.7 = (bf16[3,320,640]{2,1,0:T(8,128)(2,1)}, bf16[3,320,640]{2,1,0:T(8,128)(2,1)S(1)}, u32[]{:S(2)}, u32[]{:S(2)}) collective-permute-start(bf16[3,320,640]{2,1,0:T(8,128)(2,1)} %pad_maximum_fusion), channel_id=1, source_target_pairs={{0,1},{1,0},{2,3},{3,2},{4,5},{5,4},{6,7},{7,6},{8,9},{9,8},{10,11... | collective-permute-start | bytes 3686408 | tf_op jit(solution)/shard_map/ppermute | solution.py:30
  38.9 3.9 %collective-permute-start.8 = (bf16[3,160,640]{2,1,0:T(8,128)(2,1)}, bf16[3,160,640]{2,1,0:T(8,128)(2,1)}, u32[]{:S(2)}, u32[]{:S(2)}) collective-permute-start(bf16[3,160,640]{2,1,0:T(8,128)(2,1)} %copy-done.26), channel_id=1, source_target_pairs={{0,4},{4,0},{1,5},{5,1},{2,6},{6,2},{3,7},{7,3},{8,12},{12,8},{9,1... | collective-permute-start | bytes 1843208 | tf_op jit(solution)/shard_map/ppermute | solution.py:30
  63.8 9.0 %copy-start.4 = (bf16[3,320,640]{2,1,0:T(8,128)(2,1)}, bf16[3,320,640]{2,1,0:T(8,128)(2,1)S(1)}, u32[]{:S(2)}) copy-start(bf16[3,320,640]{2,1,0:T(8,128)(2,1)S(1)} %collective-permute-done.7.hy) | copy-start | bytes 3686404
  64.8 30.7 %copy-start.34 = (f32[640]{0:T(1024)S(1)}, f32[640]{0:T(1024)}, u32[]{:S(2)}) copy-start(f32[640]{0:T(1024)} %param.18) | copy-start | bytes 7684
  64.8 28.9 %collective-permute-start.10 = (bf16[3,208,640]{2,1,0:T(8,128)(2,1)}, bf16[3,208,640]{2,1,0:T(8,128)(2,1)}, u32[]{:S(2)}, u32[]{:S(2)}) collective-permute-start(bf16[3,208,640]{2,1,0:T(8,128)(2,1)} %slice.49), channel_id=1, source_target_pairs={{0,2},{2,0},{1,3},{3,1},{4,6},{6,4},{5,7},{7,5},{8,10},{10,8},{9,1... | collective-permute-start | bytes 2396168 | tf_op jit(solution)/shard_map/ppermute | solution.py:30
  66.2 23.6 %all-to-all-start = ((bf16[4,320,256]{2,1,0:T(8,128)(2,1)}), bf16[4,320,256]{2,1,0:T(8,128)(2,1)S(1)}, u32[]{:S(2)}, u32[]{:S(2)}) async-start(bf16[4,320,256]{2,1,0:T(8,128)(2,1)} %bitcast.16), calls=%async_computation | async-start | bytes 1310720 | tf_op jit(solution)/shard_map/all_to_all | solution.py:757
  70.9 22.7 %collective-permute-start.9 = (bf16[3,112,640]{2,1,0:T(8,128)(2,1)S(1)}, bf16[3,112,640]{2,1,0:T(8,128)(2,1)}, u32[]{:S(2)}, u32[]{:S(2)}) collective-permute-start(bf16[3,112,640]{2,1,0:T(8,128)(2,1)S(1)} %slice.48), channel_id=1, source_target_pairs={{0,1},{1,0},{2,3},{3,2},{4,5},{5,4},{6,7},{7,6},{8,9},{9,8},{10,11... | collective-permute-start | bytes 1290248 | tf_op jit(solution)/shard_map/ppermute | solution.py:30
  72.8 25.3 %collective-permute-start.12 = (bf16[3,320,640]{2,1,0:T(8,128)(2,1)}, bf16[3,320,640]{2,1,0:T(8,128)(2,1)S(1)}, u32[]{:S(2)}, u32[]{:S(2)}) collective-permute-start(bf16[3,320,640]{2,1,0:T(8,128)(2,1)} %collective-permute-done.6.hx), channel_id=1, source_target_pairs={{0,4},{4,0},{1,5},{5,1},{2,6},{6,2},{3,7},{7,3},{8,12},{12,8},{9,1... | collective-permute-start | bytes 3686408 | tf_op jit(solution)/shard_map/ppermute | solution.py:30
  72.8 25.3 %collective-permute-start.13 = (bf16[3,320,640]{2,1,0:T(8,128)(2,1)S(1)}, bf16[3,320,640]{2,1,0:T(8,128)(2,1)}, u32[]{:S(2)}, u32[]{:S(2)}) collective-permute-start(bf16[3,320,640]{2,1,0:T(8,128)(2,1)S(1)} %collective-permute-done.7.hy), channel_id=1, source_target_pairs={{0,4},{4,0},{1,5},{5,1},{2,6},{6,2},{3,7},{7,3},{8,12},{12,8},{9,1... | collective-permute-start | bytes 3686408 | tf_op jit(solution)/shard_map/ppermute | solution.py:30
  73.3 20.3 %collective-permute-start.11 = (bf16[256,640]{1,0:T(8,128)(2,1)}, bf16[256,640]{1,0:T(8,128)(2,1)}, u32[]{:S(2)}, u32[]{:S(2)}) collective-permute-start(bf16[256,640]{1,0:T(8,128)(2,1)} %constant_dynamic-slice_fusion), channel_id=1, source_target_pairs={{0,1},{1,0},{2,3},{3,2},{4,5},{5,4},{6,7},{7,6},{8,9},{9,8},{10,11... | collective-permute-start | bytes 983048 | tf_op jit(solution)/shard_map/ppermute | solution.py:30
  89.8 8.3 %copy-start.5 = (bf16[4,320,256]{2,1,0:T(8,128)(2,1)}, bf16[4,320,256]{2,1,0:T(8,128)(2,1)S(1)}, u32[]{:S(2)}) copy-start(bf16[4,320,256]{2,1,0:T(8,128)(2,1)S(1)} %all-to-all-done.a) | copy-start | bytes 1966084
  93.7 4.4 %collective-permute-start.15 = (bf16[3,208,640]{2,1,0:T(8,128)(2,1)}, bf16[3,208,640]{2,1,0:T(8,128)(2,1)}, u32[]{:S(2)}, u32[]{:S(2)}) collective-permute-start(bf16[3,208,640]{2,1,0:T(8,128)(2,1)} %collective-permute-done.10.d1), channel_id=1, source_target_pairs={{0,4},{4,0},{1,5},{5,1},{2,6},{6,2},{3,7},{7,3},{8,12},{12,8},{9,1... | collective-permute-start | bytes 2396168 | tf_op jit(solution)/shard_map/ppermute | solution.py:30
  93.7 4.4 %collective-permute-start.14 = (bf16[3,112,640]{2,1,0:T(8,128)(2,1)}, bf16[3,112,640]{2,1,0:T(8,128)(2,1)S(1)}, u32[]{:S(2)}, u32[]{:S(2)}) collective-permute-start(bf16[3,112,640]{2,1,0:T(8,128)(2,1)} %collective-permute-done.9.d0), channel_id=1, source_target_pairs={{0,4},{4,0},{1,5},{5,1},{2,6},{6,2},{3,7},{7,3},{8,12},{12,8},{9,1... | collective-permute-start | bytes 1290248 | tf_op jit(solution)/shard_map/ppermute | solution.py:30
  119.5 5.0 %collective-permute-start.19 = (bf16[3,160,640]{2,1,0:T(8,128)(2,1)}, bf16[3,160,640]{2,1,0:T(8,128)(2,1)S(1)}, u32[]{:S(2)}, u32[]{:S(2)}) collective-permute-start(bf16[3,160,640]{2,1,0:T(8,128)(2,1)} %get-tuple-element.144), channel_id=1, source_target_pairs={{0,4},{4,0},{1,5},{5,1},{2,6},{6,2},{3,7},{7,3},{8,12},{12,8},{9,1... | collective-permute-start | bytes 1843208 | tf_op jit(solution)/shard_map/ppermute | solution.py:30
  119.6 6.9 %collective-permute-start.18 = (bf16[3,160,640]{2,1,0:T(8,128)(2,1)}, bf16[3,160,640]{2,1,0:T(8,128)(2,1)}, u32[]{:S(2)}, u32[]{:S(2)}) collective-permute-start(bf16[3,160,640]{2,1,0:T(8,128)(2,1)} %get-tuple-element.142), channel_id=1, source_target_pairs={{0,4},{4,0},{1,5},{5,1},{2,6},{6,2},{3,7},{7,3},{8,12},{12,8},{9,1... | collective-permute-start | bytes 1843208 | tf_op jit(solution)/shard_map/ppermute | solution.py:30
  120.1 8.2 %collective-permute-start.17 = (bf16[3,160,640]{2,1,0:T(8,128)(2,1)}, bf16[3,160,640]{2,1,0:T(8,128)(2,1)S(1)}, u32[]{:S(2)}, u32[]{:S(2)}) collective-permute-start(bf16[3,160,640]{2,1,0:T(8,128)(2,1)} %get-tuple-element.140), channel_id=1, source_target_pairs={{0,4},{4,0},{1,5},{5,1},{2,6},{6,2},{3,7},{7,3},{8,12},{12,8},{9,1... | collective-permute-start | bytes 1843208 | tf_op jit(solution)/shard_map/ppermute | solution.py:30
  120.1 10.2 %collective-permute-start.16 = (bf16[3,160,640]{2,1,0:T(8,128)(2,1)}, bf16[3,160,640]{2,1,0:T(8,128)(2,1)S(1)}, u32[]{:S(2)}, u32[]{:S(2)}) collective-permute-start(bf16[3,160,640]{2,1,0:T(8,128)(2,1)} %get-tuple-element.138), channel_id=1, source_target_pairs={{0,4},{4,0},{1,5},{5,1},{2,6},{6,2},{3,7},{7,3},{8,12},{12,8},{9,1... | collective-permute-start | bytes 1843208 | tf_op jit(solution)/shard_map/ppermute | solution.py:30
  120.6 13.4 %all-to-all-start.1 = ((bf16[4,320,256]{2,1,0:T(8,128)(2,1)}), bf16[4,320,256]{2,1,0:T(8,128)(2,1)S(1)}, u32[]{:S(2)}, u32[]{:S(2)}) async-start(bf16[4,320,256]{2,1,0:T(8,128)(2,1)} %get-tuple-element.136), calls=%async_computation.1 | async-start | bytes 1310720 | tf_op jit(solution)/shard_map/all_to_all | solution.py:757
  124.3 11.1 %collective-permute-start.24 = (bf16[3,160,640]{2,1,0:T(8,128)(2,1)}, bf16[3,160,640]{2,1,0:T(8,128)(2,1)}, u32[]{:S(2)}, u32[]{:S(2)}) collective-permute-start(bf16[3,160,640]{2,1,0:T(8,128)(2,1)} %get-tuple-element.153), channel_id=1, source_target_pairs={{0,4},{4,0},{1,5},{5,1},{2,6},{6,2},{3,7},{7,3},{8,12},{12,8},{9,1... | collective-permute-start | bytes 1843208 | tf_op jit(solution)/shard_map/ppermute | solution.py:30
  124.4 11.6 %collective-permute-start.25 = (bf16[3,160,640]{2,1,0:T(8,128)(2,1)}, bf16[3,160,640]{2,1,0:T(8,128)(2,1)}, u32[]{:S(2)}, u32[]{:S(2)}) collective-permute-start(bf16[3,160,640]{2,1,0:T(8,128)(2,1)} %get-tuple-element.154), channel_id=1, source_target_pairs={{0,4},{4,0},{1,5},{5,1},{2,6},{6,2},{3,7},{7,3},{8,12},{12,8},{9,1... | collective-permute-start | bytes 1843208 | tf_op jit(solution)/shard_map/ppermute | solution.py:30
  126.6 10.9 %collective-permute-start.26 = (bf16[3,160,640]{2,1,0:T(8,128)(2,1)}, bf16[3,160,640]{2,1,0:T(8,128)(2,1)}, u32[]{:S(2)}, u32[]{:S(2)}) collective-permute-start(bf16[3,160,640]{2,1,0:T(8,128)(2,1)} %get-tuple-element.155), channel_id=1, source_target_pairs={{0,4},{4,0},{1,5},{5,1},{2,6},{6,2},{3,7},{7,3},{8,12},{12,8},{9,1... | collective-permute-start | bytes 1843208 | tf_op jit(solution)/shard_map/ppermute | solution.py:30
  128.3 29.2 %collective-permute-start.27 = (bf16[3,160,640]{2,1,0:T(8,128)(2,1)}, bf16[3,160,640]{2,1,0:T(8,128)(2,1)}, u32[]{:S(2)}, u32[]{:S(2)}) collective-permute-start(bf16[3,160,640]{2,1,0:T(8,128)(2,1)} %get-tuple-element.156), channel_id=1, source_target_pairs={{0,4},{4,0},{1,5},{5,1},{2,6},{6,2},{3,7},{7,3},{8,12},{12,8},{9,1... | collective-permute-start | bytes 1843208 | tf_op jit(solution)/shard_map/ppermute | solution.py:30
  130.3 7.7 %copy-start.39 = (f32[80]{0:T(128)S(1)}, f32[80]{0:T(128)}, u32[]{:S(2)}) copy-start(f32[80]{0:T(128)} %param.16) | copy-start | bytes 964
  134.0 23.5 %collective-permute-start.20 = (bf16[3,160,640]{2,1,0:T(8,128)(2,1)S(1)}, bf16[3,160,640]{2,1,0:T(8,128)(2,1)}, u32[]{:S(2)}, u32[]{:S(2)}) collective-permute-start(bf16[3,160,640]{2,1,0:T(8,128)(2,1)S(1)} %add_convert_fusion.11), channel_id=1, source_target_pairs={{0,2},{2,0},{1,3},{3,1},{4,6},{6,4},{5,7},{7,5},{8,10},{10,8},{9,1... | collective-permute-start | bytes 1843208 | tf_op jit(solution)/shard_map/ppermute | solution.py:30
  135.4 22.1 %collective-permute-start.21 = (bf16[3,160,640]{2,1,0:T(8,128)(2,1)S(1)}, bf16[3,160,640]{2,1,0:T(8,128)(2,1)}, u32[]{:S(2)}, u32[]{:S(2)}) collective-permute-start(bf16[3,160,640]{2,1,0:T(8,128)(2,1)S(1)} %add_convert_fusion.10), channel_id=1, source_target_pairs={{0,1},{1,0},{2,3},{3,2},{4,5},{5,4},{6,7},{7,6},{8,9},{9,8},{10,11... | collective-permute-start | bytes 1843208 | tf_op jit(solution)/shard_map/ppermute | solution.py:30
  136.0 26.7 %collective-permute-start.22 = (bf16[3,160,640]{2,1,0:T(8,128)(2,1)S(1)}, bf16[3,160,640]{2,1,0:T(8,128)(2,1)}, u32[]{:S(2)}, u32[]{:S(2)}) collective-permute-start(bf16[3,160,640]{2,1,0:T(8,128)(2,1)S(1)} %add_convert_fusion.9), channel_id=1, source_target_pairs={{0,2},{2,0},{1,3},{3,1},{4,6},{6,4},{5,7},{7,5},{8,10},{10,8},{9,1... | collective-permute-start | bytes 1843208 | tf_op jit(solution)/shard_map/ppermute | solution.py:30
  137.5 26.7 %collective-permute-start.23 = (bf16[3,160,640]{2,1,0:T(8,128)(2,1)S(1)}, bf16[3,160,640]{2,1,0:T(8,128)(2,1)}, u32[]{:S(2)}, u32[]{:S(2)}) collective-permute-start(bf16[3,160,640]{2,1,0:T(8,128)(2,1)S(1)} %add_convert_fusion.8), channel_id=1, source_target_pairs={{0,1},{1,0},{2,3},{3,2},{4,5},{5,4},{6,7},{7,6},{8,9},{9,8},{10,11... | collective-permute-start | bytes 1843208 | tf_op jit(solution)/shard_map/ppermute | solution.py:30
  151.3 12.9 %copy-start.31 = (f32[4,80,1]{2,1,0:T(8,128)S(1)}, f32[4,80,1]{2,1,0:T(8,128)}, u32[]{:S(2)}) copy-start(f32[4,80,1]{2,1,0:T(8,128)} %get-tuple-element.167) | copy-start | bytes 3844
  151.3 13.0 %copy-start.24 = (bf16[3,160,640]{2,1,0:T(8,128)(2,1)S(1)}, bf16[3,160,640]{2,1,0:T(8,128)(2,1)}, u32[]{:S(2)}) copy-start(bf16[3,160,640]{2,1,0:T(8,128)(2,1)} %get-tuple-element.159) | copy-start | bytes 1843204
  164.2 4.7 %collective-permute-start.30 = (bf16[2,3,160,640]{3,2,1,0:T(8,128)(2,1)}, bf16[2,3,160,640]{3,2,1,0:T(8,128)(2,1)S(1)}, u32[]{:S(2)}, u32[]{:S(2)}) collective-permute-start(bf16[2,3,160,640]{3,2,1,0:T(8,128)(2,1)} %get-tuple-element.163), channel_id=1, source_target_pairs={{0,4},{4,0},{1,5},{5,1},{2,6},{6,2},{3,7},{7,3},{8,12},{12,8},{9,1... | collective-permute-start | bytes 3686408 | tf_op jit(solution)/shard_map/ppermute | solution.py:30
  165.9 18.0 %collective-permute-start.29 = (bf16[3,160,640]{2,1,0:T(8,128)(2,1)S(1)}, bf16[3,160,640]{2,1,0:T(8,128)(2,1)}, u32[]{:S(2)}, u32[]{:S(2)}) collective-permute-start(bf16[3,160,640]{2,1,0:T(8,128)(2,1)S(1)} %add_convert_fusion.6), channel_id=1, source_target_pairs={{0,2},{2,0},{1,3},{3,1},{4,6},{6,4},{5,7},{7,5},{8,10},{10,8},{9,1... | collective-permute-start | bytes 1843208 | tf_op jit(solution)/shard_map/ppermute | solution.py:30
  167.9 16.2 %collective-permute-start.28 = (bf16[3,160,640]{2,1,0:T(8,128)(2,1)S(1)}, bf16[3,160,640]{2,1,0:T(8,128)(2,1)}, u32[]{:S(2)}, u32[]{:S(2)}) collective-permute-start(bf16[3,160,640]{2,1,0:T(8,128)(2,1)S(1)} %add_convert_fusion.7), channel_id=1, source_target_pairs={{0,1},{1,0},{2,3},{3,2},{4,5},{5,4},{6,7},{7,6},{8,9},{9,8},{10,11... | collective-permute-start | bytes 1843208 | tf_op jit(solution)/shard_map/ppermute | solution.py:30
  170.1 15.9 %collective-permute-start.31 = (bf16[3,160,640]{2,1,0:T(8,128)(2,1)}, bf16[3,160,640]{2,1,0:T(8,128)(2,1)S(1)}, u32[]{:S(2)}, u32[]{:S(2)}) collective-permute-start(bf16[3,160,640]{2,1,0:T(8,128)(2,1)} %fusion.2), channel_id=1, source_target_pairs={{0,8},{8,0},{16,24},{24,16},{1,9},{9,1},{17,25},{25,17},{2,10},{10... | collective-permute-start | bytes 1843208 | tf_op jit(solution)/shard_map/ppermute | solution.py:762
  172.3 8.6 %copy-start.22 = (bf16[3,160,640]{2,1,0:T(8,128)(2,1)S(1)}, bf16[3,160,640]{2,1,0:T(8,128)(2,1)}, u32[]{:S(2)}) copy-start(bf16[3,160,640]{2,1,0:T(8,128)(2,1)} %get-tuple-element.173) | copy-start | bytes 1843204
  188.9 65.7 %all-to-all-start.2 = ((bf16[4,528,640]{2,1,0:T(8,128)(2,1)}), bf16[4,528,640]{2,1,0:T(8,128)(2,1)S(1)}, u32[]{:S(2)}, u32[]{:S(2)}) async-start(bf16[4,528,640]{2,1,0:T(8,128)(2,1)} %project_back.1), calls=%async_computation.2 | async-start | bytes 5406720 | tf_op jit(solution)/shard_map/all_to_all | solution.py:757
  192.9 16.3 %collective-permute-start.33 = (bf16[3,160,640]{2,1,0:T(8,128)(2,1)}, bf16[3,160,640]{2,1,0:T(8,128)(2,1)S(1)}, u32[]{:S(2)}, u32[]{:S(2)}) collective-permute-start(bf16[3,160,640]{2,1,0:T(8,128)(2,1)} %get-tuple-element.209), channel_id=1, source_target_pairs={{0,8},{8,0},{16,24},{24,16},{1,9},{9,1},{17,25},{25,17},{2,10},{10... | collective-permute-start | bytes 1843208 | tf_op jit(solution)/shard_map/ppermute | solution.py:762
  194.5 28.7 %collective-permute-start.32 = (bf16[3,160,640]{2,1,0:T(8,128)(2,1)S(1)}, bf16[3,160,640]{2,1,0:T(8,128)(2,1)S(1)}, u32[]{:S(2)}, u32[]{:S(2)}) collective-permute-start(bf16[3,160,640]{2,1,0:T(8,128)(2,1)S(1)} %fusion.1), channel_id=1, source_target_pairs={{0,24},{8,16},{16,8},{24,0},{1,25},{9,17},{17,9},{25,1},{2,26},{10... | collective-permute-start | bytes 1843208 | tf_op jit(solution)/shard_map/ppermute | solution.py:762
  209.1 14.1 %copy-start.25 = (bf16[3,160,640]{2,1,0:T(8,128)(2,1)}, bf16[3,160,640]{2,1,0:T(8,128)(2,1)S(1)}, u32[]{:S(2)}) copy-start(bf16[3,160,640]{2,1,0:T(8,128)(2,1)S(1)} %collective-permute-done.33) | copy-start | bytes 1843204
  224.2 27.4 %collective-permute-start.35 = (bf16[3,160,640]{2,1,0:T(8,128)(2,1)}, bf16[3,160,640]{2,1,0:T(8,128)(2,1)}, u32[]{:S(2)}, u32[]{:S(2)}) collective-permute-start(bf16[3,160,640]{2,1,0:T(8,128)(2,1)} %add_convert_fusion.2), channel_id=1, source_target_pairs={{0,8},{8,0},{16,24},{24,16},{1,9},{9,1},{17,25},{25,17},{2,10},{10... | collective-permute-start | bytes 1843208 | tf_op jit(solution)/shard_map/ppermute | solution.py:762
  225.6 39.7 %collective-permute-start.34 = (bf16[3,160,640]{2,1,0:T(8,128)(2,1)S(1)}, bf16[3,160,640]{2,1,0:T(8,128)(2,1)}, u32[]{:S(2)}, u32[]{:S(2)}) collective-permute-start(bf16[3,160,640]{2,1,0:T(8,128)(2,1)S(1)} %add_convert_fusion.3), channel_id=1, source_target_pairs={{0,24},{8,16},{16,8},{24,0},{1,25},{9,17},{17,9},{25,1},{2,26},{10... | collective-permute-start | bytes 1843208 | tf_op jit(solution)/shard_map/ppermute | solution.py:762
  228.8 36.5 %collective-permute-start.37 = (bf16[2,256,640]{2,1,0:T(8,128)(2,1)}, bf16[2,256,640]{2,1,0:T(8,128)(2,1)}, u32[]{:S(2)}, u32[]{:S(2)}) collective-permute-start(bf16[2,256,640]{2,1,0:T(8,128)(2,1)} %get-tuple-element.188), channel_id=1, source_target_pairs={{0,1},{1,0},{2,3},{3,2},{4,5},{5,4},{6,7},{7,6},{8,9},{9,8},{10,11... | collective-permute-start | bytes 1966088 | tf_op jit(solution)/shard_map/ppermute | solution.py:30
  254.0 11.4 %collective-permute-start.36 = (bf16[3,160,640]{2,1,0:T(8,128)(2,1)}, bf16[3,160,640]{2,1,0:T(8,128)(2,1)}, u32[]{:S(2)}, u32[]{:S(2)}) collective-permute-start(bf16[3,160,640]{2,1,0:T(8,128)(2,1)} %get-tuple-element.216), channel_id=1, source_target_pairs={{0,1},{1,0},{2,3},{3,2},{4,5},{5,4},{6,7},{7,6},{8,9},{9,8},{10,11... | collective-permute-start | bytes 1843208 | tf_op jit(solution)/shard_map/ppermute | solution.py:30
  254.7 1.5 collective-permute-start.38
  256.2 4.1 %collective-permute-start.39 = (f32[9,640]{1,0:T(8,128)S(1)}, f32[9,640]{1,0:T(8,128)S(1)}, u32[]{:S(2)}, u32[]{:S(2)}) collective-permute-start(f32[9,640]{1,0:T(8,128)S(1)} %add.150), channel_id=1, source_target_pairs={{0,8},{8,0},{16,24},{24,16},{1,9},{9,1},{17,25},{25,17},{2,10},{10... | collective-permute-start | bytes 69128 | tf_op jit(solution)/shard_map/ppermute | solution.py:762
  260.3 5.0 %collective-permute-start.40 = (f32[9,640]{1,0:T(8,128)S(1)}, f32[9,640]{1,0:T(8,128)S(1)}, u32[]{:S(2)}, u32[]{:S(2)}) collective-permute-start(f32[9,640]{1,0:T(8,128)S(1)} %add.151), channel_id=1, source_target_pairs={{0,16},{8,24},{16,0},{24,8},{1,17},{9,25},{17,1},{25,9},{2,18},{10... | collective-permute-start | bytes 69128 | tf_op jit(solution)/shard_map/ppermute | solution.py:762
  260.3 7.1 %copy-start.30 = (bf16[256,640]{1,0:T(8,128)(2,1)S(1)}, bf16[256,640]{1,0:T(8,128)(2,1)}, u32[]{:S(2)}) copy-start(bf16[256,640]{1,0:T(8,128)(2,1)} %get-tuple-element.126) | copy-start | bytes 983044
  265.4 7.0 %collective-permute-start.41 = (bf16[3,160,640]{2,1,0:T(8,128)(2,1)}, bf16[3,160,640]{2,1,0:T(8,128)(2,1)S(1)}, u32[]{:S(2)}, u32[]{:S(2)}) collective-permute-start(bf16[3,160,640]{2,1,0:T(8,128)(2,1)} %get-tuple-element.195.mine), channel_id=1, source_target_pairs={{0,4},{4,0},{1,5},{5,1},{2,6},{6,2},{3,7},{7,3},{8,12},{12,8},{9,1... | collective-permute-start | bytes 1843208 | tf_op jit(solution)/shard_map/ppermute | solution.py:30
  265.4 6.9 %collective-permute-start.42 = (bf16[3,160,640]{2,1,0:T(8,128)(2,1)}, bf16[3,160,640]{2,1,0:T(8,128)(2,1)S(1)}, u32[]{:S(2)}, u32[]{:S(2)}) collective-permute-start(bf16[3,160,640]{2,1,0:T(8,128)(2,1)} %collective-permute-done.36.theirs), channel_id=1, source_target_pairs={{0,4},{4,0},{1,5},{5,1},{2,6},{6,2},{3,7},{7,3},{8,12},{12,8},{9,1... | collective-permute-start | bytes 1843208 | tf_op jit(solution)/shard_map/ppermute | solution.py:30
  267.2 15.9 %collective-permute-start.43 = (bf16[3,160,640]{2,1,0:T(8,128)(2,1)S(1)}, bf16[3,160,640]{2,1,0:T(8,128)(2,1)S(1)}, u32[]{:S(2)}, u32[]{:S(2)}) collective-permute-start(bf16[3,160,640]{2,1,0:T(8,128)(2,1)S(1)} %add_convert_fusion.1), channel_id=1, source_target_pairs={{0,8},{8,0},{16,24},{24,16},{1,9},{9,1},{17,25},{25,17},{2,10},{10... | collective-permute-start | bytes 1843208 | tf_op jit(solution)/shard_map/ppermute | solution.py:762
  283.2 2.1 collective-permute-start.44
  283.3 2.9 %collective-permute-start.45 = (bf16[3,160,640]{2,1,0:T(8,128)(2,1)S(1)}, bf16[3,160,640]{2,1,0:T(8,128)(2,1)S(1)}, u32[]{:S(2)}, u32[]{:S(2)}) collective-permute-start(bf16[3,160,640]{2,1,0:T(8,128)(2,1)S(1)} %get-tuple-element.214.b), channel_id=1, source_target_pairs={{0,4},{4,0},{1,5},{5,1},{2,6},{6,2},{3,7},{7,3},{8,12},{12,8},{9,1... | collective-permute-start | bytes 1843208 | tf_op jit(solution)/shard_map/ppermute | solution.py:30
  (25 other events, 57.5 us)
where the time goes:
time: 290 us; the launch traced here: 289 us
  waiting for transfers between devices  110 us (38%)
  Pallas kernels  74.5 us (26%)
  starting transfers between devices  44.5 us (15%)
  other arithmetic  34.8 us (12%)
  local copies, waits for them, and re-layouts  23.9 us (8%)
    ppermute x8, waiting for transfers between devices, z_swap(): return lax.ppermute(x, 'z', [(i, i ^ step) for i in range(n)])  60.7 us
    pallas_call x7, Pallas kernels, call(): pl.pallas_call(kernel, in_specs=specs, **more, out_shape=outs, scratch_sh...  51.6 us
    ppermute x38, waiting for transfers between devices, swap(): return lax.ppermute(x, axis, [(0, 1), (1, 0)])  31.9 us
    ppermute x38, starting transfers between devices, swap(): return lax.ppermute(x, axis, [(0, 1), (1, 0)])  24 us
    all_to_all x3, waiting for transfers between devices, all_four(): return lax.all_to_all(x, ('row', 'col'), 0, 0, tiled=True)  17.9 us
    pallas_call x1, Pallas kernels, attention_backward(): pl.pallas_call(functools.partial(backward_kernel, block), grid=(heads,),...  12.5 us
    convert_element_type x11, other arithmetic, add(): return total.astype(BF)  12.2 us
    all_to_all x3, starting transfers between devices, all_four(): return lax.all_to_all(x, ('row', 'col'), 0, 0, tiled=True)  11.3 us
  transfers between devices with their start and end apart: 49, of which 19 were waited for; matrix products, arithmetic and copies ran while one was open for 17% of the time, Pallas kernels for 18%

commit v1 on v0

--- a/solution.py
+++ b/solution.py
@@ -933,7 +933,7 @@
     total = total + swap(total, "core")
     total = total + z_swap(total, 1)
     total = total + z_swap(total, 2)
-    met_c, mine_c, w_own, w_theirs, post, total = together((met_c, mine_c, w_own, w_theirs, post, total))
+    met_c, mine_c, total = together((met_c, mine_c, total))
     mine_c = add(mine_c, met_c)
     other_c = z_swap(mine_c, 1)
     w_args = (at, w_own, w_theirs, swap(w_own, "core"), swap(w_theirs, "core"))

time: 290 us -> 291 us (level)
    ppermute x8, waiting for transfers between devices: 60.7 us -> 55.6 us  [z_swap(): return lax.ppermute(x, 'z', [(i, i ^ step) for i in range(n)])]
    ppermute x38, waiting for transfers between devices: 31.9 us -> 36.2 us  [swap(): return lax.ppermute(x, axis, [(0, 1), (1, 0)])]
    unnamed x81 -> x79, local copies, waits for them, and re-layouts: 10 us -> 8.07 us
where the time goes in v1:
time: 291 us; the launch traced here: 290 us
  waiting for transfers between devices  110 us (38%)
  Pallas kernels  74.5 us (26%)
  starting transfers between devices  44.4 us (15%)
  other arithmetic  36.8 us (13%)
  local copies, waits for them, and re-layouts  22.6 us (8%)
    ppermute x8, waiting for transfers between devices, z_swap(): return lax.ppermute(x, 'z', [(i, i ^ step) for i in range(n)])  55.6 us
    pallas_call x7, Pallas kernels, call(): pl.pallas_call(kernel, in_specs=specs, **more, out_shape=outs, scratch_sh...  51.6 us
    ppermute x38, waiting for transfers between devices, swap(): return lax.ppermute(x, axis, [(0, 1), (1, 0)])  36.2 us
    ppermute x38, starting transfers between devices, swap(): return lax.ppermute(x, axis, [(0, 1), (1, 0)])  23.9 us
    all_to_all x3, waiting for transfers between devices, all_four(): return lax.all_to_all(x, ('row', 'col'), 0, 0, tiled=True)  18.5 us
    convert_element_type x11, other arithmetic, add(): return total.astype(BF)  14.5 us
    pallas_call x1, Pallas kernels, attention_backward(): pl.pallas_call(functools.partial(backward_kernel, block), grid=(heads,),...  12.5 us
    all_to_all x3, starting transfers between devices, all_four(): return lax.all_to_all(x, ('row', 'col'), 0, 0, tiled=True)  11.3 us
  transfers between devices with their start and end apart: 49, of which 19 were waited for; matrix products, arithmetic and copies ran while one was open for 17% of the time, Pallas kernels for 18%

profile of v1, /device:TPU:0, one launch (start us, length us, event | category | flops | bytes accessed | tf_op | source)
XLA Modules:
  0.0 289.8 jit_solution(17053325171968127512)
XLA Ops:
  0.6 3.0 %collective-permute-start = (bf16[512,640]{1,0:T(8,128)(2,1)}, bf16[512,640]{1,0:T(8,128)(2,1)S(1)}, u32[]{:S(2)}, u32[]{:S(2)}) collective-permute-start(bf16[512,640]{1,0:T(8,128)(2,1)} %x00.3), channel_id=1, source_target_pairs={{0,1},{1,0},{2,3},{3,2},{4,5},{5,4},{6,7},{7,6},{8,9},{9,8},{10,11... | collective-permute-start | bytes 1966088 | tf_op jit(solution)/shard_map/ppermute | solution.py:30
  3.7 1.5 collective-permute-start.1
  7.9 3.9 %copy.27 = bf16[640,3,640]{0,2,1:T(8,128)(2,1)S(1)} copy(bf16[640,3,640]{2,0,1:T(8,128)(2,1)} %param.15) | data formatting | bytes 4915200 | tf_op args[2]
  11.9 1.1 dynamic-slice_bitcast_fusion.4
  13.3 1.1 dynamic-slice_bitcast_fusion.w_mine
  14.5 1.2 pad_maximum_fusion
  16.5 3.8 %collective-permute-done.3 = f32[640]{0:T(1024)S(1)} collective-permute-done((f32[640]{0:T(1024)S(1)}, f32[640]{0:T(1024)S(1)}, u32[]{:S(2)}, u32[]{:S(2)}) %collective-permute-start.3) | collective-permute-done | bytes 2592 | tf_op jit(solution)/shard_map/ppermute | solution.py:30
  20.3 1.6 collective-permute-start.4
  22.3 13.7 %collective-permute-done.5.w_a = bf16[3,160,640]{2,1,0:T(8,128)(2,1)S(1)} collective-permute-done((bf16[3,160,640]{2,1,0:T(8,128)(2,1)S(1)}, bf16[3,160,640]{2,1,0:T(8,128)(2,1)S(1)}, u32[]{:S(2)}, u32[]{:S(2)}) %collective-permute-start.5) | collective-permute-done | bytes 614432 | tf_op jit(solution)/shard_map/ppermute | solution.py:30
  36.0 1.2 collective-permute-start.6
  38.7 1.0 copy.30.kpos_ref
  39.7 1.0 copy.29.scol_ref
  42.7 8.1 %project.1 = (bf16[3,320,1024]{2,1,0:T(8,128)(2,1)}, f32[320,1024]{1,0:T(8,128)}, bf16[1024,1280]{1,0:T(8,128)(2,1)}, f32[512,1]{1,0:T(8,128)}, bf16[960,1280]{1,0:T(8,128)(2,1)}) custom-call(s32[4]{0:T(128)} %pad_add_fusion.at, bf16[512,640]{1,0:T(8,128)(2,1)} %x00.3, bf16[512,640]{1,0:T(8,128)(2,1)} %copy-done.2, ...), custom_call_target="tpu_custom_call" | custom-call | flops 1 | bytes 1 | tf_op jit(solution)/shard_map/project/pallas_call | solution.py:508
  50.8 10.4 %attention_forward.1 = (bf16[4,80,1024]{2,1,0:T(8,128)(2,1)}, f32[4,1,1024]{2,1,0:T(1,128)}, bf16[4,4,80,256]{3,2,1,0:T(8,128)(2,1)}) custom-call(s32[4]{0:T(128)} %pad_add_fusion.at, bf16[3,4,80,1024]{3,2,1,0:T(8,128)(2,1)} %bitcast.52, s32[1,1024]{1,0:T(1,128)} %bitcast.59, s32[1024,1]{1,0:T(8,128)} %copy.29.scol_ref, s32[1024,1]{1,0:T(8,128)} %copy.30.kpos_ref), custom_call_target="tpu_custom_call" | custom-call | flops 1 | bytes 1 | tf_op jit(solution)/shard_map/attention_forward/pallas_call | solution.py:260
  61.1 1.6 collective-permute-done.6.hx
  65.4 3.7 %all-to-all-start = ((bf16[4,320,256]{2,1,0:T(8,128)(2,1)}), bf16[4,320,256]{2,1,0:T(8,128)(2,1)S(1)}, u32[]{:S(2)}, u32[]{:S(2)}) async-start(bf16[4,320,256]{2,1,0:T(8,128)(2,1)} %bitcast.16), calls=%async_computation | async-start | bytes 1310720 | tf_op jit(solution)/shard_map/all_to_all | solution.py:757
  69.1 1.1 slice.48
  70.2 1.9 collective-permute-start.9
  72.8 16.9 %all-to-all-done.a = bf16[4,320,256]{2,1,0:T(8,128)(2,1)S(1)} async-done(((bf16[4,320,256]{2,1,0:T(8,128)(2,1)}), bf16[4,320,256]{2,1,0:T(8,128)(2,1)S(1)}, u32[]{:S(2)}, u32[]{:S(2)}) %all-to-all-start) | async-done | bytes 655392 | tf_op jit(solution)/shard_map/all_to_all | solution.py:757
  89.7 3.3 %collective-permute-done.11.g_col = bf16[256,640]{1,0:T(8,128)(2,1)} collective-permute-done((bf16[256,640]{1,0:T(8,128)(2,1)}, bf16[256,640]{1,0:T(8,128)(2,1)}, u32[]{:S(2)}, u32[]{:S(2)}) %collective-permute-start.11) | collective-permute-done | bytes 327712 | tf_op jit(solution)/shard_map/ppermute | solution.py:30
  98.5 13.4 %feed_forward.1 = (bf16[256,640]{1,0:T(8,128)(2,1)}, f32[256,640]{1,0:T(8,128)}, bf16[2,256,640]{2,1,0:T(8,128)(2,1)}, bf16[4,320,256]{2,1,0:T(8,128)(2,1)}, f32...) custom-call(s32[4]{0:T(128)} %pad_add_fusion.at, ...), custom_call_target="tpu_custom_call" | custom-call | flops 1 | bytes 1 | tf_op jit(solution)/shard_map/feed_forward/pallas_call | solution.py:508
  112.0 6.8 %feed_weights.1 = (bf16[3,160,640]{2,1,0:T(8,128)(2,1)}, bf16[3,160,640]{2,1,0:T(8,128)(2,1)}, bf16[3,160,640]{2,1,0:T(8,128)(2,1)}, bf16[3,160,640]{2,1,0:T(8,1...) custom-call(s32[4]{0:T(128)} %pad_add_fusion.at, ...), custom_call_target="tpu_custom_call" | custom-call | flops 1 | bytes 1 | tf_op jit(solution)/shard_map/feed_weights/pallas_call | solution.py:508
  119.9 3.7 %all-to-all-start.1 = ((bf16[4,320,256]{2,1,0:T(8,128)(2,1)}), bf16[4,320,256]{2,1,0:T(8,128)(2,1)S(1)}, u32[]{:S(2)}, u32[]{:S(2)}) async-start(bf16[4,320,256]{2,1,0:T(8,128)(2,1)} %get-tuple-element.133), calls=%async_computation.1 | async-start | bytes 1310720 | tf_op jit(solution)/shard_map/all_to_all | solution.py:757
  124.6 1.2 add_convert_fusion.8
  126.3 1.2 add_convert_fusion.9
  128.4 1.2 add_convert_fusion.10
  130.5 1.2 add_convert_fusion.11
  131.7 1.6 all-to-all-done.1
  133.3 1.4 collective-permute-start.20
  135.3 1.5 collective-permute-start.22
  138.1 12.5 %attention_backward.1 = (bf16[3,4,80,1024]{3,2,1,0:T(8,128)(2,1)}, f32[4,80,1]{2,1,0:T(8,128)}) custom-call(s32[4]{0:T(128)} %pad_add_fusion.at, bf16[3,4,80,1024]{3,2,1,0:T(8,128)(2,1)} %bitcast.53, f32[4,80,1024]{2,1,0:T(8,128)} %bitcast.58, f32[80,1]{1,0:T(8,128)} %copy.31.factor_ref, bf16[4,80,1024]{2,1,0:T(8,128)(2,1)} %get-tuple-element.132.out_ref, ...), custom_call_target="tpu_custom_call" | custom-call | flops 1 | bytes 1 | tf_op jit(solution)/shard_map/attention_backward/pallas_call | solution.py:297
  150.6 6.2 %weight_back.1 = (bf16[2,3,160,640]{3,2,1,0:T(8,128)(2,1)}, bf16[2,3,160,640]{3,2,1,0:T(8,128)(2,1)}) custom-call(s32[4]{0:T(128)} %pad_add_fusion.at, bf16[3,320,1024]{2,1,0:T(8,128)(2,1)} %bitcast.50, bf16[1024,1280]{1,0:T(8,128)(2,1)} %get-tuple-element.144.normed), custom_call_target="tpu_custom_call" | custom-call | flops 1 | bytes 1 | tf_op jit(solution)/shard_map/weight_back/pallas_call | solution.py:508
  156.8 5.2 %collective-permute-done.22 = bf16[3,160,640]{2,1,0:T(8,128)(2,1)} collective-permute-done((bf16[3,160,640]{2,1,0:T(8,128)(2,1)S(1)}, bf16[3,160,640]{2,1,0:T(8,128)(2,1)}, u32[]{:S(2)}, u32[]{:S(2)}) %collective-permute-start.22) | collective-permute-done | bytes 614432 | tf_op jit(solution)/shard_map/ppermute | solution.py:30
  162.0 1.5 collective-permute-done.23
  163.6 1.5 add_convert_fusion.6
  165.6 1.6 add_convert_fusion.7
  169.4 1.6 collective-permute-start.31
  171.6 8.6 %project_back.1 = bf16[4,528,640]{2,1,0:T(8,128)(2,1)} custom-call(s32[4]{0:T(128)} %pad_add_fusion.at, bf16[960,1024]{1,0:T(8,128)(2,1)} %bitcast.51, bf16[960,1280]{1,0:T(8,128)(2,1)} %get-tuple-element.162.w_full, bf16[512,640]{1,0:T(8,128)(2,1)} %x00.3, bf16[512,640]{1,0:T(8,128)(2,1)} %copy-done.2, bf16[512,640]{1,0:T(8,128)(2,1)} %collective-permute-done.1.x10, ...), custom_call_target="tpu_custom_call" | custom-call | flops 1 | bytes 1 | tf_op jit(solution)/shard_map/project_back/pallas_call | solution.py:508
  180.1 1.5 convert_add_fusion.1
  181.7 1.5 convert_add_fusion.2
  183.3 2.0 collective-permute-done.31
  185.3 2.7 broadcast_select_fusion.4
  188.0 1.6 collective-permute-start.33
  189.8 2.5 collective-permute-start.32
  192.4 3.9 %all-to-all-start.2 = ((bf16[4,528,640]{2,1,0:T(8,128)(2,1)}), bf16[4,528,640]{2,1,0:T(8,128)(2,1)S(1)}, u32[]{:S(2)}, u32[]{:S(2)}) async-start(bf16[4,528,640]{2,1,0:T(8,128)(2,1)} %project_back.1), calls=%async_computation.2 | async-start | bytes 5406720 | tf_op jit(solution)/shard_map/all_to_all | solution.py:757
  196.3 7.9 %collective-permute-done.33 = bf16[3,160,640]{2,1,0:T(8,128)(2,1)} collective-permute-done((bf16[3,160,640]{2,1,0:T(8,128)(2,1)}, bf16[3,160,640]{2,1,0:T(8,128)(2,1)}, u32[]{:S(2)}, u32[]{:S(2)}) %collective-permute-start.33) | collective-permute-done | bytes 614432 | tf_op jit(solution)/shard_map/ppermute | solution.py:762
  204.2 14.3 %collective-permute-done.32 = bf16[3,160,640]{2,1,0:T(8,128)(2,1)} collective-permute-done((bf16[3,160,640]{2,1,0:T(8,128)(2,1)S(1)}, bf16[3,160,640]{2,1,0:T(8,128)(2,1)}, u32[]{:S(2)}, u32[]{:S(2)}) %collective-permute-start.32) | collective-permute-done | bytes 614432 | tf_op jit(solution)/shard_map/ppermute | solution.py:762
  218.5 1.4 add_convert_fusion.2
  220.6 1.1 collective-permute-start.34
  221.7 2.3 add_convert_fusion.3
  224.0 2.6 collective-permute-start.35
  226.6 20.4 %collective-permute-done.39 = bf16[3,160,640]{2,1,0:T(8,128)(2,1)} collective-permute-done((bf16[3,160,640]{2,1,0:T(8,128)(2,1)S(1)}, bf16[3,160,640]{2,1,0:T(8,128)(2,1)}, u32[]{:S(2)}, u32[]{:S(2)}) %collective-permute-start.39) | collective-permute-done | bytes 614432 | tf_op jit(solution)/shard_map/ppermute | solution.py:762
  247.1 2.2 broadcast_select_fusion.2
  249.3 1.1 collective-permute-start.40
  250.4 1.9 convert_select_fusion.1
  252.9 1.1 broadcast_select_fusion.6
  255.0 4.7 %collective-permute-done.40.theirs = bf16[3,160,640]{2,1,0:T(8,128)(2,1)} collective-permute-done((bf16[3,160,640]{2,1,0:T(8,128)(2,1)}, bf16[3,160,640]{2,1,0:T(8,128)(2,1)}, u32[]{:S(2)}, u32[]{:S(2)}) %collective-permute-start.40) | collective-permute-done | bytes 614432 | tf_op jit(solution)/shard_map/ppermute | solution.py:30
  260.7 4.0 %collective-permute-done.38 = f32[9,640]{1,0:T(8,128)S(1)} collective-permute-done((f32[9,640]{1,0:T(8,128)S(1)}, f32[9,640]{1,0:T(8,128)S(1)}, u32[]{:S(2)}, u32[]{:S(2)}) %collective-permute-start.38) | collective-permute-done | bytes 23072 | tf_op jit(solution)/shard_map/ppermute | solution.py:762
  264.7 2.2 add_convert_fusion.1
  268.5 1.4 fusion
  269.9 5.5 %finish_qkv.1 = f32[3,640,640]{2,1,0:T(8,128)} custom-call(s32[4]{0:T(128)} %pad_add_fusion.at, bf16[3,160,640]{2,1,0:T(8,128)(2,1)} %get-tuple-element.211.mine, bf16[3,160,640]{2,1,0:T(8,128)(2,1)} %collective-permute-done.40.theirs, bf16[3,160,640]{2,1,0:T(8,128)(2,1)} %collective-permute-done.41.mine2, bf16[3,160,640]{2,1,0:T(8,128)(2,1)} %collective-permute-done.42.theirs2), custom_call_target="tpu_custom_call" | custom-call | flops 1 | bytes 1 | tf_op jit(solution)/shard_map/finish_qkv/pallas_call | solution.py:508
  275.4 7.1 %collective-permute-done.43 = bf16[3,160,640]{2,1,0:T(8,128)(2,1)} collective-permute-done((bf16[3,160,640]{2,1,0:T(8,128)(2,1)}, bf16[3,160,640]{2,1,0:T(8,128)(2,1)}, u32[]{:S(2)}, u32[]{:S(2)}) %collective-permute-start.43) | collective-permute-done | bytes 614432 | tf_op jit(solution)/shard_map/ppermute | solution.py:762
  282.4 1.4 broadcast_select_fusion
  286.8 3.0 %finish_feed.1 = (f32[640,640]{1,0:T(8,128)}, f32[640,640]{1,0:T(8,128)}, f32[640,640]{1,0:T(8,128)}) custom-call(s32[4]{0:T(128)S(1)} %copy-done, bf16[3,160,640]{2,1,0:T(8,128)(2,1)S(1)} %get-tuple-element.209.a, bf16[3,160,640]{2,1,0:T(8,128)(2,1)S(1)} %get-tuple-element.208.b, bf16[3,160,640]{2,1,0:T(8,128)(2,1)S(1)} %collective-permute-done.44.a2, ...), custom_call_target="tpu_custom_call" | custom-call | flops 1 | bytes 1 | tf_op jit(solution)/shard_map/finish_feed/pallas_call | solution.py:508
  (186 shorter events, 34.5 us)
Async XLA Ops:
  0.6 19.6 %collective-permute-start = (bf16[512,640]{1,0:T(8,128)(2,1)}, bf16[512,640]{1,0:T(8,128)(2,1)S(1)}, u32[]{:S(2)}, u32[]{:S(2)}) collective-permute-start(bf16[512,640]{1,0:T(8,128)(2,1)} %x00.3), channel_id=1, source_target_pairs={{0,1},{1,0},{2,3},{3,2},{4,5},{5,4},{6,7},{7,6},{8,9},{9,8},{10,11... | collective-permute-start | bytes 1966088 | tf_op jit(solution)/shard_map/ppermute | solution.py:30
  3.7 16.6 %collective-permute-start.1 = (bf16[512,640]{1,0:T(8,128)(2,1)}, bf16[512,640]{1,0:T(8,128)(2,1)}, u32[]{:S(2)}, u32[]{:S(2)}) collective-permute-start(bf16[512,640]{1,0:T(8,128)(2,1)} %x00.3), channel_id=1, source_target_pairs={{0,2},{2,0},{1,3},{3,1},{4,6},{6,4},{5,7},{7,5},{8,10},{10,8},{9,1... | collective-permute-start | bytes 1966088 | tf_op jit(solution)/shard_map/ppermute | solution.py:30
  6.6 13.7 %collective-permute-start.2 = (f32[1920]{0:T(1024)S(1)}, f32[1920]{0:T(1024)S(1)}, u32[]{:S(2)}, u32[]{:S(2)}) collective-permute-start(f32[1920]{0:T(1024)S(1)} %pad_maximum_fusion.2), channel_id=1, source_target_pairs={{0,1},{1,0},{2,3},{3,2},{4,5},{5,4},{6,7},{7,6},{8,9},{9,8},{10,11... | collective-permute-start | bytes 23048 | tf_op jit(solution)/shard_map/ppermute | solution.py:30
  7.8 12.5 %collective-permute-start.3 = (f32[640]{0:T(1024)S(1)}, f32[640]{0:T(1024)S(1)}, u32[]{:S(2)}, u32[]{:S(2)}) collective-permute-start(f32[640]{0:T(1024)S(1)} %convert_element_type.167), channel_id=1, source_target_pairs={{0,2},{2,0},{1,3},{3,1},{4,6},{6,4},{5,7},{7,5},{8,10},{10,8},{9,1... | collective-permute-start | bytes 7688 | tf_op jit(solution)/shard_map/ppermute | solution.py:30
  14.5 23.3 %copy-start.37 = (f32[80]{0:T(128)S(1)}, f32[80]{0:T(128)}, u32[]{:S(2)}) copy-start(f32[80]{0:T(128)} %param.16) | copy-start | bytes 964
  14.5 24.2 %copy-start.35 = (s32[1024]{0:T(1024)S(1)}, s32[1024]{0:T(1024)}, u32[]{:S(2)}) copy-start(s32[1024]{0:T(1024)} %param.24) | copy-start | bytes 12292
  15.7 24.0 %copy-start.31 = (s32[1024]{0:T(1024)S(1)}, s32[1024]{0:T(1024)}, u32[]{:S(2)}) copy-start(s32[1024]{0:T(1024)} %param.23) | copy-start | bytes 12292
  15.7 26.4 %copy-start.32 = (f32[640]{0:T(1024)S(1)}, f32[640]{0:T(1024)}, u32[]{:S(2)}) copy-start(f32[640]{0:T(1024)} %param.14) | copy-start | bytes 7684
  20.2 30.6 %copy-start.36 = (f32[640]{0:T(1024)}, f32[640]{0:T(1024)S(1)}, u32[]{:S(2)}) copy-start(f32[640]{0:T(1024)S(1)} %collective-permute-done.3) | copy-start | bytes 7684
  20.2 22.4 %copy-start.2 = (bf16[512,640]{1,0:T(8,128)(2,1)}, bf16[512,640]{1,0:T(8,128)(2,1)S(1)}, u32[]{:S(2)}) copy-start(bf16[512,640]{1,0:T(8,128)(2,1)S(1)} %collective-permute-done.x01.x_col) | copy-start | bytes 1966084
  20.3 15.7 %collective-permute-start.4 = (bf16[512,640]{1,0:T(8,128)(2,1)S(1)}, bf16[512,640]{1,0:T(8,128)(2,1)S(1)}, u32[]{:S(2)}, u32[]{:S(2)}) collective-permute-start(bf16[512,640]{1,0:T(8,128)(2,1)S(1)} %collective-permute-done.x01.x_col), channel_id=1, source_target_pairs={{0,2},{2,0},{1,3},{3,1},{4,6},{6,4},{5,7},{7,5},{8,10},{10,8},{9,1... | collective-permute-start | bytes 1966088 | tf_op jit(solution)/shard_map/ppermute | solution.py:30
  21.8 14.2 %collective-permute-start.5 = (bf16[3,160,640]{2,1,0:T(8,128)(2,1)S(1)}, bf16[3,160,640]{2,1,0:T(8,128)(2,1)S(1)}, u32[]{:S(2)}, u32[]{:S(2)}) collective-permute-start(bf16[3,160,640]{2,1,0:T(8,128)(2,1)S(1)} %dynamic-slice_bitcast_fusion.1), channel_id=1, source_target_pairs={{0,1},{1,0},{2,3},{3,2},{4,5},{5,4},{6,7},{7,6},{8,9},{9,8},{10,11... | collective-permute-start | bytes 1843208 | tf_op jit(solution)/shard_map/ppermute | solution.py:30
  36.0 26.8 %collective-permute-start.6 = (bf16[3,320,640]{2,1,0:T(8,128)(2,1)}, bf16[3,320,640]{2,1,0:T(8,128)(2,1)}, u32[]{:S(2)}, u32[]{:S(2)}) collective-permute-start(bf16[3,320,640]{2,1,0:T(8,128)(2,1)} %pad_maximum_fusion), channel_id=1, source_target_pairs={{0,2},{2,0},{1,3},{3,1},{4,6},{6,4},{5,7},{7,5},{8,10},{10,8},{9,1... | collective-permute-start | bytes 3686408 | tf_op jit(solution)/shard_map/ppermute | solution.py:30
  37.1 26.6 %collective-permute-start.7 = (bf16[3,320,640]{2,1,0:T(8,128)(2,1)}, bf16[3,320,640]{2,1,0:T(8,128)(2,1)S(1)}, u32[]{:S(2)}, u32[]{:S(2)}) collective-permute-start(bf16[3,320,640]{2,1,0:T(8,128)(2,1)} %pad_maximum_fusion), channel_id=1, source_target_pairs={{0,1},{1,0},{2,3},{3,2},{4,5},{5,4},{6,7},{7,6},{8,9},{9,8},{10,11... | collective-permute-start | bytes 3686408 | tf_op jit(solution)/shard_map/ppermute | solution.py:30
  38.7 4.0 %collective-permute-start.8 = (bf16[3,160,640]{2,1,0:T(8,128)(2,1)S(1)}, bf16[3,160,640]{2,1,0:T(8,128)(2,1)}, u32[]{:S(2)}, u32[]{:S(2)}) collective-permute-start(bf16[3,160,640]{2,1,0:T(8,128)(2,1)S(1)} %collective-permute-done.5.w_a), channel_id=1, source_target_pairs={{0,4},{4,0},{1,5},{5,1},{2,6},{6,2},{3,7},{7,3},{8,12},{12,8},{9,1... | collective-permute-start | bytes 1843208 | tf_op jit(solution)/shard_map/ppermute | solution.py:30
  63.8 8.3 %copy-start.3 = (bf16[3,320,640]{2,1,0:T(8,128)(2,1)}, bf16[3,320,640]{2,1,0:T(8,128)(2,1)S(1)}, u32[]{:S(2)}) copy-start(bf16[3,320,640]{2,1,0:T(8,128)(2,1)S(1)} %collective-permute-done.7.hy) | copy-start | bytes 3686404
  64.8 30.0 %copy-start.33 = (f32[640]{0:T(1024)S(1)}, f32[640]{0:T(1024)}, u32[]{:S(2)}) copy-start(f32[640]{0:T(1024)} %param.18) | copy-start | bytes 7684
  64.8 28.2 %collective-permute-start.10 = (bf16[3,208,640]{2,1,0:T(8,128)(2,1)}, bf16[3,208,640]{2,1,0:T(8,128)(2,1)}, u32[]{:S(2)}, u32[]{:S(2)}) collective-permute-start(bf16[3,208,640]{2,1,0:T(8,128)(2,1)} %slice.49), channel_id=1, source_target_pairs={{0,2},{2,0},{1,3},{3,1},{4,6},{6,4},{5,7},{7,5},{8,10},{10,8},{9,1... | collective-permute-start | bytes 2396168 | tf_op jit(solution)/shard_map/ppermute | solution.py:30
  65.4 24.2 %all-to-all-start = ((bf16[4,320,256]{2,1,0:T(8,128)(2,1)}), bf16[4,320,256]{2,1,0:T(8,128)(2,1)S(1)}, u32[]{:S(2)}, u32[]{:S(2)}) async-start(bf16[4,320,256]{2,1,0:T(8,128)(2,1)} %bitcast.16), calls=%async_computation | async-start | bytes 1310720 | tf_op jit(solution)/shard_map/all_to_all | solution.py:757
  70.2 22.8 %collective-permute-start.9 = (bf16[3,112,640]{2,1,0:T(8,128)(2,1)S(1)}, bf16[3,112,640]{2,1,0:T(8,128)(2,1)}, u32[]{:S(2)}, u32[]{:S(2)}) collective-permute-start(bf16[3,112,640]{2,1,0:T(8,128)(2,1)S(1)} %slice.48), channel_id=1, source_target_pairs={{0,1},{1,0},{2,3},{3,2},{4,5},{5,4},{6,7},{7,6},{8,9},{9,8},{10,11... | collective-permute-start | bytes 1290248 | tf_op jit(solution)/shard_map/ppermute | solution.py:30
  72.0 25.3 %collective-permute-start.12 = (bf16[3,320,640]{2,1,0:T(8,128)(2,1)}, bf16[3,320,640]{2,1,0:T(8,128)(2,1)S(1)}, u32[]{:S(2)}, u32[]{:S(2)}) collective-permute-start(bf16[3,320,640]{2,1,0:T(8,128)(2,1)} %collective-permute-done.6.hx), channel_id=1, source_target_pairs={{0,4},{4,0},{1,5},{5,1},{2,6},{6,2},{3,7},{7,3},{8,12},{12,8},{9,1... | collective-permute-start | bytes 3686408 | tf_op jit(solution)/shard_map/ppermute | solution.py:30
  72.0 25.4 %collective-permute-start.13 = (bf16[3,320,640]{2,1,0:T(8,128)(2,1)S(1)}, bf16[3,320,640]{2,1,0:T(8,128)(2,1)}, u32[]{:S(2)}, u32[]{:S(2)}) collective-permute-start(bf16[3,320,640]{2,1,0:T(8,128)(2,1)S(1)} %collective-permute-done.7.hy), channel_id=1, source_target_pairs={{0,4},{4,0},{1,5},{5,1},{2,6},{6,2},{3,7},{7,3},{8,12},{12,8},{9,1... | collective-permute-start | bytes 3686408 | tf_op jit(solution)/shard_map/ppermute | solution.py:30
  72.5 20.4 %collective-permute-start.11 = (bf16[256,640]{1,0:T(8,128)(2,1)}, bf16[256,640]{1,0:T(8,128)(2,1)}, u32[]{:S(2)}, u32[]{:S(2)}) collective-permute-start(bf16[256,640]{1,0:T(8,128)(2,1)} %constant_dynamic-slice_fusion), channel_id=1, source_target_pairs={{0,1},{1,0},{2,3},{3,2},{4,5},{5,4},{6,7},{7,6},{8,9},{9,8},{10,11... | collective-permute-start | bytes 983048 | tf_op jit(solution)/shard_map/ppermute | solution.py:30
  89.7 7.7 %copy-start.4 = (bf16[4,320,256]{2,1,0:T(8,128)(2,1)}, bf16[4,320,256]{2,1,0:T(8,128)(2,1)S(1)}, u32[]{:S(2)}) copy-start(bf16[4,320,256]{2,1,0:T(8,128)(2,1)S(1)} %all-to-all-done.a) | copy-start | bytes 1966084
  93.0 4.4 %collective-permute-start.15 = (bf16[3,208,640]{2,1,0:T(8,128)(2,1)}, bf16[3,208,640]{2,1,0:T(8,128)(2,1)}, u32[]{:S(2)}, u32[]{:S(2)}) collective-permute-start(bf16[3,208,640]{2,1,0:T(8,128)(2,1)} %collective-permute-done.10.d1), channel_id=1, source_target_pairs={{0,4},{4,0},{1,5},{5,1},{2,6},{6,2},{3,7},{7,3},{8,12},{12,8},{9,1... | collective-permute-start | bytes 2396168 | tf_op jit(solution)/shard_map/ppermute | solution.py:30
  93.0 4.4 %collective-permute-start.14 = (bf16[3,112,640]{2,1,0:T(8,128)(2,1)}, bf16[3,112,640]{2,1,0:T(8,128)(2,1)S(1)}, u32[]{:S(2)}, u32[]{:S(2)}) collective-permute-start(bf16[3,112,640]{2,1,0:T(8,128)(2,1)} %collective-permute-done.9.d0), channel_id=1, source_target_pairs={{0,4},{4,0},{1,5},{5,1},{2,6},{6,2},{3,7},{7,3},{8,12},{12,8},{9,1... | collective-permute-start | bytes 1290248 | tf_op jit(solution)/shard_map/ppermute | solution.py:30
  118.8 5.0 %collective-permute-start.19 = (bf16[3,160,640]{2,1,0:T(8,128)(2,1)}, bf16[3,160,640]{2,1,0:T(8,128)(2,1)S(1)}, u32[]{:S(2)}, u32[]{:S(2)}) collective-permute-start(bf16[3,160,640]{2,1,0:T(8,128)(2,1)} %get-tuple-element.141), channel_id=1, source_target_pairs={{0,4},{4,0},{1,5},{5,1},{2,6},{6,2},{3,7},{7,3},{8,12},{12,8},{9,1... | collective-permute-start | bytes 1843208 | tf_op jit(solution)/shard_map/ppermute | solution.py:30
  118.9 6.9 %collective-permute-start.18 = (bf16[3,160,640]{2,1,0:T(8,128)(2,1)}, bf16[3,160,640]{2,1,0:T(8,128)(2,1)}, u32[]{:S(2)}, u32[]{:S(2)}) collective-permute-start(bf16[3,160,640]{2,1,0:T(8,128)(2,1)} %get-tuple-element.139), channel_id=1, source_target_pairs={{0,4},{4,0},{1,5},{5,1},{2,6},{6,2},{3,7},{7,3},{8,12},{12,8},{9,1... | collective-permute-start | bytes 1843208 | tf_op jit(solution)/shard_map/ppermute | solution.py:30
  119.4 8.2 %collective-permute-start.17 = (bf16[3,160,640]{2,1,0:T(8,128)(2,1)}, bf16[3,160,640]{2,1,0:T(8,128)(2,1)S(1)}, u32[]{:S(2)}, u32[]{:S(2)}) collective-permute-start(bf16[3,160,640]{2,1,0:T(8,128)(2,1)} %get-tuple-element.137), channel_id=1, source_target_pairs={{0,4},{4,0},{1,5},{5,1},{2,6},{6,2},{3,7},{7,3},{8,12},{12,8},{9,1... | collective-permute-start | bytes 1843208 | tf_op jit(solution)/shard_map/ppermute | solution.py:30
  119.4 10.2 %collective-permute-start.16 = (bf16[3,160,640]{2,1,0:T(8,128)(2,1)}, bf16[3,160,640]{2,1,0:T(8,128)(2,1)S(1)}, u32[]{:S(2)}, u32[]{:S(2)}) collective-permute-start(bf16[3,160,640]{2,1,0:T(8,128)(2,1)} %get-tuple-element.135), channel_id=1, source_target_pairs={{0,4},{4,0},{1,5},{5,1},{2,6},{6,2},{3,7},{7,3},{8,12},{12,8},{9,1... | collective-permute-start | bytes 1843208 | tf_op jit(solution)/shard_map/ppermute | solution.py:30
  119.9 13.4 %all-to-all-start.1 = ((bf16[4,320,256]{2,1,0:T(8,128)(2,1)}), bf16[4,320,256]{2,1,0:T(8,128)(2,1)S(1)}, u32[]{:S(2)}, u32[]{:S(2)}) async-start(bf16[4,320,256]{2,1,0:T(8,128)(2,1)} %get-tuple-element.133), calls=%async_computation.1 | async-start | bytes 1310720 | tf_op jit(solution)/shard_map/all_to_all | solution.py:757
  123.6 11.1 %collective-permute-start.24 = (bf16[3,160,640]{2,1,0:T(8,128)(2,1)}, bf16[3,160,640]{2,1,0:T(8,128)(2,1)}, u32[]{:S(2)}, u32[]{:S(2)}) collective-permute-start(bf16[3,160,640]{2,1,0:T(8,128)(2,1)} %get-tuple-element.150), channel_id=1, source_target_pairs={{0,4},{4,0},{1,5},{5,1},{2,6},{6,2},{3,7},{7,3},{8,12},{12,8},{9,1... | collective-permute-start | bytes 1843208 | tf_op jit(solution)/shard_map/ppermute | solution.py:30
  123.7 11.6 %collective-permute-start.25 = (bf16[3,160,640]{2,1,0:T(8,128)(2,1)}, bf16[3,160,640]{2,1,0:T(8,128)(2,1)}, u32[]{:S(2)}, u32[]{:S(2)}) collective-permute-start(bf16[3,160,640]{2,1,0:T(8,128)(2,1)} %get-tuple-element.151), channel_id=1, source_target_pairs={{0,4},{4,0},{1,5},{5,1},{2,6},{6,2},{3,7},{7,3},{8,12},{12,8},{9,1... | collective-permute-start | bytes 1843208 | tf_op jit(solution)/shard_map/ppermute | solution.py:30
  125.8 10.9 %collective-permute-start.26 = (bf16[3,160,640]{2,1,0:T(8,128)(2,1)}, bf16[3,160,640]{2,1,0:T(8,128)(2,1)}, u32[]{:S(2)}, u32[]{:S(2)}) collective-permute-start(bf16[3,160,640]{2,1,0:T(8,128)(2,1)} %get-tuple-element.152), channel_id=1, source_target_pairs={{0,4},{4,0},{1,5},{5,1},{2,6},{6,2},{3,7},{7,3},{8,12},{12,8},{9,1... | collective-permute-start | bytes 1843208 | tf_op jit(solution)/shard_map/ppermute | solution.py:30
  127.6 29.2 %collective-permute-start.27 = (bf16[3,160,640]{2,1,0:T(8,128)(2,1)}, bf16[3,160,640]{2,1,0:T(8,128)(2,1)}, u32[]{:S(2)}, u32[]{:S(2)}) collective-permute-start(bf16[3,160,640]{2,1,0:T(8,128)(2,1)} %get-tuple-element.153), channel_id=1, source_target_pairs={{0,4},{4,0},{1,5},{5,1},{2,6},{6,2},{3,7},{7,3},{8,12},{12,8},{9,1... | collective-permute-start | bytes 1843208 | tf_op jit(solution)/shard_map/ppermute | solution.py:30
  129.6 7.7 %copy-start.38 = (f32[80]{0:T(128)S(1)}, f32[80]{0:T(128)}, u32[]{:S(2)}) copy-start(f32[80]{0:T(128)} %param.16) | copy-start | bytes 964
  133.3 23.5 %collective-permute-start.20 = (bf16[3,160,640]{2,1,0:T(8,128)(2,1)S(1)}, bf16[3,160,640]{2,1,0:T(8,128)(2,1)}, u32[]{:S(2)}, u32[]{:S(2)}) collective-permute-start(bf16[3,160,640]{2,1,0:T(8,128)(2,1)S(1)} %add_convert_fusion.11), channel_id=1, source_target_pairs={{0,2},{2,0},{1,3},{3,1},{4,6},{6,4},{5,7},{7,5},{8,10},{10,8},{9,1... | collective-permute-start | bytes 1843208 | tf_op jit(solution)/shard_map/ppermute | solution.py:30
  134.7 22.1 %collective-permute-start.21 = (bf16[3,160,640]{2,1,0:T(8,128)(2,1)S(1)}, bf16[3,160,640]{2,1,0:T(8,128)(2,1)}, u32[]{:S(2)}, u32[]{:S(2)}) collective-permute-start(bf16[3,160,640]{2,1,0:T(8,128)(2,1)S(1)} %add_convert_fusion.10), channel_id=1, source_target_pairs={{0,1},{1,0},{2,3},{3,2},{4,5},{5,4},{6,7},{7,6},{8,9},{9,8},{10,11... | collective-permute-start | bytes 1843208 | tf_op jit(solution)/shard_map/ppermute | solution.py:30
  135.3 26.7 %collective-permute-start.22 = (bf16[3,160,640]{2,1,0:T(8,128)(2,1)S(1)}, bf16[3,160,640]{2,1,0:T(8,128)(2,1)}, u32[]{:S(2)}, u32[]{:S(2)}) collective-permute-start(bf16[3,160,640]{2,1,0:T(8,128)(2,1)S(1)} %add_convert_fusion.9), channel_id=1, source_target_pairs={{0,2},{2,0},{1,3},{3,1},{4,6},{6,4},{5,7},{7,5},{8,10},{10,8},{9,1... | collective-permute-start | bytes 1843208 | tf_op jit(solution)/shard_map/ppermute | solution.py:30
  136.8 26.7 %collective-permute-start.23 = (bf16[3,160,640]{2,1,0:T(8,128)(2,1)S(1)}, bf16[3,160,640]{2,1,0:T(8,128)(2,1)}, u32[]{:S(2)}, u32[]{:S(2)}) collective-permute-start(bf16[3,160,640]{2,1,0:T(8,128)(2,1)S(1)} %add_convert_fusion.8), channel_id=1, source_target_pairs={{0,1},{1,0},{2,3},{3,2},{4,5},{5,4},{6,7},{7,6},{8,9},{9,8},{10,11... | collective-permute-start | bytes 1843208 | tf_op jit(solution)/shard_map/ppermute | solution.py:30
  150.6 12.9 %copy-start.30 = (f32[4,80,1]{2,1,0:T(8,128)S(1)}, f32[4,80,1]{2,1,0:T(8,128)}, u32[]{:S(2)}) copy-start(f32[4,80,1]{2,1,0:T(8,128)} %get-tuple-element.164) | copy-start | bytes 3844
  150.6 13.0 %copy-start.26 = (bf16[3,160,640]{2,1,0:T(8,128)(2,1)S(1)}, bf16[3,160,640]{2,1,0:T(8,128)(2,1)}, u32[]{:S(2)}) copy-start(bf16[3,160,640]{2,1,0:T(8,128)(2,1)} %get-tuple-element.156) | copy-start | bytes 1843204
  163.5 4.7 %collective-permute-start.30 = (bf16[2,3,160,640]{3,2,1,0:T(8,128)(2,1)}, bf16[2,3,160,640]{3,2,1,0:T(8,128)(2,1)S(1)}, u32[]{:S(2)}, u32[]{:S(2)}) collective-permute-start(bf16[2,3,160,640]{3,2,1,0:T(8,128)(2,1)} %get-tuple-element.160), channel_id=1, source_target_pairs={{0,4},{4,0},{1,5},{5,1},{2,6},{6,2},{3,7},{7,3},{8,12},{12,8},{9,1... | collective-permute-start | bytes 3686408 | tf_op jit(solution)/shard_map/ppermute | solution.py:30
  165.2 18.0 %collective-permute-start.29 = (bf16[3,160,640]{2,1,0:T(8,128)(2,1)S(1)}, bf16[3,160,640]{2,1,0:T(8,128)(2,1)}, u32[]{:S(2)}, u32[]{:S(2)}) collective-permute-start(bf16[3,160,640]{2,1,0:T(8,128)(2,1)S(1)} %add_convert_fusion.6), channel_id=1, source_target_pairs={{0,2},{2,0},{1,3},{3,1},{4,6},{6,4},{5,7},{7,5},{8,10},{10,8},{9,1... | collective-permute-start | bytes 1843208 | tf_op jit(solution)/shard_map/ppermute | solution.py:30
  167.2 16.2 %collective-permute-start.28 = (bf16[3,160,640]{2,1,0:T(8,128)(2,1)S(1)}, bf16[3,160,640]{2,1,0:T(8,128)(2,1)}, u32[]{:S(2)}, u32[]{:S(2)}) collective-permute-start(bf16[3,160,640]{2,1,0:T(8,128)(2,1)S(1)} %add_convert_fusion.7), channel_id=1, source_target_pairs={{0,1},{1,0},{2,3},{3,2},{4,5},{5,4},{6,7},{7,6},{8,9},{9,8},{10,11... | collective-permute-start | bytes 1843208 | tf_op jit(solution)/shard_map/ppermute | solution.py:30
  169.4 15.9 %collective-permute-start.31 = (bf16[3,160,640]{2,1,0:T(8,128)(2,1)}, bf16[3,160,640]{2,1,0:T(8,128)(2,1)S(1)}, u32[]{:S(2)}, u32[]{:S(2)}) collective-permute-start(bf16[3,160,640]{2,1,0:T(8,128)(2,1)} %fusion.2), channel_id=1, source_target_pairs={{0,8},{8,0},{16,24},{24,16},{1,9},{9,1},{17,25},{25,17},{2,10},{10... | collective-permute-start | bytes 1843208 | tf_op jit(solution)/shard_map/ppermute | solution.py:762
  171.6 8.6 %copy-start.24 = (bf16[3,160,640]{2,1,0:T(8,128)(2,1)S(1)}, bf16[3,160,640]{2,1,0:T(8,128)(2,1)}, u32[]{:S(2)}) copy-start(bf16[3,160,640]{2,1,0:T(8,128)(2,1)} %get-tuple-element.170) | copy-start | bytes 1843204
  188.0 16.2 %collective-permute-start.33 = (bf16[3,160,640]{2,1,0:T(8,128)(2,1)}, bf16[3,160,640]{2,1,0:T(8,128)(2,1)}, u32[]{:S(2)}, u32[]{:S(2)}) collective-permute-start(bf16[3,160,640]{2,1,0:T(8,128)(2,1)} %get-tuple-element.203), channel_id=1, source_target_pairs={{0,8},{8,0},{16,24},{24,16},{1,9},{9,1},{17,25},{25,17},{2,10},{10... | collective-permute-start | bytes 1843208 | tf_op jit(solution)/shard_map/ppermute | solution.py:762
  189.8 28.6 %collective-permute-start.32 = (bf16[3,160,640]{2,1,0:T(8,128)(2,1)S(1)}, bf16[3,160,640]{2,1,0:T(8,128)(2,1)}, u32[]{:S(2)}, u32[]{:S(2)}) collective-permute-start(bf16[3,160,640]{2,1,0:T(8,128)(2,1)S(1)} %fusion.1), channel_id=1, source_target_pairs={{0,24},{8,16},{16,8},{24,0},{1,25},{9,17},{17,9},{25,1},{2,26},{10... | collective-permute-start | bytes 1843208 | tf_op jit(solution)/shard_map/ppermute | solution.py:762
  192.4 59.9 %all-to-all-start.2 = ((bf16[4,528,640]{2,1,0:T(8,128)(2,1)}), bf16[4,528,640]{2,1,0:T(8,128)(2,1)S(1)}, u32[]{:S(2)}, u32[]{:S(2)}) async-start(bf16[4,528,640]{2,1,0:T(8,128)(2,1)} %project_back.1), calls=%async_computation.2 | async-start | bytes 5406720 | tf_op jit(solution)/shard_map/all_to_all | solution.py:757
  219.9 27.2 %collective-permute-start.39 = (bf16[3,160,640]{2,1,0:T(8,128)(2,1)S(1)}, bf16[3,160,640]{2,1,0:T(8,128)(2,1)}, u32[]{:S(2)}, u32[]{:S(2)}) collective-permute-start(bf16[3,160,640]{2,1,0:T(8,128)(2,1)S(1)} %add_convert_fusion.2), channel_id=1, source_target_pairs={{0,8},{8,0},{16,24},{24,16},{1,9},{9,1},{17,25},{25,17},{2,10},{10... | collective-permute-start | bytes 1843208 | tf_op jit(solution)/shard_map/ppermute | solution.py:762
  220.6 29.8 %collective-permute-start.34 = (bf16[2,256,640]{2,1,0:T(8,128)(2,1)}, bf16[2,256,640]{2,1,0:T(8,128)(2,1)}, u32[]{:S(2)}, u32[]{:S(2)}) collective-permute-start(bf16[2,256,640]{2,1,0:T(8,128)(2,1)} %get-tuple-element.180), channel_id=1, source_target_pairs={{0,1},{1,0},{2,3},{3,2},{4,5},{5,4},{6,7},{7,6},{8,9},{9,8},{10,11... | collective-permute-start | bytes 1966088 | tf_op jit(solution)/shard_map/ppermute | solution.py:30
  224.0 26.4 %copy-start.15 = (f32[256,640]{1,0:T(8,128)S(1)}, f32[256,640]{1,0:T(8,128)}, u32[]{:S(2)}) copy-start(f32[256,640]{1,0:T(8,128)} %get-tuple-element.181) | copy-start | bytes 1966084
  224.0 40.7 %collective-permute-start.35 = (bf16[3,160,640]{2,1,0:T(8,128)(2,1)}, bf16[3,160,640]{2,1,0:T(8,128)(2,1)}, u32[]{:S(2)}, u32[]{:S(2)}) collective-permute-start(bf16[3,160,640]{2,1,0:T(8,128)(2,1)} %add_convert_fusion.3), channel_id=1, source_target_pairs={{0,24},{8,16},{16,8},{24,0},{1,25},{9,17},{17,9},{25,1},{2,26},{10... | collective-permute-start | bytes 1843208 | tf_op jit(solution)/shard_map/ppermute | solution.py:762
  249.3 10.5 %collective-permute-start.40 = (bf16[3,160,640]{2,1,0:T(8,128)(2,1)}, bf16[3,160,640]{2,1,0:T(8,128)(2,1)}, u32[]{:S(2)}, u32[]{:S(2)}) collective-permute-start(bf16[3,160,640]{2,1,0:T(8,128)(2,1)} %get-tuple-element.210), channel_id=1, source_target_pairs={{0,1},{1,0},{2,3},{3,2},{4,5},{5,4},{6,7},{7,6},{8,9},{9,8},{10,11... | collective-permute-start | bytes 1843208 | tf_op jit(solution)/shard_map/ppermute | solution.py:30
  250.4 19.5 %collective-permute-start.41 = (bf16[3,160,640]{2,1,0:T(8,128)(2,1)}, bf16[3,160,640]{2,1,0:T(8,128)(2,1)}, u32[]{:S(2)}, u32[]{:S(2)}) collective-permute-start(bf16[3,160,640]{2,1,0:T(8,128)(2,1)} %get-tuple-element.211.mine), channel_id=1, source_target_pairs={{0,4},{4,0},{1,5},{5,1},{2,6},{6,2},{3,7},{7,3},{8,12},{12,8},{9,1... | collective-permute-start | bytes 1843208 | tf_op jit(solution)/shard_map/ppermute | solution.py:30
  252.3 1.7 collective-permute-start.36
  254.1 5.7 %collective-permute-start.37 = (f32[9,640]{1,0:T(8,128)S(1)}, f32[9,640]{1,0:T(8,128)S(1)}, u32[]{:S(2)}, u32[]{:S(2)}) collective-permute-start(f32[9,640]{1,0:T(8,128)S(1)} %add.150), channel_id=1, source_target_pairs={{0,8},{8,0},{16,24},{24,16},{1,9},{9,1},{17,25},{25,17},{2,10},{10... | collective-permute-start | bytes 69128 | tf_op jit(solution)/shard_map/ppermute | solution.py:762
  259.7 10.1 %collective-permute-start.42 = (bf16[3,160,640]{2,1,0:T(8,128)(2,1)}, bf16[3,160,640]{2,1,0:T(8,128)(2,1)}, u32[]{:S(2)}, u32[]{:S(2)}) collective-permute-start(bf16[3,160,640]{2,1,0:T(8,128)(2,1)} %collective-permute-done.40.theirs), channel_id=1, source_target_pairs={{0,4},{4,0},{1,5},{5,1},{2,6},{6,2},{3,7},{7,3},{8,12},{12,8},{9,1... | collective-permute-start | bytes 1843208 | tf_op jit(solution)/shard_map/ppermute | solution.py:30
  259.8 5.0 %collective-permute-start.38 = (f32[9,640]{1,0:T(8,128)S(1)}, f32[9,640]{1,0:T(8,128)S(1)}, u32[]{:S(2)}, u32[]{:S(2)}) collective-permute-start(f32[9,640]{1,0:T(8,128)S(1)} %add.151), channel_id=1, source_target_pairs={{0,16},{8,24},{16,0},{24,8},{1,17},{9,25},{17,1},{25,9},{2,18},{10... | collective-permute-start | bytes 69128 | tf_op jit(solution)/shard_map/ppermute | solution.py:762
  267.0 15.4 %collective-permute-start.43 = (bf16[3,160,640]{2,1,0:T(8,128)(2,1)}, bf16[3,160,640]{2,1,0:T(8,128)(2,1)}, u32[]{:S(2)}, u32[]{:S(2)}) collective-permute-start(bf16[3,160,640]{2,1,0:T(8,128)(2,1)} %add_convert_fusion.1), channel_id=1, source_target_pairs={{0,8},{8,0},{16,24},{24,16},{1,9},{9,1},{17,25},{25,17},{2,10},{10... | collective-permute-start | bytes 1843208 | tf_op jit(solution)/shard_map/ppermute | solution.py:762
  275.4 11.4 %copy-start = (s32[4]{0:T(128)S(1)}, s32[4]{0:T(128)}, u32[]{:S(2)}) copy-start(s32[4]{0:T(128)} %pad_add_fusion.at) | copy-start | bytes 52
  283.8 2.1 collective-permute-start.44
  283.9 2.9 %collective-permute-start.45 = (bf16[3,160,640]{2,1,0:T(8,128)(2,1)S(1)}, bf16[3,160,640]{2,1,0:T(8,128)(2,1)S(1)}, u32[]{:S(2)}, u32[]{:S(2)}) collective-permute-start(bf16[3,160,640]{2,1,0:T(8,128)(2,1)S(1)} %get-tuple-element.208.b), channel_id=1, source_target_pairs={{0,4},{4,0},{1,5},{5,1},{2,6},{6,2},{3,7},{7,3},{8,12},{12,8},{9,1... | collective-permute-start | bytes 1843208 | tf_op jit(solution)/shard_map/ppermute | solution.py:30
  (24 other events, 68.2 us)

commit v2 on v1

--- a/solution.py
+++ b/solution.py
@@ -931,11 +931,12 @@
     w_theirs = swap(w_theirs, "col")
     total = jnp.sum(es[:, tok + 2 : tok + 11].astype(F32), axis=0)
     total = total + swap(total, "core")
-    total = total + z_swap(total, 1)
-    total = total + z_swap(total, 2)
-    met_c, mine_c, total = together((met_c, mine_c, total))
+    total_z = z_swap(total, 1)
     mine_c = add(mine_c, met_c)
     other_c = z_swap(mine_c, 1)
+    w_theirs = after(w_theirs, mine_c)
+    total = total + after(total_z, mine_c)
+    total = total + z_swap(total, 2)
     w_args = (at, w_own, w_theirs, swap(w_own, "core"), swap(w_theirs, "core"))
     sum_qkv = call(
         finish_qkv_kernel,

time: 291 us -> 290 us (level)
  other arithmetic: 36.8 us -> 40 us
  waiting for transfers between devices: 110 us -> 107 us
    unnamed x79 -> x77, local copies, waits for them, and re-layouts: 8.07 us -> 7.16 us
  transfers between devices with their start and end apart: 49 -> 49, of which waited for: 19 -> 19; matrix products, arithmetic and copies ran while one was open for 17% -> 18% of each run, Pallas kernels for 18% -> 18%
where the time goes in v2:
time: 290 us; the launch traced here: 288 us
  waiting for transfers between devices  107 us (37%)
  Pallas kernels  74.4 us (26%)
  starting transfers between devices  44.3 us (15%)
  other arithmetic  40 us (14%)
  local copies, waits for them, and re-layouts  21 us (7%)
    ppermute x8, waiting for transfers between devices, z_swap(): return lax.ppermute(x, 'z', [(i, i ^ step) for i in range(n)])  54.4 us
    pallas_call x7, Pallas kernels, call(): pl.pallas_call(kernel, in_specs=specs, **more, out_shape=outs, scratch_sh...  51.6 us
    ppermute x38, waiting for transfers between devices, swap(): return lax.ppermute(x, axis, [(0, 1), (1, 0)])  34.6 us
    ppermute x38, starting transfers between devices, swap(): return lax.ppermute(x, axis, [(0, 1), (1, 0)])  23.9 us
    all_to_all x3, waiting for transfers between devices, all_four(): return lax.all_to_all(x, ('row', 'col'), 0, 0, tiled=True)  18.4 us
    convert_element_type x11, other arithmetic, add(): return total.astype(BF)  13.9 us
    pallas_call x1, Pallas kernels, attention_backward(): pl.pallas_call(functools.partial(backward_kernel, block), grid=(heads,),...  12.5 us
    all_to_all x3, starting transfers between devices, all_four(): return lax.all_to_all(x, ('row', 'col'), 0, 0, tiled=True)  11.3 us
  transfers between devices with their start and end apart: 49, of which 19 were waited for; matrix products, arithmetic and copies ran while one was open for 18% of the time, Pallas kernels for 18%

profile of v2, /device:TPU:0, one launch (start us, length us, event | category | flops | bytes accessed | tf_op | source)
XLA Modules:
  0.0 288.4 jit_solution(524501437565273185)
XLA Ops:
  0.6 3.0 %collective-permute-start = (bf16[512,640]{1,0:T(8,128)(2,1)}, bf16[512,640]{1,0:T(8,128)(2,1)S(1)}, u32[]{:S(2)}, u32[]{:S(2)}) collective-permute-start(bf16[512,640]{1,0:T(8,128)(2,1)} %x00.3), channel_id=1, source_target_pairs={{0,1},{1,0},{2,3},{3,2},{4,5},{5,4},{6,7},{7,6},{8,9},{9,8},{10,11... | collective-permute-start | bytes 1966088 | tf_op jit(solution)/shard_map/ppermute | solution.py:30
  3.7 1.5 collective-permute-start.1
  7.9 3.9 %copy.27 = bf16[640,3,640]{0,2,1:T(8,128)(2,1)S(1)} copy(bf16[640,3,640]{2,0,1:T(8,128)(2,1)} %param.15) | data formatting | bytes 4915200 | tf_op args[2]
  11.9 1.1 dynamic-slice_bitcast_fusion.4
  13.3 1.1 dynamic-slice_bitcast_fusion.w_mine
  14.5 1.2 pad_maximum_fusion
  16.5 3.8 %collective-permute-done.3 = f32[640]{0:T(1024)S(1)} collective-permute-done((f32[640]{0:T(1024)S(1)}, f32[640]{0:T(1024)S(1)}, u32[]{:S(2)}, u32[]{:S(2)}) %collective-permute-start.3) | collective-permute-done | bytes 2592 | tf_op jit(solution)/shard_map/ppermute | solution.py:30
  20.3 1.6 collective-permute-start.4
  22.3 13.7 %collective-permute-done.5.w_a = bf16[3,160,640]{2,1,0:T(8,128)(2,1)S(1)} collective-permute-done((bf16[3,160,640]{2,1,0:T(8,128)(2,1)S(1)}, bf16[3,160,640]{2,1,0:T(8,128)(2,1)S(1)}, u32[]{:S(2)}, u32[]{:S(2)}) %collective-permute-start.5) | collective-permute-done | bytes 614432 | tf_op jit(solution)/shard_map/ppermute | solution.py:30
  36.0 1.2 collective-permute-start.6
  42.6 8.1 %project.1 = (bf16[3,320,1024]{2,1,0:T(8,128)(2,1)}, f32[320,1024]{1,0:T(8,128)}, bf16[1024,1280]{1,0:T(8,128)(2,1)}, f32[512,1]{1,0:T(8,128)}, bf16[960,1280]{1,0:T(8,128)(2,1)}) custom-call(s32[4]{0:T(128)} %pad_add_fusion.at, bf16[512,640]{1,0:T(8,128)(2,1)} %x00.3, bf16[512,640]{1,0:T(8,128)(2,1)} %copy-done.2, ...), custom_call_target="tpu_custom_call" | custom-call | flops 1 | bytes 1 | tf_op jit(solution)/shard_map/project/pallas_call | solution.py:508
  50.7 10.3 %attention_forward.1 = (bf16[4,80,1024]{2,1,0:T(8,128)(2,1)}, f32[4,1,1024]{2,1,0:T(1,128)}, bf16[4,4,80,256]{3,2,1,0:T(8,128)(2,1)}) custom-call(s32[4]{0:T(128)} %pad_add_fusion.at, bf16[3,4,80,1024]{3,2,1,0:T(8,128)(2,1)} %bitcast.52, s32[1,1024]{1,0:T(1,128)} %bitcast.59, s32[1024,1]{1,0:T(8,128)} %copy.29.scol_ref, s32[1024,1]{1,0:T(8,128)} %copy.30.kpos_ref), custom_call_target="tpu_custom_call" | custom-call | flops 1 | bytes 1 | tf_op jit(solution)/shard_map/attention_forward/pallas_call | solution.py:260
  61.0 1.8 collective-permute-done.6.hx
  65.4 3.7 %all-to-all-start = ((bf16[4,320,256]{2,1,0:T(8,128)(2,1)}), bf16[4,320,256]{2,1,0:T(8,128)(2,1)S(1)}, u32[]{:S(2)}, u32[]{:S(2)}) async-start(bf16[4,320,256]{2,1,0:T(8,128)(2,1)} %bitcast.16), calls=%async_computation | async-start | bytes 1310720 | tf_op jit(solution)/shard_map/all_to_all | solution.py:757
  69.1 1.1 slice.48
  70.2 1.9 collective-permute-start.9
  72.8 16.8 %all-to-all-done.a = bf16[4,320,256]{2,1,0:T(8,128)(2,1)S(1)} async-done(((bf16[4,320,256]{2,1,0:T(8,128)(2,1)}), bf16[4,320,256]{2,1,0:T(8,128)(2,1)S(1)}, u32[]{:S(2)}, u32[]{:S(2)}) %all-to-all-start) | async-done | bytes 655392 | tf_op jit(solution)/shard_map/all_to_all | solution.py:757
  89.5 3.3 %collective-permute-done.11.g_col = bf16[256,640]{1,0:T(8,128)(2,1)} collective-permute-done((bf16[256,640]{1,0:T(8,128)(2,1)}, bf16[256,640]{1,0:T(8,128)(2,1)}, u32[]{:S(2)}, u32[]{:S(2)}) %collective-permute-start.11) | collective-permute-done | bytes 327712 | tf_op jit(solution)/shard_map/ppermute | solution.py:30
  98.4 13.4 %feed_forward.1 = (bf16[256,640]{1,0:T(8,128)(2,1)}, f32[256,640]{1,0:T(8,128)}, bf16[2,256,640]{2,1,0:T(8,128)(2,1)}, bf16[4,320,256]{2,1,0:T(8,128)(2,1)}, f32...) custom-call(s32[4]{0:T(128)} %pad_add_fusion.at, ...), custom_call_target="tpu_custom_call" | custom-call | flops 1 | bytes 1 | tf_op jit(solution)/shard_map/feed_forward/pallas_call | solution.py:508
  111.8 6.8 %feed_weights.1 = (bf16[3,160,640]{2,1,0:T(8,128)(2,1)}, bf16[3,160,640]{2,1,0:T(8,128)(2,1)}, bf16[3,160,640]{2,1,0:T(8,128)(2,1)}, bf16[3,160,640]{2,1,0:T(8,1...) custom-call(s32[4]{0:T(128)} %pad_add_fusion.at, ...), custom_call_target="tpu_custom_call" | custom-call | flops 1 | bytes 1 | tf_op jit(solution)/shard_map/feed_weights/pallas_call | solution.py:508
  119.7 3.7 %all-to-all-start.1 = ((bf16[4,320,256]{2,1,0:T(8,128)(2,1)}), bf16[4,320,256]{2,1,0:T(8,128)(2,1)S(1)}, u32[]{:S(2)}, u32[]{:S(2)}) async-start(bf16[4,320,256]{2,1,0:T(8,128)(2,1)} %get-tuple-element.132), calls=%async_computation.1 | async-start | bytes 1310720 | tf_op jit(solution)/shard_map/all_to_all | solution.py:757
  124.4 1.2 add_convert_fusion.8
  126.2 1.2 add_convert_fusion.9
  128.2 1.2 add_convert_fusion.10
  130.3 1.2 add_convert_fusion.11
  131.5 1.6 all-to-all-done.1
  133.1 1.4 collective-permute-start.20
  135.2 1.5 collective-permute-start.22
  137.9 12.5 %attention_backward.1 = (bf16[3,4,80,1024]{3,2,1,0:T(8,128)(2,1)}, f32[4,80,1]{2,1,0:T(8,128)}) custom-call(s32[4]{0:T(128)} %pad_add_fusion.at, bf16[3,4,80,1024]{3,2,1,0:T(8,128)(2,1)} %bitcast.53, f32[4,80,1024]{2,1,0:T(8,128)} %bitcast.58, f32[80,1]{1,0:T(8,128)} %copy.31.factor_ref, bf16[4,80,1024]{2,1,0:T(8,128)(2,1)} %get-tuple-element.131.out_ref, ...), custom_call_target="tpu_custom_call" | custom-call | flops 1 | bytes 1 | tf_op jit(solution)/shard_map/attention_backward/pallas_call | solution.py:297
  150.5 6.2 %weight_back.1 = (bf16[2,3,160,640]{3,2,1,0:T(8,128)(2,1)}, bf16[2,3,160,640]{3,2,1,0:T(8,128)(2,1)}) custom-call(s32[4]{0:T(128)} %pad_add_fusion.at, bf16[3,320,1024]{2,1,0:T(8,128)(2,1)} %bitcast.50, bf16[1024,1280]{1,0:T(8,128)(2,1)} %get-tuple-element.143.normed), custom_call_target="tpu_custom_call" | custom-call | flops 1 | bytes 1 | tf_op jit(solution)/shard_map/weight_back/pallas_call | solution.py:508
  156.7 5.2 %collective-permute-done.22 = bf16[3,160,640]{2,1,0:T(8,128)(2,1)} collective-permute-done((bf16[3,160,640]{2,1,0:T(8,128)(2,1)S(1)}, bf16[3,160,640]{2,1,0:T(8,128)(2,1)}, u32[]{:S(2)}, u32[]{:S(2)}) %collective-permute-start.22) | collective-permute-done | bytes 614432 | tf_op jit(solution)/shard_map/ppermute | solution.py:30
  161.9 1.5 collective-permute-done.23
  163.5 1.5 add_convert_fusion.6
  165.4 1.6 add_convert_fusion.7
  169.2 1.6 collective-permute-start.31
  171.4 8.6 %project_back.1 = bf16[4,528,640]{2,1,0:T(8,128)(2,1)} custom-call(s32[4]{0:T(128)} %pad_add_fusion.at, bf16[960,1024]{1,0:T(8,128)(2,1)} %bitcast.51, bf16[960,1280]{1,0:T(8,128)(2,1)} %get-tuple-element.161.w_full, bf16[512,640]{1,0:T(8,128)(2,1)} %x00.3, bf16[512,640]{1,0:T(8,128)(2,1)} %copy-done.2, bf16[512,640]{1,0:T(8,128)(2,1)} %collective-permute-done.1.x10, ...), custom_call_target="tpu_custom_call" | custom-call | flops 1 | bytes 1 | tf_op jit(solution)/shard_map/project_back/pallas_call | solution.py:508
  180.0 1.5 convert_add_fusion.1
  181.5 1.5 convert_add_fusion.2
  183.2 2.0 collective-permute-done.31
  185.1 2.7 broadcast_select_fusion.4
  187.8 1.6 collective-permute-start.33
  189.7 2.5 collective-permute-start.32
  192.2 3.9 %all-to-all-start.2 = ((bf16[4,528,640]{2,1,0:T(8,128)(2,1)}), bf16[4,528,640]{2,1,0:T(8,128)(2,1)S(1)}, u32[]{:S(2)}, u32[]{:S(2)}) async-start(bf16[4,528,640]{2,1,0:T(8,128)(2,1)} %project_back.1), calls=%async_computation.2 | async-start | bytes 5406720 | tf_op jit(solution)/shard_map/all_to_all | solution.py:757
  196.1 7.9 %collective-permute-done.33 = bf16[3,160,640]{2,1,0:T(8,128)(2,1)} collective-permute-done((bf16[3,160,640]{2,1,0:T(8,128)(2,1)}, bf16[3,160,640]{2,1,0:T(8,128)(2,1)}, u32[]{:S(2)}, u32[]{:S(2)}) %collective-permute-start.33) | collective-permute-done | bytes 614432 | tf_op jit(solution)/shard_map/ppermute | solution.py:762
  204.1 14.3 %collective-permute-done.32 = bf16[3,160,640]{2,1,0:T(8,128)(2,1)} collective-permute-done((bf16[3,160,640]{2,1,0:T(8,128)(2,1)S(1)}, bf16[3,160,640]{2,1,0:T(8,128)(2,1)}, u32[]{:S(2)}, u32[]{:S(2)}) %collective-permute-start.32) | collective-permute-done | bytes 614432 | tf_op jit(solution)/shard_map/ppermute | solution.py:762
  218.3 2.0 add_convert_fusion.1
  221.0 1.3 add_convert_fusion.3
  222.3 2.7 collective-permute-start.37
  225.0 1.1 collective-permute-start.34
  226.1 21.6 %collective-permute-done.39 = bf16[3,160,640]{2,1,0:T(8,128)(2,1)} collective-permute-done((bf16[3,160,640]{2,1,0:T(8,128)(2,1)}, bf16[3,160,640]{2,1,0:T(8,128)(2,1)}, u32[]{:S(2)}, u32[]{:S(2)}) %collective-permute-start.39) | collective-permute-done | bytes 614432 | tf_op jit(solution)/shard_map/ppermute | solution.py:762
  247.7 2.2 broadcast_select_fusion.2
  249.9 1.1 collective-permute-start.40
  251.0 2.0 add_convert_fusion.2
  253.1 1.1 broadcast_select_fusion.6
  255.1 2.1 convert_select_fusion.1
  257.2 3.0 %collective-permute-done.40.theirs = bf16[3,160,640]{2,1,0:T(8,128)(2,1)} collective-permute-done((bf16[3,160,640]{2,1,0:T(8,128)(2,1)S(1)}, bf16[3,160,640]{2,1,0:T(8,128)(2,1)}, u32[]{:S(2)}, u32[]{:S(2)}) %collective-permute-start.40) | collective-permute-done | bytes 614432 | tf_op jit(solution)/shard_map/ppermute | solution.py:30
  260.8 1.4 convert_reduce_fusion
  262.5 1.2 fusion.7
  263.6 6.7 %collective-permute-done.36 = f32[9,640]{1,0:T(8,128)S(1)} collective-permute-done((f32[9,640]{1,0:T(8,128)S(1)}, f32[9,640]{1,0:T(8,128)S(1)}, u32[]{:S(2)}, u32[]{:S(2)}) %collective-permute-start.36) | collective-permute-done | bytes 23072 | tf_op jit(solution)/shard_map/ppermute | solution.py:762
  270.4 3.1 %fusion = f32[512,640]{1,0:T(8,128)} fusion(f32[256,640]{1,0:T(8,128)} %get-tuple-element.205, f32[256,640]{1,0:T(8,128)} %get-tuple-element.204, bf16[512,640]{1,0:T(8,128)(2,1)S(1)} %copy-done.1, f32[512,640]{1,0:T(8,128)} %convert_reduce_fusion, f32[512]{0:T(512)S(1)} %get-tuple-element.196, f32[640]{0:T(1024)S(1)} %copy-done.31, f32[512]{0:T(512)S(1)} %get-tuple-element.195), kind=kLoop, calls=%fused_computation.3 | loop fusion | flops 2293760 | bytes 4594176 | tf_op jit(solution)/shard_map/sub | solution.py:954
  273.5 1.9 collective-permute-done.38
  275.5 5.5 %finish_qkv.1 = f32[3,640,640]{2,1,0:T(8,128)} custom-call(s32[4]{0:T(128)} %pad_add_fusion.at, bf16[3,160,640]{2,1,0:T(8,128)(2,1)} %get-tuple-element.209.mine, bf16[3,160,640]{2,1,0:T(8,128)(2,1)} %collective-permute-done.40.theirs, bf16[3,160,640]{2,1,0:T(8,128)(2,1)} %collective-permute-done.41.mine2, bf16[3,160,640]{2,1,0:T(8,128)(2,1)} %collective-permute-done.42.theirs2), custom_call_target="tpu_custom_call" | custom-call | flops 1 | bytes 1 | tf_op jit(solution)/shard_map/finish_qkv/pallas_call | solution.py:508
  281.0 1.4 broadcast_select_fusion
  285.3 3.0 %finish_feed.1 = (f32[640,640]{1,0:T(8,128)}, f32[640,640]{1,0:T(8,128)}, f32[640,640]{1,0:T(8,128)}) custom-call(s32[4]{0:T(128)S(1)} %copy-done, bf16[3,160,640]{2,1,0:T(8,128)(2,1)S(1)} %get-tuple-element.207.a, bf16[3,160,640]{2,1,0:T(8,128)(2,1)S(1)} %get-tuple-element.206.b, bf16[3,160,640]{2,1,0:T(8,128)(2,1)S(1)} %collective-permute-done.44.a2, ...), custom_call_target="tpu_custom_call" | custom-call | flops 1 | bytes 1 | tf_op jit(solution)/shard_map/finish_feed/pallas_call | solution.py:508
  (184 shorter events, 34.1 us)
Async XLA Ops:
  0.6 19.6 %collective-permute-start = (bf16[512,640]{1,0:T(8,128)(2,1)}, bf16[512,640]{1,0:T(8,128)(2,1)S(1)}, u32[]{:S(2)}, u32[]{:S(2)}) collective-permute-start(bf16[512,640]{1,0:T(8,128)(2,1)} %x00.3), channel_id=1, source_target_pairs={{0,1},{1,0},{2,3},{3,2},{4,5},{5,4},{6,7},{7,6},{8,9},{9,8},{10,11... | collective-permute-start | bytes 1966088 | tf_op jit(solution)/shard_map/ppermute | solution.py:30
  3.7 16.6 %collective-permute-start.1 = (bf16[512,640]{1,0:T(8,128)(2,1)}, bf16[512,640]{1,0:T(8,128)(2,1)}, u32[]{:S(2)}, u32[]{:S(2)}) collective-permute-start(bf16[512,640]{1,0:T(8,128)(2,1)} %x00.3), channel_id=1, source_target_pairs={{0,2},{2,0},{1,3},{3,1},{4,6},{6,4},{5,7},{7,5},{8,10},{10,8},{9,1... | collective-permute-start | bytes 1966088 | tf_op jit(solution)/shard_map/ppermute | solution.py:30
  6.6 13.7 %collective-permute-start.2 = (f32[1920]{0:T(1024)S(1)}, f32[1920]{0:T(1024)S(1)}, u32[]{:S(2)}, u32[]{:S(2)}) collective-permute-start(f32[1920]{0:T(1024)S(1)} %pad_maximum_fusion.2), channel_id=1, source_target_pairs={{0,1},{1,0},{2,3},{3,2},{4,5},{5,4},{6,7},{7,6},{8,9},{9,8},{10,11... | collective-permute-start | bytes 23048 | tf_op jit(solution)/shard_map/ppermute | solution.py:30
  7.8 12.5 %collective-permute-start.3 = (f32[640]{0:T(1024)S(1)}, f32[640]{0:T(1024)S(1)}, u32[]{:S(2)}, u32[]{:S(2)}) collective-permute-start(f32[640]{0:T(1024)S(1)} %convert_element_type.167), channel_id=1, source_target_pairs={{0,2},{2,0},{1,3},{3,1},{4,6},{6,4},{5,7},{7,5},{8,10},{10,8},{9,1... | collective-permute-start | bytes 7688 | tf_op jit(solution)/shard_map/ppermute | solution.py:30
  14.5 23.3 %copy-start.36 = (f32[80]{0:T(128)S(1)}, f32[80]{0:T(128)}, u32[]{:S(2)}) copy-start(f32[80]{0:T(128)} %param.16) | copy-start | bytes 964
  14.5 24.2 %copy-start.34 = (s32[1024]{0:T(1024)S(1)}, s32[1024]{0:T(1024)}, u32[]{:S(2)}) copy-start(s32[1024]{0:T(1024)} %param.24) | copy-start | bytes 12292
  15.7 24.0 %copy-start.30 = (s32[1024]{0:T(1024)S(1)}, s32[1024]{0:T(1024)}, u32[]{:S(2)}) copy-start(s32[1024]{0:T(1024)} %param.23) | copy-start | bytes 12292
  15.7 26.2 %copy-start.31 = (f32[640]{0:T(1024)S(1)}, f32[640]{0:T(1024)}, u32[]{:S(2)}) copy-start(f32[640]{0:T(1024)} %param.14) | copy-start | bytes 7684
  20.2 30.4 %copy-start.35 = (f32[640]{0:T(1024)}, f32[640]{0:T(1024)S(1)}, u32[]{:S(2)}) copy-start(f32[640]{0:T(1024)S(1)} %collective-permute-done.3) | copy-start | bytes 7684
  20.2 22.3 %copy-start.2 = (bf16[512,640]{1,0:T(8,128)(2,1)}, bf16[512,640]{1,0:T(8,128)(2,1)S(1)}, u32[]{:S(2)}) copy-start(bf16[512,640]{1,0:T(8,128)(2,1)S(1)} %collective-permute-done.x01.x_col) | copy-start | bytes 1966084
  20.3 15.7 %collective-permute-start.4 = (bf16[512,640]{1,0:T(8,128)(2,1)S(1)}, bf16[512,640]{1,0:T(8,128)(2,1)S(1)}, u32[]{:S(2)}, u32[]{:S(2)}) collective-permute-start(bf16[512,640]{1,0:T(8,128)(2,1)S(1)} %collective-permute-done.x01.x_col), channel_id=1, source_target_pairs={{0,2},{2,0},{1,3},{3,1},{4,6},{6,4},{5,7},{7,5},{8,10},{10,8},{9,1... | collective-permute-start | bytes 1966088 | tf_op jit(solution)/shard_map/ppermute | solution.py:30
  21.8 14.2 %collective-permute-start.5 = (bf16[3,160,640]{2,1,0:T(8,128)(2,1)S(1)}, bf16[3,160,640]{2,1,0:T(8,128)(2,1)S(1)}, u32[]{:S(2)}, u32[]{:S(2)}) collective-permute-start(bf16[3,160,640]{2,1,0:T(8,128)(2,1)S(1)} %dynamic-slice_bitcast_fusion.1), channel_id=1, source_target_pairs={{0,1},{1,0},{2,3},{3,2},{4,5},{5,4},{6,7},{7,6},{8,9},{9,8},{10,11... | collective-permute-start | bytes 1843208 | tf_op jit(solution)/shard_map/ppermute | solution.py:30
  36.0 26.8 %collective-permute-start.6 = (bf16[3,320,640]{2,1,0:T(8,128)(2,1)}, bf16[3,320,640]{2,1,0:T(8,128)(2,1)}, u32[]{:S(2)}, u32[]{:S(2)}) collective-permute-start(bf16[3,320,640]{2,1,0:T(8,128)(2,1)} %pad_maximum_fusion), channel_id=1, source_target_pairs={{0,2},{2,0},{1,3},{3,1},{4,6},{6,4},{5,7},{7,5},{8,10},{10,8},{9,1... | collective-permute-start | bytes 3686408 | tf_op jit(solution)/shard_map/ppermute | solution.py:30
  37.1 26.6 %collective-permute-start.7 = (bf16[3,320,640]{2,1,0:T(8,128)(2,1)}, bf16[3,320,640]{2,1,0:T(8,128)(2,1)S(1)}, u32[]{:S(2)}, u32[]{:S(2)}) collective-permute-start(bf16[3,320,640]{2,1,0:T(8,128)(2,1)} %pad_maximum_fusion), channel_id=1, source_target_pairs={{0,1},{1,0},{2,3},{3,2},{4,5},{5,4},{6,7},{7,6},{8,9},{9,8},{10,11... | collective-permute-start | bytes 3686408 | tf_op jit(solution)/shard_map/ppermute | solution.py:30
  38.7 3.9 %collective-permute-start.8 = (bf16[3,160,640]{2,1,0:T(8,128)(2,1)S(1)}, bf16[3,160,640]{2,1,0:T(8,128)(2,1)}, u32[]{:S(2)}, u32[]{:S(2)}) collective-permute-start(bf16[3,160,640]{2,1,0:T(8,128)(2,1)S(1)} %collective-permute-done.5.w_a), channel_id=1, source_target_pairs={{0,4},{4,0},{1,5},{5,1},{2,6},{6,2},{3,7},{7,3},{8,12},{12,8},{9,1... | collective-permute-start | bytes 1843208 | tf_op jit(solution)/shard_map/ppermute | solution.py:30
  63.8 8.3 %copy-start.3 = (bf16[3,320,640]{2,1,0:T(8,128)(2,1)}, bf16[3,320,640]{2,1,0:T(8,128)(2,1)S(1)}, u32[]{:S(2)}) copy-start(bf16[3,320,640]{2,1,0:T(8,128)(2,1)S(1)} %collective-permute-done.7.hy) | copy-start | bytes 3686404
  64.8 29.9 %copy-start.32 = (f32[640]{0:T(1024)S(1)}, f32[640]{0:T(1024)}, u32[]{:S(2)}) copy-start(f32[640]{0:T(1024)} %param.18) | copy-start | bytes 7684
  64.8 28.1 %collective-permute-start.10 = (bf16[3,208,640]{2,1,0:T(8,128)(2,1)}, bf16[3,208,640]{2,1,0:T(8,128)(2,1)}, u32[]{:S(2)}, u32[]{:S(2)}) collective-permute-start(bf16[3,208,640]{2,1,0:T(8,128)(2,1)} %slice.49), channel_id=1, source_target_pairs={{0,2},{2,0},{1,3},{3,1},{4,6},{6,4},{5,7},{7,5},{8,10},{10,8},{9,1... | collective-permute-start | bytes 2396168 | tf_op jit(solution)/shard_map/ppermute | solution.py:30
  65.4 24.1 %all-to-all-start = ((bf16[4,320,256]{2,1,0:T(8,128)(2,1)}), bf16[4,320,256]{2,1,0:T(8,128)(2,1)S(1)}, u32[]{:S(2)}, u32[]{:S(2)}) async-start(bf16[4,320,256]{2,1,0:T(8,128)(2,1)} %bitcast.16), calls=%async_computation | async-start | bytes 1310720 | tf_op jit(solution)/shard_map/all_to_all | solution.py:757
  70.2 22.7 %collective-permute-start.9 = (bf16[3,112,640]{2,1,0:T(8,128)(2,1)S(1)}, bf16[3,112,640]{2,1,0:T(8,128)(2,1)}, u32[]{:S(2)}, u32[]{:S(2)}) collective-permute-start(bf16[3,112,640]{2,1,0:T(8,128)(2,1)S(1)} %slice.48), channel_id=1, source_target_pairs={{0,1},{1,0},{2,3},{3,2},{4,5},{5,4},{6,7},{7,6},{8,9},{9,8},{10,11... | collective-permute-start | bytes 1290248 | tf_op jit(solution)/shard_map/ppermute | solution.py:30
  72.0 25.2 %collective-permute-start.12 = (bf16[3,320,640]{2,1,0:T(8,128)(2,1)}, bf16[3,320,640]{2,1,0:T(8,128)(2,1)S(1)}, u32[]{:S(2)}, u32[]{:S(2)}) collective-permute-start(bf16[3,320,640]{2,1,0:T(8,128)(2,1)} %collective-permute-done.6.hx), channel_id=1, source_target_pairs={{0,4},{4,0},{1,5},{5,1},{2,6},{6,2},{3,7},{7,3},{8,12},{12,8},{9,1... | collective-permute-start | bytes 3686408 | tf_op jit(solution)/shard_map/ppermute | solution.py:30
  72.0 25.2 %collective-permute-start.13 = (bf16[3,320,640]{2,1,0:T(8,128)(2,1)S(1)}, bf16[3,320,640]{2,1,0:T(8,128)(2,1)}, u32[]{:S(2)}, u32[]{:S(2)}) collective-permute-start(bf16[3,320,640]{2,1,0:T(8,128)(2,1)S(1)} %collective-permute-done.7.hy), channel_id=1, source_target_pairs={{0,4},{4,0},{1,5},{5,1},{2,6},{6,2},{3,7},{7,3},{8,12},{12,8},{9,1... | collective-permute-start | bytes 3686408 | tf_op jit(solution)/shard_map/ppermute | solution.py:30
  72.5 20.3 %collective-permute-start.11 = (bf16[256,640]{1,0:T(8,128)(2,1)}, bf16[256,640]{1,0:T(8,128)(2,1)}, u32[]{:S(2)}, u32[]{:S(2)}) collective-permute-start(bf16[256,640]{1,0:T(8,128)(2,1)} %constant_dynamic-slice_fusion), channel_id=1, source_target_pairs={{0,1},{1,0},{2,3},{3,2},{4,5},{5,4},{6,7},{7,6},{8,9},{9,8},{10,11... | collective-permute-start | bytes 983048 | tf_op jit(solution)/shard_map/ppermute | solution.py:30
  89.5 7.7 %copy-start.4 = (bf16[4,320,256]{2,1,0:T(8,128)(2,1)}, bf16[4,320,256]{2,1,0:T(8,128)(2,1)S(1)}, u32[]{:S(2)}) copy-start(bf16[4,320,256]{2,1,0:T(8,128)(2,1)S(1)} %all-to-all-done.a) | copy-start | bytes 1966084
  92.8 4.4 %collective-permute-start.15 = (bf16[3,208,640]{2,1,0:T(8,128)(2,1)}, bf16[3,208,640]{2,1,0:T(8,128)(2,1)}, u32[]{:S(2)}, u32[]{:S(2)}) collective-permute-start(bf16[3,208,640]{2,1,0:T(8,128)(2,1)} %collective-permute-done.10.d1), channel_id=1, source_target_pairs={{0,4},{4,0},{1,5},{5,1},{2,6},{6,2},{3,7},{7,3},{8,12},{12,8},{9,1... | collective-permute-start | bytes 2396168 | tf_op jit(solution)/shard_map/ppermute | solution.py:30
  92.8 4.4 %collective-permute-start.14 = (bf16[3,112,640]{2,1,0:T(8,128)(2,1)}, bf16[3,112,640]{2,1,0:T(8,128)(2,1)S(1)}, u32[]{:S(2)}, u32[]{:S(2)}) collective-permute-start(bf16[3,112,640]{2,1,0:T(8,128)(2,1)} %collective-permute-done.9.d0), channel_id=1, source_target_pairs={{0,4},{4,0},{1,5},{5,1},{2,6},{6,2},{3,7},{7,3},{8,12},{12,8},{9,1... | collective-permute-start | bytes 1290248 | tf_op jit(solution)/shard_map/ppermute | solution.py:30
  118.6 5.0 %collective-permute-start.19 = (bf16[3,160,640]{2,1,0:T(8,128)(2,1)}, bf16[3,160,640]{2,1,0:T(8,128)(2,1)S(1)}, u32[]{:S(2)}, u32[]{:S(2)}) collective-permute-start(bf16[3,160,640]{2,1,0:T(8,128)(2,1)} %get-tuple-element.140), channel_id=1, source_target_pairs={{0,4},{4,0},{1,5},{5,1},{2,6},{6,2},{3,7},{7,3},{8,12},{12,8},{9,1... | collective-permute-start | bytes 1843208 | tf_op jit(solution)/shard_map/ppermute | solution.py:30
  118.8 6.9 %collective-permute-start.18 = (bf16[3,160,640]{2,1,0:T(8,128)(2,1)}, bf16[3,160,640]{2,1,0:T(8,128)(2,1)}, u32[]{:S(2)}, u32[]{:S(2)}) collective-permute-start(bf16[3,160,640]{2,1,0:T(8,128)(2,1)} %get-tuple-element.138), channel_id=1, source_target_pairs={{0,4},{4,0},{1,5},{5,1},{2,6},{6,2},{3,7},{7,3},{8,12},{12,8},{9,1... | collective-permute-start | bytes 1843208 | tf_op jit(solution)/shard_map/ppermute | solution.py:30
  119.2 8.2 %collective-permute-start.17 = (bf16[3,160,640]{2,1,0:T(8,128)(2,1)}, bf16[3,160,640]{2,1,0:T(8,128)(2,1)S(1)}, u32[]{:S(2)}, u32[]{:S(2)}) collective-permute-start(bf16[3,160,640]{2,1,0:T(8,128)(2,1)} %get-tuple-element.136), channel_id=1, source_target_pairs={{0,4},{4,0},{1,5},{5,1},{2,6},{6,2},{3,7},{7,3},{8,12},{12,8},{9,1... | collective-permute-start | bytes 1843208 | tf_op jit(solution)/shard_map/ppermute | solution.py:30
  119.3 10.2 %collective-permute-start.16 = (bf16[3,160,640]{2,1,0:T(8,128)(2,1)}, bf16[3,160,640]{2,1,0:T(8,128)(2,1)S(1)}, u32[]{:S(2)}, u32[]{:S(2)}) collective-permute-start(bf16[3,160,640]{2,1,0:T(8,128)(2,1)} %get-tuple-element.134), channel_id=1, source_target_pairs={{0,4},{4,0},{1,5},{5,1},{2,6},{6,2},{3,7},{7,3},{8,12},{12,8},{9,1... | collective-permute-start | bytes 1843208 | tf_op jit(solution)/shard_map/ppermute | solution.py:30
  119.7 13.4 %all-to-all-start.1 = ((bf16[4,320,256]{2,1,0:T(8,128)(2,1)}), bf16[4,320,256]{2,1,0:T(8,128)(2,1)S(1)}, u32[]{:S(2)}, u32[]{:S(2)}) async-start(bf16[4,320,256]{2,1,0:T(8,128)(2,1)} %get-tuple-element.132), calls=%async_computation.1 | async-start | bytes 1310720 | tf_op jit(solution)/shard_map/all_to_all | solution.py:757
  123.4 11.1 %collective-permute-start.24 = (bf16[3,160,640]{2,1,0:T(8,128)(2,1)}, bf16[3,160,640]{2,1,0:T(8,128)(2,1)}, u32[]{:S(2)}, u32[]{:S(2)}) collective-permute-start(bf16[3,160,640]{2,1,0:T(8,128)(2,1)} %get-tuple-element.149), channel_id=1, source_target_pairs={{0,4},{4,0},{1,5},{5,1},{2,6},{6,2},{3,7},{7,3},{8,12},{12,8},{9,1... | collective-permute-start | bytes 1843208 | tf_op jit(solution)/shard_map/ppermute | solution.py:30
  123.6 11.6 %collective-permute-start.25 = (bf16[3,160,640]{2,1,0:T(8,128)(2,1)}, bf16[3,160,640]{2,1,0:T(8,128)(2,1)}, u32[]{:S(2)}, u32[]{:S(2)}) collective-permute-start(bf16[3,160,640]{2,1,0:T(8,128)(2,1)} %get-tuple-element.150), channel_id=1, source_target_pairs={{0,4},{4,0},{1,5},{5,1},{2,6},{6,2},{3,7},{7,3},{8,12},{12,8},{9,1... | collective-permute-start | bytes 1843208 | tf_op jit(solution)/shard_map/ppermute | solution.py:30
  125.7 11.0 %collective-permute-start.26 = (bf16[3,160,640]{2,1,0:T(8,128)(2,1)}, bf16[3,160,640]{2,1,0:T(8,128)(2,1)}, u32[]{:S(2)}, u32[]{:S(2)}) collective-permute-start(bf16[3,160,640]{2,1,0:T(8,128)(2,1)} %get-tuple-element.151), channel_id=1, source_target_pairs={{0,4},{4,0},{1,5},{5,1},{2,6},{6,2},{3,7},{7,3},{8,12},{12,8},{9,1... | collective-permute-start | bytes 1843208 | tf_op jit(solution)/shard_map/ppermute | solution.py:30
  127.4 29.2 %collective-permute-start.27 = (bf16[3,160,640]{2,1,0:T(8,128)(2,1)}, bf16[3,160,640]{2,1,0:T(8,128)(2,1)}, u32[]{:S(2)}, u32[]{:S(2)}) collective-permute-start(bf16[3,160,640]{2,1,0:T(8,128)(2,1)} %get-tuple-element.152), channel_id=1, source_target_pairs={{0,4},{4,0},{1,5},{5,1},{2,6},{6,2},{3,7},{7,3},{8,12},{12,8},{9,1... | collective-permute-start | bytes 1843208 | tf_op jit(solution)/shard_map/ppermute | solution.py:30
  133.1 23.5 %collective-permute-start.20 = (bf16[3,160,640]{2,1,0:T(8,128)(2,1)S(1)}, bf16[3,160,640]{2,1,0:T(8,128)(2,1)}, u32[]{:S(2)}, u32[]{:S(2)}) collective-permute-start(bf16[3,160,640]{2,1,0:T(8,128)(2,1)S(1)} %add_convert_fusion.11), channel_id=1, source_target_pairs={{0,2},{2,0},{1,3},{3,1},{4,6},{6,4},{5,7},{7,5},{8,10},{10,8},{9,1... | collective-permute-start | bytes 1843208 | tf_op jit(solution)/shard_map/ppermute | solution.py:30
  134.5 22.1 %collective-permute-start.21 = (bf16[3,160,640]{2,1,0:T(8,128)(2,1)S(1)}, bf16[3,160,640]{2,1,0:T(8,128)(2,1)}, u32[]{:S(2)}, u32[]{:S(2)}) collective-permute-start(bf16[3,160,640]{2,1,0:T(8,128)(2,1)S(1)} %add_convert_fusion.10), channel_id=1, source_target_pairs={{0,1},{1,0},{2,3},{3,2},{4,5},{5,4},{6,7},{7,6},{8,9},{9,8},{10,11... | collective-permute-start | bytes 1843208 | tf_op jit(solution)/shard_map/ppermute | solution.py:30
  135.2 26.7 %collective-permute-start.22 = (bf16[3,160,640]{2,1,0:T(8,128)(2,1)S(1)}, bf16[3,160,640]{2,1,0:T(8,128)(2,1)}, u32[]{:S(2)}, u32[]{:S(2)}) collective-permute-start(bf16[3,160,640]{2,1,0:T(8,128)(2,1)S(1)} %add_convert_fusion.9), channel_id=1, source_target_pairs={{0,2},{2,0},{1,3},{3,1},{4,6},{6,4},{5,7},{7,5},{8,10},{10,8},{9,1... | collective-permute-start | bytes 1843208 | tf_op jit(solution)/shard_map/ppermute | solution.py:30
  136.6 26.7 %collective-permute-start.23 = (bf16[3,160,640]{2,1,0:T(8,128)(2,1)S(1)}, bf16[3,160,640]{2,1,0:T(8,128)(2,1)}, u32[]{:S(2)}, u32[]{:S(2)}) collective-permute-start(bf16[3,160,640]{2,1,0:T(8,128)(2,1)S(1)} %add_convert_fusion.8), channel_id=1, source_target_pairs={{0,1},{1,0},{2,3},{3,2},{4,5},{5,4},{6,7},{7,6},{8,9},{9,8},{10,11... | collective-permute-start | bytes 1843208 | tf_op jit(solution)/shard_map/ppermute | solution.py:30
  150.5 12.9 %copy-start.29 = (f32[4,80,1]{2,1,0:T(8,128)S(1)}, f32[4,80,1]{2,1,0:T(8,128)}, u32[]{:S(2)}) copy-start(f32[4,80,1]{2,1,0:T(8,128)} %get-tuple-element.163) | copy-start | bytes 3844
  150.5 13.0 %copy-start.25 = (bf16[3,160,640]{2,1,0:T(8,128)(2,1)S(1)}, bf16[3,160,640]{2,1,0:T(8,128)(2,1)}, u32[]{:S(2)}) copy-start(bf16[3,160,640]{2,1,0:T(8,128)(2,1)} %get-tuple-element.155) | copy-start | bytes 1843204
  163.3 4.7 %collective-permute-start.30 = (bf16[2,3,160,640]{3,2,1,0:T(8,128)(2,1)}, bf16[2,3,160,640]{3,2,1,0:T(8,128)(2,1)S(1)}, u32[]{:S(2)}, u32[]{:S(2)}) collective-permute-start(bf16[2,3,160,640]{3,2,1,0:T(8,128)(2,1)} %get-tuple-element.159), channel_id=1, source_target_pairs={{0,4},{4,0},{1,5},{5,1},{2,6},{6,2},{3,7},{7,3},{8,12},{12,8},{9,1... | collective-permute-start | bytes 3686408 | tf_op jit(solution)/shard_map/ppermute | solution.py:30
  165.0 18.0 %collective-permute-start.29 = (bf16[3,160,640]{2,1,0:T(8,128)(2,1)S(1)}, bf16[3,160,640]{2,1,0:T(8,128)(2,1)}, u32[]{:S(2)}, u32[]{:S(2)}) collective-permute-start(bf16[3,160,640]{2,1,0:T(8,128)(2,1)S(1)} %add_convert_fusion.6), channel_id=1, source_target_pairs={{0,2},{2,0},{1,3},{3,1},{4,6},{6,4},{5,7},{7,5},{8,10},{10,8},{9,1... | collective-permute-start | bytes 1843208 | tf_op jit(solution)/shard_map/ppermute | solution.py:30
  167.0 16.2 %collective-permute-start.28 = (bf16[3,160,640]{2,1,0:T(8,128)(2,1)S(1)}, bf16[3,160,640]{2,1,0:T(8,128)(2,1)}, u32[]{:S(2)}, u32[]{:S(2)}) collective-permute-start(bf16[3,160,640]{2,1,0:T(8,128)(2,1)S(1)} %add_convert_fusion.7), channel_id=1, source_target_pairs={{0,1},{1,0},{2,3},{3,2},{4,5},{5,4},{6,7},{7,6},{8,9},{9,8},{10,11... | collective-permute-start | bytes 1843208 | tf_op jit(solution)/shard_map/ppermute | solution.py:30
  169.2 15.9 %collective-permute-start.31 = (bf16[3,160,640]{2,1,0:T(8,128)(2,1)}, bf16[3,160,640]{2,1,0:T(8,128)(2,1)S(1)}, u32[]{:S(2)}, u32[]{:S(2)}) collective-permute-start(bf16[3,160,640]{2,1,0:T(8,128)(2,1)} %fusion.2), channel_id=1, source_target_pairs={{0,8},{8,0},{16,24},{24,16},{1,9},{9,1},{17,25},{25,17},{2,10},{10... | collective-permute-start | bytes 1843208 | tf_op jit(solution)/shard_map/ppermute | solution.py:762
  171.4 8.6 %copy-start.23 = (bf16[3,160,640]{2,1,0:T(8,128)(2,1)S(1)}, bf16[3,160,640]{2,1,0:T(8,128)(2,1)}, u32[]{:S(2)}) copy-start(bf16[3,160,640]{2,1,0:T(8,128)(2,1)} %get-tuple-element.169) | copy-start | bytes 1843204
  187.8 16.2 %collective-permute-start.33 = (bf16[3,160,640]{2,1,0:T(8,128)(2,1)}, bf16[3,160,640]{2,1,0:T(8,128)(2,1)}, u32[]{:S(2)}, u32[]{:S(2)}) collective-permute-start(bf16[3,160,640]{2,1,0:T(8,128)(2,1)} %get-tuple-element.201), channel_id=1, source_target_pairs={{0,8},{8,0},{16,24},{24,16},{1,9},{9,1},{17,25},{25,17},{2,10},{10... | collective-permute-start | bytes 1843208 | tf_op jit(solution)/shard_map/ppermute | solution.py:762
  189.7 28.7 %collective-permute-start.32 = (bf16[3,160,640]{2,1,0:T(8,128)(2,1)S(1)}, bf16[3,160,640]{2,1,0:T(8,128)(2,1)}, u32[]{:S(2)}, u32[]{:S(2)}) collective-permute-start(bf16[3,160,640]{2,1,0:T(8,128)(2,1)S(1)} %fusion.1), channel_id=1, source_target_pairs={{0,24},{8,16},{16,8},{24,0},{1,25},{9,17},{17,9},{25,1},{2,26},{10... | collective-permute-start | bytes 1843208 | tf_op jit(solution)/shard_map/ppermute | solution.py:762
  192.2 68.0 %all-to-all-start.2 = ((bf16[4,528,640]{2,1,0:T(8,128)(2,1)}), bf16[4,528,640]{2,1,0:T(8,128)(2,1)S(1)}, u32[]{:S(2)}, u32[]{:S(2)}) async-start(bf16[4,528,640]{2,1,0:T(8,128)(2,1)} %project_back.1), calls=%async_computation.2 | async-start | bytes 5406720 | tf_op jit(solution)/shard_map/all_to_all | solution.py:757
  196.1 24.9 %copy-start.7 = (bf16[3,160,640]{2,1,0:T(8,128)(2,1)S(1)}, bf16[3,160,640]{2,1,0:T(8,128)(2,1)}, u32[]{:S(2)}) copy-start(bf16[3,160,640]{2,1,0:T(8,128)(2,1)} %get-tuple-element.184) | copy-start | bytes 1843204
  196.1 24.9 %copy-start.8 = (bf16[3,160,640]{2,1,0:T(8,128)(2,1)S(1)}, bf16[3,160,640]{2,1,0:T(8,128)(2,1)}, u32[]{:S(2)}) copy-start(bf16[3,160,640]{2,1,0:T(8,128)(2,1)} %get-tuple-element.185) | copy-start | bytes 1843204
  220.4 27.3 %collective-permute-start.39 = (bf16[3,160,640]{2,1,0:T(8,128)(2,1)}, bf16[3,160,640]{2,1,0:T(8,128)(2,1)}, u32[]{:S(2)}, u32[]{:S(2)}) collective-permute-start(bf16[3,160,640]{2,1,0:T(8,128)(2,1)} %add_convert_fusion.1), channel_id=1, source_target_pairs={{0,8},{8,0},{16,24},{24,16},{1,9},{9,1},{17,25},{25,17},{2,10},{10... | collective-permute-start | bytes 1843208 | tf_op jit(solution)/shard_map/ppermute | solution.py:762
  222.3 28.7 %collective-permute-start.37 = (bf16[3,160,640]{2,1,0:T(8,128)(2,1)S(1)}, bf16[3,160,640]{2,1,0:T(8,128)(2,1)}, u32[]{:S(2)}, u32[]{:S(2)}) collective-permute-start(bf16[3,160,640]{2,1,0:T(8,128)(2,1)S(1)} %add_convert_fusion.3), channel_id=1, source_target_pairs={{0,24},{8,16},{16,8},{24,0},{1,25},{9,17},{17,9},{25,1},{2,26},{10... | collective-permute-start | bytes 1843208 | tf_op jit(solution)/shard_map/ppermute | solution.py:762
  225.0 28.0 %collective-permute-start.34 = (bf16[2,256,640]{2,1,0:T(8,128)(2,1)}, bf16[2,256,640]{2,1,0:T(8,128)(2,1)}, u32[]{:S(2)}, u32[]{:S(2)}) collective-permute-start(bf16[2,256,640]{2,1,0:T(8,128)(2,1)} %get-tuple-element.179), channel_id=1, source_target_pairs={{0,1},{1,0},{2,3},{3,2},{4,5},{5,4},{6,7},{7,6},{8,9},{9,8},{10,11... | collective-permute-start | bytes 1966088 | tf_op jit(solution)/shard_map/ppermute | solution.py:30
  249.9 10.3 %collective-permute-start.40 = (bf16[3,160,640]{2,1,0:T(8,128)(2,1)S(1)}, bf16[3,160,640]{2,1,0:T(8,128)(2,1)}, u32[]{:S(2)}, u32[]{:S(2)}) collective-permute-start(bf16[3,160,640]{2,1,0:T(8,128)(2,1)S(1)} %get-tuple-element.208), channel_id=1, source_target_pairs={{0,1},{1,0},{2,3},{3,2},{4,5},{5,4},{6,7},{7,6},{8,9},{9,8},{10,11... | collective-permute-start | bytes 1843208 | tf_op jit(solution)/shard_map/ppermute | solution.py:30
  251.0 24.5 %collective-permute-start.41 = (bf16[3,160,640]{2,1,0:T(8,128)(2,1)}, bf16[3,160,640]{2,1,0:T(8,128)(2,1)}, u32[]{:S(2)}, u32[]{:S(2)}) collective-permute-start(bf16[3,160,640]{2,1,0:T(8,128)(2,1)} %get-tuple-element.209.mine), channel_id=1, source_target_pairs={{0,4},{4,0},{1,5},{5,1},{2,6},{6,2},{3,7},{7,3},{8,12},{12,8},{9,1... | collective-permute-start | bytes 1843208 | tf_op jit(solution)/shard_map/ppermute | solution.py:30
  253.0 27.9 %collective-permute-start.43 = (bf16[3,160,640]{2,1,0:T(8,128)(2,1)}, bf16[3,160,640]{2,1,0:T(8,128)(2,1)}, u32[]{:S(2)}, u32[]{:S(2)}) collective-permute-start(bf16[3,160,640]{2,1,0:T(8,128)(2,1)} %add_convert_fusion.2), channel_id=1, source_target_pairs={{0,8},{8,0},{16,24},{24,16},{1,9},{9,1},{17,25},{25,17},{2,10},{10... | collective-permute-start | bytes 1843208 | tf_op jit(solution)/shard_map/ppermute | solution.py:762
  260.2 15.3 %collective-permute-start.42 = (bf16[3,160,640]{2,1,0:T(8,128)(2,1)}, bf16[3,160,640]{2,1,0:T(8,128)(2,1)}, u32[]{:S(2)}, u32[]{:S(2)}) collective-permute-start(bf16[3,160,640]{2,1,0:T(8,128)(2,1)} %collective-permute-done.40.theirs), channel_id=1, source_target_pairs={{0,4},{4,0},{1,5},{5,1},{2,6},{6,2},{3,7},{7,3},{8,12},{12,8},{9,1... | collective-permute-start | bytes 1843208 | tf_op jit(solution)/shard_map/ppermute | solution.py:30
  260.2 2.2 collective-permute-start.35
  262.2 8.2 %copy-start.1 = (bf16[512,640]{1,0:T(8,128)(2,1)S(1)}, bf16[512,640]{1,0:T(8,128)(2,1)}, u32[]{:S(2)}) copy-start(bf16[512,640]{1,0:T(8,128)(2,1)} %x00.3) | copy-start | bytes 1966084
  262.4 8.0 %collective-permute-start.36 = (f32[9,640]{1,0:T(8,128)S(1)}, f32[9,640]{1,0:T(8,128)S(1)}, u32[]{:S(2)}, u32[]{:S(2)}) collective-permute-start(f32[9,640]{1,0:T(8,128)S(1)} %add.149), channel_id=1, source_target_pairs={{0,8},{8,0},{16,24},{24,16},{1,9},{9,1},{17,25},{25,17},{2,10},{10... | collective-permute-start | bytes 69128 | tf_op jit(solution)/shard_map/ppermute | solution.py:762
  270.4 5.1 %collective-permute-start.38 = (f32[9,640]{1,0:T(8,128)S(1)}, f32[9,640]{1,0:T(8,128)S(1)}, u32[]{:S(2)}, u32[]{:S(2)}) collective-permute-start(f32[9,640]{1,0:T(8,128)S(1)} %add.152), channel_id=1, source_target_pairs={{0,16},{8,24},{16,0},{24,8},{1,17},{9,25},{17,1},{25,9},{2,18},{10... | collective-permute-start | bytes 69128 | tf_op jit(solution)/shard_map/ppermute | solution.py:762
  282.3 2.1 collective-permute-start.44
  282.4 2.9 %collective-permute-start.45 = (bf16[3,160,640]{2,1,0:T(8,128)(2,1)S(1)}, bf16[3,160,640]{2,1,0:T(8,128)(2,1)S(1)}, u32[]{:S(2)}, u32[]{:S(2)}) collective-permute-start(bf16[3,160,640]{2,1,0:T(8,128)(2,1)S(1)} %get-tuple-element.206.b), channel_id=1, source_target_pairs={{0,4},{4,0},{1,5},{5,1},{2,6},{6,2},{3,7},{7,3},{8,12},{12,8},{9,1... | collective-permute-start | bytes 1843208 | tf_op jit(solution)/shard_map/ppermute | solution.py:30
  (23 other events, 67.8 us)
